TPU v7x, 32 devices: a whole 2x2x4 slice. The times are simulated.
32 devices in a mesh: seq: 4 (over x, core), head: 2 (over y), blk: 4 (over z).
Axes of the slice: x: 2, y: 2, z: 4, core: 2. Of those that a mesh axis runs over, the one named last changes fastest.
Arguments:
- tokens: bfloat16 [4096, 1024], P(('seq', 'head', 'blk')), may hold values from -6 to 6
- out_grad: bfloat16 [4096, 1024], P(('seq', 'head', 'blk')), may hold values from -6 to 6
- w_qkv: bfloat16 [1024, 3072], P(('head', 'blk')), may hold values from -0.1875 to 0.1875
- w_out: bfloat16 [1024, 1024], P(('head', 'blk')), may hold values from -9 to 9
- fc_in: bfloat16 [4096, 1024], P(('head', 'blk')), may hold values from -0.1875 to 0.1875
- fc_out: bfloat16 [4096, 1024], P(('head', 'blk')), may hold values from -0.09375 to 0.09375
- fc_in_bias: bfloat16 [4096], P(('head', 'blk')), may hold values from -3 to 3
- vectors: bfloat16 [1024, 8], P(('head', 'blk')), may hold values from -1.5 to 1.5
Outputs:
- layer_output: float32 [4096, 1024], P(('seq', 'head', 'blk'))
- input_grad: float32 [4096, 1024], P(('seq', 'head', 'blk'))
- grad_w_qkv: float32 [1024, 3072], P(('seq', 'head', 'blk'))
- grad_w_out: float32 [1024, 1024], P(('seq', 'head', 'blk'))
- grad_fc_in: float32 [4096, 1024], P(('seq', 'head', 'blk'))
- grad_fc_out: float32 [4096, 1024], P(('seq', 'head', 'blk'))
- grad_fc_in_bias: float32 [4096], P(('seq', 'head', 'blk'))
- grad_vectors: float32 [1024, 8], P(('seq', 'head', 'blk'))
All inputs are finite; a program needn't handle non-finite values.
Results may differ from a plain program's by a relative error of at most 0.015.
Values may be sent and summed in bfloat16 or wider, within the bound.
No kernel may reach another device: no remote copies, remote signals or barrier semaphores. Data moves between devices by JAX's collectives and lax.ppermute only.
A program may use at most 256 MiB of HBM per device.

v0:
```python
import math

import jax
import jax.numpy as jnp
from jax import lax
from jax.sharding import PartitionSpec as P

HEAD_DIM = 64


def layer_norm(values, gain_vec, shift_vec):
    center = values - jnp.mean(values, axis=-1, keepdims=True)
    spread = jnp.mean(center * center, axis=-1, keepdims=True)
    return center * lax.rsqrt(spread + 1e-05) * gain_vec + shift_vec


def gelu_exact(values):
    return jax.nn.gelu(values, approximate=False)


def split_heads(values):
    return values.reshape(values.shape[0], values.shape[1] // HEAD_DIM, HEAD_DIM)


def head_scores(left_rows, right_rows):
    return jnp.einsum("qhd,khd->hqk", left_rows, right_rows, preferred_element_type=jnp.float32)


def ffn_part(factors):
    middle_low, grad_pre_full, act_full, grad_ffn = factors
    return jnp.concatenate(
        [
            jnp.einsum("tf,td->fd", grad_pre_full, middle_low, preferred_element_type=jnp.float32),
            jnp.einsum("tf,td->fd", act_full, grad_ffn, preferred_element_type=jnp.float32),
        ],
        axis=1,
    )


def attn_part(factors, extra_cols):
    tokens, grad_proj, context, grad_attn = factors
    return jnp.concatenate(
        [
            jnp.einsum("tn,tc->nc", tokens, grad_proj, preferred_element_type=jnp.float32),
            jnp.einsum("tn,tc->nc", context, grad_attn, preferred_element_type=jnp.float32),
            extra_cols,
        ],
        axis=1,
    )


def body(tokens, out_grad, w_qkv, w_out, fc_in, fc_out, fc_in_bias, vectors):
    model_width = tokens.shape[1]
    hidden_units = fc_in.shape[0] * lax.axis_size(("head", "blk"))
    ratio = hidden_units // model_width
    scale = HEAD_DIM ** (-0.5)
    part_qkv = lax.all_gather(w_qkv, ("head", "blk"), axis=0, tiled=True)
    part_out = lax.all_gather(w_out, ("head", "blk"), axis=0, tiled=True)
    part_vec = lax.all_gather(vectors, ("head", "blk"), axis=0, tiled=True)
    part_rows = part_qkv.shape[0]
    projected = jnp.dot(tokens, part_qkv, preferred_element_type=jnp.float32)
    out_full = part_out
    attn_state = (projected, out_full, part_vec)
    projected = attn_state[0]
    out_full = attn_state[1]
    vec_float = attn_state[2].astype(jnp.float32)
    gain_one, gain_two = (vec_float[:, 0], vec_float[:, 1])
    shift_one, shift_two = (vec_float[:, 2], vec_float[:, 3])
    bias_query, bias_value = (vec_float[:, 4], vec_float[:, 5])
    bias_output, bias_ffn = (vec_float[:, 6], vec_float[:, 7])
    queries = ((projected[:, :model_width] + bias_query) * scale).astype(jnp.bfloat16)
    key_rows = projected[:, model_width : 2 * model_width].astype(jnp.bfloat16)
    value_rows = (projected[:, 2 * model_width :] + bias_value).astype(jnp.bfloat16)
    query_heads, key_heads, value_heads = (
        lax.all_to_all(queries, "head", split_axis=1, concat_axis=0, tiled=True),
        lax.all_to_all(key_rows, "head", split_axis=1, concat_axis=0, tiled=True),
        lax.all_to_all(value_rows, "head", split_axis=1, concat_axis=0, tiled=True),
    )
    query_split = split_heads(query_heads)
    group_rows = query_split.shape[0]
    group_width = key_heads.shape[1]
    seq_rows = group_rows * lax.axis_size("blk")
    portion = (
        lax.all_gather(key_heads, "blk", axis=0, tiled=True),
        lax.all_gather(value_heads, "blk", axis=0, tiled=True),
    )
    scores = head_scores(query_split, split_heads(portion[0]))
    run_sum = jnp.sum(jnp.exp(scores), axis=-1)
    key_all = portion[0]
    value_all = portion[1]
    run_sum, key_all, value_all = (run_sum, key_all, value_all)
    log_total = jnp.log(run_sum)
    block_rows = math.gcd(512, seq_rows)
    block_count = seq_rows // block_rows
    key_blocks = key_all.reshape(block_count, block_rows, group_width)
    value_blocks = value_all.reshape(block_count, block_rows, group_width)

    def mix_block(totals, pair):
        scores = head_scores(query_split, split_heads(pair[0]))
        probs_low = jnp.exp(scores - log_total[:, :, None]).astype(jnp.bfloat16)
        return (
            totals
            + jnp.einsum(
                "hqk,khd->qhd", probs_low, split_heads(pair[1]), preferred_element_type=jnp.float32
            ),
            None,
        )

    mixed, unused = lax.scan(
        mix_block, jnp.zeros(query_split.shape, jnp.float32), (key_blocks, value_blocks)
    )
    context = lax.all_to_all(
        mixed.reshape(group_rows, -1).astype(jnp.bfloat16),
        "head",
        split_axis=0,
        concat_axis=1,
        tiled=True,
    )
    attn_out = jnp.dot(context, out_full, preferred_element_type=jnp.float32) + bias_output
    residual_one = tokens.astype(jnp.float32) + attn_out
    middle, norm_one_back = jax.vjp(layer_norm, residual_one, gain_one, shift_one)
    middle_low = middle.astype(jnp.bfloat16)
    part_in = lax.all_gather(fc_in, ("head", "blk"), axis=0, tiled=True)
    part_out = lax.all_gather(fc_out, ("head", "blk"), axis=0, tiled=True)
    part_bias = lax.all_gather(fc_in_bias, ("head", "blk"), axis=0, tiled=True)
    pre_part = jnp.einsum("td,fd->tf", middle_low, part_in, preferred_element_type=jnp.float32)
    pre_part = pre_part + part_bias.astype(jnp.float32)
    act_part = gelu_exact(pre_part).astype(jnp.bfloat16)
    summed = jnp.dot(act_part, part_out, preferred_element_type=jnp.float32)
    ffn_pre_full = pre_part
    residual_two = middle + summed + bias_ffn
    layer_output, norm_two_back = jax.vjp(layer_norm, residual_two, gain_two, shift_two)
    grad_resid_two, grad_gain_two, grad_shift_two = norm_two_back(out_grad.astype(jnp.float32))
    grad_ffn = grad_resid_two.astype(jnp.bfloat16)
    qkv_flat = w_qkv.reshape(fc_in.shape[0], -1)
    portion = (
        lax.all_gather(fc_in, ("head", "blk"), axis=0, tiled=True),
        lax.all_gather(fc_out, ("head", "blk"), axis=0, tiled=True),
        lax.all_gather(qkv_flat, ("head", "blk"), axis=0, tiled=True),
    )
    part_in = portion[0]
    part_rows = part_in.shape[0]
    pre_part = ffn_pre_full
    grad_act = jnp.einsum("td,fd->tf", grad_ffn, portion[1], preferred_element_type=jnp.float32)
    grad_pre = jax.vjp(gelu_exact, pre_part)[1](grad_act)[0].astype(jnp.bfloat16)
    grad_mid = jnp.dot(grad_pre, part_in, preferred_element_type=jnp.float32)
    grad_mid, grad_pre_all = (grad_mid, grad_pre)
    qkv_gathered = portion[2]
    qkv_full = qkv_gathered.reshape(model_width, 3 * model_width)
    grad_resid_one, grad_gain_one, grad_shift_one = norm_one_back(grad_resid_two + grad_mid)
    grad_attn = grad_resid_one.astype(jnp.bfloat16)
    grad_context = jnp.einsum(
        "td,ed->te", grad_attn, out_full, preferred_element_type=jnp.float32
    ).astype(jnp.bfloat16)
    grad_ctx_heads = lax.all_to_all(grad_context, "head", split_axis=1, concat_axis=0, tiled=True)
    grad_ctx_split = split_heads(grad_ctx_heads)
    delta_heads = jnp.sum(grad_ctx_split.astype(jnp.float32) * mixed, axis=-1).T

    def back_block(grad_query, pair):
        key_part = split_heads(pair[0])
        value_part = split_heads(pair[1])
        scores = head_scores(query_split, key_part)
        probs = jnp.exp(scores - log_total[:, :, None])
        dprobs = head_scores(grad_ctx_split, value_part)
        dscores = (probs * (dprobs - delta_heads[:, :, None])).astype(jnp.bfloat16)
        grad_query = grad_query + jnp.einsum(
            "hqk,khd->qhd", dscores, key_part, preferred_element_type=jnp.float32
        )
        grad_key = jnp.einsum(
            "hqk,qhd->khd", dscores, query_split, preferred_element_type=jnp.float32
        )
        grad_value = jnp.einsum(
            "hqk,qhd->khd",
            probs.astype(jnp.bfloat16),
            grad_ctx_split,
            preferred_element_type=jnp.float32,
        )
        part_rows = pair[0].shape[0]
        return (
            grad_query,
            jnp.concatenate(
                [grad_key.reshape(part_rows, -1), grad_value.reshape(part_rows, -1)], axis=1
            ),
        )

    grad_query_heads, kv_terms = lax.scan(
        back_block, jnp.zeros(query_split.shape, jnp.float32), (key_blocks, value_blocks)
    )
    kv_own = lax.psum_scatter(
        kv_terms.reshape(seq_rows, 2 * group_width).astype(jnp.bfloat16),
        "blk",
        scatter_dimension=0,
        tiled=True,
    ).astype(jnp.float32)
    grad_query_tok, grad_key_tok, grad_value_tok = (
        lax.all_to_all(
            grad_query_heads.reshape(group_rows, -1).astype(jnp.bfloat16),
            "head",
            split_axis=0,
            concat_axis=1,
            tiled=True,
        ),
        lax.all_to_all(
            kv_own[:, :group_width].astype(jnp.bfloat16),
            "head",
            split_axis=0,
            concat_axis=1,
            tiled=True,
        ),
        lax.all_to_all(
            kv_own[:, group_width:].astype(jnp.bfloat16),
            "head",
            split_axis=0,
            concat_axis=1,
            tiled=True,
        ),
    )
    grad_proj = jnp.concatenate(
        [grad_query_tok * jnp.bfloat16(scale), grad_key_tok, grad_value_tok], axis=1
    )
    through_proj = jnp.einsum("tc,nc->tn", grad_proj, qkv_full, preferred_element_type=jnp.float32)
    input_grad = grad_resid_one + through_proj
    grad_proj_float = grad_proj.astype(jnp.float32)
    vec_term = jnp.stack(
        [
            grad_gain_one,
            grad_gain_two,
            grad_shift_one,
            grad_shift_two,
            jnp.sum(grad_proj_float[:, :model_width], axis=0),
            jnp.sum(grad_proj_float[:, 2 * model_width :], axis=0),
            jnp.sum(grad_attn.astype(jnp.float32), axis=0),
            jnp.sum(grad_ffn.astype(jnp.float32), axis=0),
        ],
        axis=1,
    )
    bias_term = jnp.sum(grad_pre_all.astype(jnp.float32), axis=0).reshape(model_width, -1)
    bias_cols = bias_term.shape[1]
    padding = jnp.zeros((model_width, 128 - 8 - bias_cols), jnp.float32)
    extra_cols = jnp.concatenate([vec_term, bias_term, padding], axis=1)
    rows_dev = hidden_units // lax.axis_size(("seq", "head", "blk"))
    ffn_block = ffn_part((middle_low, grad_pre_all, act_part, grad_ffn))
    attn_block = attn_part((tokens, grad_proj, context, grad_attn), extra_cols)
    merged = lax.psum_scatter(
        jnp.concatenate(
            [ffn_block, attn_block.reshape(lax.axis_size(("seq", "head", "blk")) * rows_dev, -1)],
            axis=1,
        ),
        ("seq", "head", "blk"),
        scatter_dimension=0,
        tiled=True,
    )
    grad_fc_in = merged[:, :model_width]
    grad_fc_out = merged[:, model_width : 2 * model_width]
    attn_grad = merged[:, 2 * model_width :].reshape(rows_dev // ratio, 4 * model_width + 128)
    grad_w_qkv = attn_grad[:, : 3 * model_width]
    grad_w_out = attn_grad[:, 3 * model_width : 4 * model_width]
    grad_vectors = attn_grad[:, 4 * model_width : 4 * model_width + 8]
    grad_fc_in_bias = attn_grad[:, 4 * model_width + 8 : 4 * model_width + 8 + bias_cols].reshape(
        -1
    )
    return (
        layer_output,
        input_grad,
        grad_w_qkv,
        grad_w_out,
        grad_fc_in,
        grad_fc_out,
        grad_fc_in_bias,
        grad_vectors,
    )


def solution(mesh):
    return jax.shard_map(
        body,
        mesh=mesh,
        in_specs=(
            P(("seq", "head", "blk"), None),
            P(("seq", "head", "blk"), None),
            P(("head", "blk"), None),
            P(("head", "blk"), None),
            P(("head", "blk"), None),
            P(("head", "blk"), None),
            P(("head", "blk")),
            P(("head", "blk"), None),
        ),
        out_specs=(
            P(("seq", "head", "blk"), None),
            P(("seq", "head", "blk"), None),
            P(("seq", "head", "blk"), None),
            P(("seq", "head", "blk"), None),
            P(("seq", "head", "blk"), None),
            P(("seq", "head", "blk"), None),
            P(("seq", "head", "blk")),
            P(("seq", "head", "blk"), None),
        ),
        check_vma=False,
    )
```

profile of v0, /device:TPU:2, one launch (start us, length us, event | category | flops | bytes accessed | tf_op | source)
XLA Modules:
  0.0 1827.3 jit_solution(11426575448178396895)
XLA Ops:
  7.9 27.7 %all_gather.30 = bf16[1024,8]{0,1:T(8,128)(2,1)S(1)} all-gather(bf16[128,8]{0,1:T(8,128)(2,1)} %param.19), channel_id=1, replica_groups=mesh['seq'=4,'head'=2,'blk'=4] {'head','blk'}, dimensions={0}, use_global_device_ids=true | all-gather | bytes 18432 | tf_op jit(solution)/shard_map/all_gather | solution.py:59
  35.7 74.8 %all-gather.9.cloned.1.call-done = bf16[1024,3072]{1,0:T(8,128)(2,1)} async-done(((bf16[128,3072]{1,0:T(8,128)(2,1)}), bf16[1024,3072]{1,0:T(8,128)(2,1)}) %all-gather.9.cloned.1.call-update) | async-done | bytes 6291472 | tf_op jit(solution)/shard_map/all_gather | solution.py:57
  110.5 3.9 fusion.40
  114.5 8.3 all_to_all.134
  122.9 8.3 all_to_all.135
  137.2 5.2 all-to-all-done.2
  143.4 6.1 all-gather.11.cloned.1.call-done
  151.0 27.5 %all-gather.13.cloned.1.call-done = bf16[1024,512]{1,0:T(8,128)(2,1)} async-done(((bf16[256,512]{1,0:T(8,128)(2,1)}), bf16[1024,512]{1,0:T(8,128)(2,1)}) %all-gather.13.cloned.1.call-update) | async-done | bytes 1048592 | tf_op jit(solution)/shard_map/all_gather | solution.py:84
  185.0 6.7 while.24
  192.6 3.4 all-to-all-start.3
  196.1 27.2 %all-gather = bf16[8,1,512]{2,1,0:T(2,128)(2,1)S(1)} all-gather(bf16[1,1,512]{2,1,0:T(2,128)(2,1)S(1)} %reshape.194), channel_id=1, replica_groups=mesh['seq'=4,'head'=2,'blk'=4] {'head','blk'}, dimensions={0}, use_global_device_ids=true | all-gather | bytes 9216 | tf_op jit(solution)/shard_map/all_gather | solution.py:125
  223.3 6.2 all-gather.15.cloned.1.call-done
  232.0 122.9 %all-gather.17.cloned.1.call-done = bf16[4096,1024]{1,0:T(8,128)(2,1)} async-done(((bf16[512,1024]{1,0:T(8,128)(2,1)}), bf16[4096,1024]{1,0:T(8,128)(2,1)}) %all-gather.17.cloned.1.call-update) | async-done | bytes 8388624 | tf_op jit(solution)/shard_map/all_gather | solution.py:123
  354.9 11.0 multiply_convert_fusion.1
  365.9 114.1 %all-gather.19.cloned.1.call-done = bf16[4096,1024]{1,0:T(8,128)(2,1)} async-done(((bf16[512,1024]{1,0:T(8,128)(2,1)}), bf16[4096,1024]{1,0:T(8,128)(2,1)}) %all-gather.19.cloned.1.call-update) | async-done | bytes 8388624 | tf_op jit(solution)/shard_map/all_gather | solution.py:124
  480.0 4.9 fusion.37
  486.7 5.4 convert_reduce_fusion
  501.0 4.9 all-to-all-done.4
  506.3 19.8 %while.25 = (s32[]{:T(128)}, f32[256,8,64]{0,2,1:T(8,128)}, bf16[2,512,1024]{2,1,0:T(8,128)(2,1)}, bf16[2,512,512]{1,2,0:T(8,128)(2,1)}, bf16[256,8,64]{0,2,1:T(...) while((s32[]{:T(128)}, f32[256,8,64]{0,2,1:T(8,128)}, ...), condition=%wide.region_13.14_spmd.clone, body=%wide.region_12.13_spmd.clone.sunk | while | flops 679739392 | bytes 32006280 | solution.py:186
  528.7 8.1 fusion.41
  536.8 8.2 fusion.27
  547.0 3.4 all-to-all-start.5
  550.4 18.3 %reduce-scatter.3.cloned.1.call-done = bf16[256,1024]{1,0:T(8,128)(2,1)} async-done(((bf16[1024,1024]{1,0:T(8,128)(2,1)}), bf16[256,1024]{1,0:T(8,128)(2,1)}) %reduce-scatter.3.cloned.1.call-update) | async-done | bytes 524304 | tf_op jit(solution)/shard_map/reduce_scatter | solution.py:189
  583.3 8.1 all-to-all-done.6
  592.0 6.4 convolution_bitcast_fusion.1
  598.4 42.0 %concatenate.13 = f32[1024,4224]{0,1:T(8,128)} concatenate(f32[1024,3072]{0,1:T(8,128)} %convolution_bitcast_fusion.1, f32[1024,1024]{0,1:T(8,128)} %fusion.42, f32[1024,1]{0,1:T(1,128)S(1)} %bitcast.222, f32[1024,1]{0,1:T(1,128)S(1)} %bitcast.219, f32[1024,1]{0,1:T(1,128)S(1)} %bitcast.223, f32[1024,1]{0,1:T(1,128)S(1)} %bitcast.220, f32[1024,1]{0,1:T(1,128)S(1)} %bitcast.226, ...), dimensions={1} | concatenate | bytes 34603008 | tf_op jit(solution)/shard_map/concatenate | solution.py:42
  640.5 18.2 copy.101
  658.7 21.3 %reshape.191 = f32[4096,1056]{1,0:T(8,128)} reshape(f32[1024,4224]{1,0:T(8,128)} %copy.101) | data formatting | bytes 34603008 | tf_op jit(solution)/shard_map/reshape | solution.py:246
  680.0 34.8 %pad_maximum_fusion = f32[4096,3104]{1,0:T(8,128)} fusion(f32[4096,1056]{1,0:T(8,128)} %reshape.191, f32[4096,1024]{1,0:T(8,128)} %fusion.41, f32[4096,1024]{1,0:T(8,128)} %fusion.27), kind=kLoop, calls=%fused_computation.17 | loop fusion | flops 25427968 | bytes 101711872 | tf_op jit(solution)/shard_map/concatenate | solution.py:245
  714.9 10.9 reshape.189
  725.8 5.8 convolution_add_fusion.4
  731.6 1083.7 %reduce-scatter.5.cloned.1.call-done = f32[128,3104]{1,0:T(8,128)} async-done(((f32[4096,3104]{1,0:T(8,128)}), f32[128,3104]{1,0:T(8,128)}) %reduce-scatter.5.cloned.1.call-update) | async-done | bytes 1589264 | tf_op jit(solution)/shard_map/reduce_scatter | solution.py:244
  (174 shorter events, 81.6 us)
Async XLA Ops:
  7.2 103.4 %all-gather.9.cloned.1.call-start = ((), (), s32[]{:S(2)}) async-start(), calls=%async_computation.10 | async-start | bytes 7077888 | tf_op jit(solution)/shard_map/all_gather | solution.py:57
  7.9 141.6 %all-gather.11.cloned.1.call-start = ((), (), s32[]{:S(2)}) async-start(), calls=%async_computation.11 | async-start | bytes 1310720 | tf_op jit(solution)/shard_map/all_gather | solution.py:85
  122.8 55.7 %all-gather.13.cloned.1.call-start = ((), (), s32[]{:S(2)}) async-start(), calls=%async_computation.12 | async-start | bytes 1310720 | tf_op jit(solution)/shard_map/all_gather | solution.py:84
  131.2 98.2 %all-gather.15.cloned.1.call-start = ((), (), s32[]{:S(2)}) async-start(), calls=%async_computation.13 | async-start | bytes 2359296 | tf_op jit(solution)/shard_map/all_gather | solution.py:58
  131.8 223.1 %all-gather.17.cloned.1.call-start = ((), (), s32[]{:S(2)}) async-start(), calls=%async_computation.14 | async-start | bytes 9437184 | tf_op jit(solution)/shard_map/all_gather | solution.py:123
  132.4 347.5 %all-gather.19.cloned.1.call-start = ((), (), s32[]{:S(2)}) async-start(), calls=%async_computation.15 | async-start | bytes 9437184 | tf_op jit(solution)/shard_map/all_gather | solution.py:124
  133.7 8.6 all-to-all-start.2
  191.7 40.0 %copy-start.15 = (f32[256,8,64]{0,2,1:T(8,128)}, f32[256,8,64]{0,2,1:T(8,128)S(1)}, u32[]{:S(2)}) copy-start(f32[256,8,64]{0,2,1:T(8,128)S(1)} %get-tuple-element.88) | copy-start | bytes 1572868
  191.7 37.8 %copy-start.8 = (bf16[128,1024]{1,0:T(8,128)(2,1)S(1)}, bf16[128,1024]{1,0:T(8,128)(2,1)}, u32[]{:S(2)}) copy-start(bf16[128,1024]{1,0:T(8,128)(2,1)} %param.12) | copy-start | bytes 786436
  192.6 36.9 %all-to-all-start.3 = ((bf16[2,128,512]{1,2,0:T(8,128)(2,1)}), bf16[2,128,512]{1,2,0:T(8,128)(2,1)S(1)}, u32[]{:S(2)}, u32[]{:S(2)}) async-start(bf16[2,128,512]{1,2,0:T(8,128)(2,1)} %copy.91), calls=%async_computation.3 | async-start | bytes 524288 | tf_op jit(solution)/shard_map/all_to_all | solution.py:112
  229.5 125.4 %copy-start.13 = (bf16[2,128,512]{1,2,0:T(8,128)(2,1)}, bf16[2,128,512]{1,2,0:T(8,128)(2,1)S(1)}, u32[]{:S(2)}) copy-start(bf16[2,128,512]{1,2,0:T(8,128)(2,1)S(1)} %all-to-all-done.3) | copy-start | bytes 786436
  231.7 262.1 %copy-start = (f32[128,1024]{1,0:T(8,128)}, f32[128,1024]{1,0:T(8,128)S(1)}, u32[]{:S(2)}) copy-start(f32[128,1024]{1,0:T(8,128)S(1)} %get-tuple-element.318) | copy-start | bytes 1572868
  365.9 119.0 %copy-start.4 = (bf16[128,4096]{1,0:T(8,128)(2,1)}, bf16[128,4096]{1,0:T(8,128)(2,1)S(1)}, u32[]{:S(2)}) copy-start(bf16[128,4096]{1,0:T(8,128)(2,1)S(1)} %get-tuple-element.296) | copy-start | bytes 3145732
  479.9 6.7 slice-start
  480.0 6.7 slice-start.1
  485.4 6.7 slice-start.2
  486.6 5.5 copy-start.20
  486.7 5.4 slice-start.3
  495.7 10.5 copy-start.16
  497.3 8.6 all-to-all-start.4
  500.7 68.0 %reduce-scatter.3.cloned.1.call-start = ((), (), s32[]{:S(2)}) async-start(), calls=%async_computation.16 | async-start | bytes 2621440 | tf_op jit(solution)/shard_map/reduce_scatter | solution.py:189
  526.2 188.7 %all-gather.21.cloned.1.call-start = ((), (), s32[]{:S(2)}) async-start(), calls=%async_computation.17 | async-start | bytes 7077888 | tf_op jit(solution)/shard_map/all_gather | solution.py:139
  528.7 8.2 copy-start.1
  528.7 8.2 copy-start.3
  545.0 29.0 %copy-start.12 = (bf16[128,1024]{1,0:T(8,128)(2,1)S(1)}, bf16[128,1024]{1,0:T(8,128)(2,1)}, u32[]{:S(2)}) copy-start(bf16[128,1024]{1,0:T(8,128)(2,1)} %copy-done.11) | copy-start | bytes 786436
  545.0 29.0 %copy-start.14 = (bf16[2,128,512]{1,2,0:T(8,128)(2,1)S(1)}, bf16[2,128,512]{1,2,0:T(8,128)(2,1)}, u32[]{:S(2)}) copy-start(bf16[2,128,512]{1,2,0:T(8,128)(2,1)} %copy-done.13) | copy-start | bytes 786436
  547.0 23.6 %all-to-all-start.5 = ((bf16[2,128,512]{1,2,0:T(8,128)(2,1)}), bf16[2,128,512]{1,2,0:T(8,128)(2,1)S(1)}, u32[]{:S(2)}, u32[]{:S(2)}) async-start(bf16[2,128,512]{1,2,0:T(8,128)(2,1)} %copy.96), calls=%async_computation.5 | async-start | bytes 524288 | tf_op jit(solution)/shard_map/all_to_all | solution.py:196
  570.6 8.7 all-to-all-start.7
  579.3 12.1 all-to-all-start.6
  582.8 1232.6 %reduce-scatter.5.cloned.1.call-start = ((), (), s32[]{:S(2)}) async-start(), calls=%async_computation.18 | async-start | bytes 54067200 | tf_op jit(solution)/shard_map/reduce_scatter | solution.py:244
  583.3 8.7 copy-start.9
  714.8 11.0 copy-start.18
  (12 other events, 33.3 us)
Sparse Core Ops, SparseCore 0:
  10.1 100.3 all-gather.8
  122.9 26.4 all-gather.10
  151.0 27.4 all-gather.12
  180.5 48.9 all-gather.14
  231.5 123.4 all-gather.16
  356.9 123.0 all-gather.18
  526.3 42.4 reduce-scatter.2
  571.0 98.3 all-gather.20
  715.0 1100.3 reduce-scatter.4
where the time goes:
time: 1830 us
  waiting for transfers between devices  1480 us (81%)
  local copies, waits for them, and re-layouts  122 us (7%)
  matrix products  82.4 us (5%)
  blocking collectives  71.5 us (4%)
  other arithmetic  39.1 us (2%)
  starting transfers between devices  21.5 us (1%)
    reduce_scatter x1, waiting for transfers between devices, body(): lax.psum_scatter(jnp.concatenate([ffn_block, attn_block.reshape(lax.axis_...  1080 us
    all_gather x1, waiting for transfers between devices, body(): part_in = lax.all_gather(fc_in, ('head', 'blk'), axis=0, tiled=True)  123 us
    all_gather x1, waiting for transfers between devices, body(): part_out = lax.all_gather(fc_out, ('head', 'blk'), axis=0, tiled=True)  114 us
    all_gather x1, waiting for transfers between devices, body(): part_qkv = lax.all_gather(w_qkv, ('head', 'blk'), axis=0, tiled=True)  74.8 us
    concatenate x2, local copies, waits for them, and re-layouts, attn_part(): jnp.concatenate([jnp.einsum('tn,tc->nc', tokens, grad_proj, preferred_ele...  60.3 us
  transfers between devices with their start and end apart: 15, of which 12 were waited for; matrix products, arithmetic and copies ran while one was open for 11% of the time, Pallas kernels for 0%

commit v1 on v0

--- a/solution.py
+++ b/solution.py
@@ -3,6 +3,8 @@
 import jax
 import jax.numpy as jnp
 from jax import lax
+from jax.experimental import pallas as pl
+from jax.experimental.pallas import tpu as pltpu
 from jax.sharding import PartitionSpec as P
 
 HEAD_DIM = 64
@@ -49,7 +51,7 @@
     )
 
 
-def body(tokens, out_grad, w_qkv, w_out, fc_in, fc_out, fc_in_bias, vectors):
+def general_body(tokens, out_grad, w_qkv, w_out, fc_in, fc_out, fc_in_bias, vectors):
     model_width = tokens.shape[1]
     hidden_units = fc_in.shape[0] * lax.axis_size(("head", "blk"))
     ratio = hidden_units // model_width
@@ -271,9 +273,385 @@
     )
 
 
+GROUP = ("head", "blk")
+FLIP = ((0, 1), (1, 0))
+PAIRS = ((0, 1), (1, 0), (2, 3), (3, 2))
+INNER = ((1, 2), (2, 1))
+OUTER = ((1, 0), (2, 3))
+INWARD = ((0, 1), (3, 2))
+CORE = tuple((at, at ^ 1) for at in range(4))
+ACROSS = tuple((at, at ^ 2) for at in range(4))
+
+
+def group_rank():
+    return lax.axis_index("head") * 4 + lax.axis_index("blk")
+
+
+def inner_blk():
+    at = lax.axis_index("blk")
+    return (at == 1) | (at == 2)
+
+
+def gather_blk(own):
+    first = lax.ppermute(own, "blk", PAIRS)
+    middle = lax.ppermute(own, "blk", INNER)
+    second_in = lax.ppermute(first, "blk", INNER)
+    second_out = lax.ppermute(middle, "blk", OUTER)
+    third = lax.ppermute(second_in, "blk", OUTER)
+    inner = inner_blk()
+    return [own, first, jnp.where(inner, second_in, second_out), jnp.where(inner, middle, third)]
+
+
+def gather_group(own):
+    slots = gather_blk(own)
+    slots = slots + [lax.ppermute(slot, "head", FLIP) for slot in slots]
+    rank = group_rank()
+    whole = jnp.zeros((8,) + own.shape, own.dtype)
+    for at, slot in enumerate(slots):
+        whole = lax.dynamic_update_slice_in_dim(whole, slot[None], rank ^ at, 0)
+    return whole
+
+
+def scatter_group(terms):
+    row, at = lax.axis_index("head"), lax.axis_index("blk")
+    away = lax.dynamic_slice_in_dim(terms, (1 - row) * 4, 4, 0).astype(jnp.bfloat16)
+    near = lax.dynamic_slice_in_dim(terms, row * 4, 4, 0)
+    near = near.astype(jnp.float32) + lax.ppermute(away, "head", FLIP).astype(jnp.float32)
+    slots = [lax.dynamic_index_in_dim(near, at ^ k, 0, keepdims=False) for k in range(4)]
+    inner = inner_blk()
+    low = jnp.bfloat16
+    from_three = lax.ppermute(slots[3].astype(low), "blk", INWARD).astype(jnp.float32)
+    from_two = lax.ppermute(slots[2].astype(low), "blk", INWARD).astype(jnp.float32)
+    second = slots[2] + from_three
+    third = slots[3] + from_two
+    to_first = lax.ppermute(second.astype(low), "blk", INNER).astype(jnp.float32)
+    to_own = lax.ppermute(third.astype(low), "blk", INNER).astype(jnp.float32)
+    first = slots[1] + to_first
+    return slots[0] + lax.ppermute(first.astype(low), "blk", PAIRS).astype(jnp.float32) + to_own
+
+
+def gather_seq(own):
+    across = lax.ppermute(own, "seq", ACROSS)
+    return [own, lax.ppermute(own, "seq", CORE), across, lax.ppermute(across, "seq", CORE)]
+
+
+def scatter_seq(terms):
+    low = jnp.bfloat16
+    sent = lax.ppermute(jnp.stack([terms[1].astype(low), terms[3].astype(low)]), "seq", CORE)
+    near = terms[0].astype(jnp.float32) + sent[0].astype(jnp.float32)
+    far = terms[2].astype(jnp.float32) + sent[1].astype(jnp.float32)
+    return near + lax.ppermute(far.astype(low), "seq", ACROSS).astype(jnp.float32)
+
+
+def put_slots(slots, rank):
+    whole = jnp.zeros((len(slots),) + slots[0].shape, slots[0].dtype)
+    for at, slot in enumerate(slots):
+        whole = lax.dynamic_update_slice_in_dim(whole, slot[None], rank ^ at, 0)
+    return whole
+
+
+ROWS_DIMS = (((1,), (1,)), ((), ()))
+COLS_DIMS = (((0,), (0,)), ((), ()))
+
+
+def attend_kernel(q_ref, k_ref, v_ref, mixed_ref, weights_ref, inverse_ref):
+    for at in range(q_ref.shape[1] // HEAD_DIM):
+        cols = slice(at * HEAD_DIM, (at + 1) * HEAD_DIM)
+        scores = lax.dot_general(
+            q_ref[:, cols], k_ref[:, cols], ROWS_DIMS, preferred_element_type=jnp.float32
+        )
+        weights = jnp.exp(scores - jnp.max(scores, axis=-1, keepdims=True))
+        inverse = 1.0 / jnp.sum(weights, axis=-1, keepdims=True)
+        weights = weights.astype(jnp.bfloat16)
+        weights_ref[at] = weights
+        mixed_ref[:, cols] = (
+            jnp.dot(weights, v_ref[:, cols], preferred_element_type=jnp.float32) * inverse
+        )
+        inverse_ref[:, cols] = jnp.broadcast_to(inverse, (inverse.shape[0], HEAD_DIM))
+
+
+def attend(queries, keys, values):
+    rows, width = queries.shape
+    heads = width // HEAD_DIM
+    block = 256
+    return pl.pallas_call(
+        attend_kernel,
+        grid=(rows // block,),
+        in_specs=[
+            pl.BlockSpec((block, width), lambda i: (i, 0)),
+            pl.BlockSpec((rows, width), lambda i: (0, 0)),
+            pl.BlockSpec((rows, width), lambda i: (0, 0)),
+        ],
+        out_specs=[
+            pl.BlockSpec((block, width), lambda i: (i, 0)),
+            pl.BlockSpec((heads, block, rows), lambda i: (0, i, 0)),
+            pl.BlockSpec((block, width), lambda i: (i, 0)),
+        ],
+        out_shape=[
+            jax.ShapeDtypeStruct((rows, width), jnp.float32),
+            jax.ShapeDtypeStruct((heads, rows, rows), jnp.bfloat16),
+            jax.ShapeDtypeStruct((rows, width), jnp.float32),
+        ],
+        compiler_params=pltpu.CompilerParams(vmem_limit_bytes=32 * 2**20),
+        cost_estimate=pl.CostEstimate(
+            flops=4 * rows * rows * width,
+            bytes_accessed=heads * rows * rows * 2 + 8 * rows * width * 2,
+            transcendentals=heads * rows * rows,
+        ),
+    )(queries, keys, values)
+
+
+def attend_back_kernel(
+    grad_ref, mixed_ref, inverse_ref, q_ref, weights_ref, k_ref, v_ref,
+    dq_ref, dk_ref, dv_ref, dk_sum, dv_sum,
+):
+    step = pl.program_id(0)
+
+    @pl.when(step == 0)
+    def _():
+        dk_sum[...] = jnp.zeros_like(dk_sum)
+        dv_sum[...] = jnp.zeros_like(dv_sum)
+
+    for at in range(q_ref.shape[1] // HEAD_DIM):
+        cols = slice(at * HEAD_DIM, (at + 1) * HEAD_DIM)
+        grad = grad_ref[:, cols]
+        inverse = inverse_ref[:, cols]
+        delta = jnp.sum(grad.astype(jnp.float32) * mixed_ref[:, cols], axis=-1, keepdims=True)
+        weights = weights_ref[at]
+        dprobs = lax.dot_general(
+            grad, v_ref[:, cols], ROWS_DIMS, preferred_element_type=jnp.float32
+        )
+        dscores = (weights.astype(jnp.float32) * (dprobs - delta)).astype(jnp.bfloat16)
+        dq = jnp.dot(dscores, k_ref[:, cols], preferred_element_type=jnp.float32) * inverse
+        dq_ref[:, cols] = dq.astype(jnp.bfloat16)
+        q_scaled = (q_ref[:, cols].astype(jnp.float32) * inverse).astype(jnp.bfloat16)
+        dk_sum[:, cols] += lax.dot_general(
+            dscores, q_scaled, COLS_DIMS, preferred_element_type=jnp.float32
+        )
+        g_scaled = (grad.astype(jnp.float32) * inverse).astype(jnp.bfloat16)
+        dv_sum[:, cols] += lax.dot_general(
+            weights, g_scaled, COLS_DIMS, preferred_element_type=jnp.float32
+        )
+
+    @pl.when(step == pl.num_programs(0) - 1)
+    def _():
+        dk_ref[...] = dk_sum[...].astype(jnp.bfloat16)
+        dv_ref[...] = dv_sum[...].astype(jnp.bfloat16)
+
+
+def attend_back(grad, mixed, inverse, queries, weights, keys, values):
+    rows, width = queries.shape
+    heads = width // HEAD_DIM
+    block = 256
+    per_block = pl.BlockSpec((block, width), lambda i: (i, 0))
+    whole = pl.BlockSpec((rows, width), lambda i: (0, 0))
+    return pl.pallas_call(
+        attend_back_kernel,
+        grid=(rows // block,),
+        in_specs=[
+            per_block, per_block, per_block, per_block,
+            pl.BlockSpec((heads, block, rows), lambda i: (0, i, 0)),
+            whole, whole,
+        ],
+        out_specs=[per_block, whole, whole],
+        out_shape=[jax.ShapeDtypeStruct((rows, width), jnp.bfloat16)] * 3,
+        scratch_shapes=[pltpu.VMEM((rows, width), jnp.float32)] * 2,
+        compiler_params=pltpu.CompilerParams(vmem_limit_bytes=32 * 2**20),
+        cost_estimate=pl.CostEstimate(
+            flops=8 * rows * rows * width,
+            bytes_accessed=heads * rows * rows * 2 + 12 * rows * width * 2,
+            transcendentals=0,
+        ),
+    )(grad, mixed, inverse, queries, weights, keys, values)
+
+
+def normalize(values):
+    center = values - jnp.mean(values, axis=-1, keepdims=True)
+    scale = lax.rsqrt(jnp.mean(center * center, axis=-1, keepdims=True) + 1e-05)
+    return center * scale, scale
+
+
+def normalize_back(cotangent, gain, normed, scale):
+    dn = cotangent * gain
+    inner = jnp.mean(dn, axis=-1, keepdims=True)
+    outer = jnp.mean(dn * normed, axis=-1, keepdims=True)
+    return scale * (dn - inner - normed * outer)
+
+
+def dot_rows(left, right):
+    return lax.dot_general(left, right, ROWS_DIMS, preferred_element_type=jnp.float32)
+
+
+def dot_cols(left, right):
+    return lax.dot_general(left, right, COLS_DIMS, preferred_element_type=jnp.float32)
+
+
+def dot(left, right):
+    return jnp.dot(left, right, preferred_element_type=jnp.float32)
+
+
+def grouped_body(tokens, out_grad, w_qkv, w_out, fc_in, fc_out, fc_in_bias, vectors):
+    rows, width = tokens.shape
+    low = jnp.bfloat16
+    scale = HEAD_DIM ** (-0.5)
+    seq_at = lax.axis_index("seq")
+    core_at = lax.rem(seq_at, 2)
+    rank = group_rank()
+    own = width // 8
+
+    quarter = own // 4
+    qkv_rows = lax.dynamic_slice_in_dim(w_qkv, seq_at * quarter, quarter, 0)
+    qkv_rows = qkv_rows.reshape(quarter, 3, 8, own).transpose(2, 0, 1, 3).reshape(8, quarter * 3, own)
+    small = jnp.concatenate([vectors.T, fc_in_bias.reshape(-1, own)], axis=0)
+    small = jnp.broadcast_to(small[None], (8,) + small.shape)
+    swapped = lax.all_to_all(jnp.concatenate([qkv_rows, small], axis=1), GROUP, 0, 0, tiled=True)
+    vec = swapped[:, quarter * 3 : quarter * 3 + 8].transpose(1, 0, 2).reshape(8, width).astype(jnp.float32)
+    bias_all = swapped[:, quarter * 3 + 8 :]
+    gain_one, gain_two, shift_one, shift_two = (vec[at] for at in range(4))
+    bias_output, bias_ffn = vec[6], vec[7]
+    bias_query, bias_value = (vectors[:, at].astype(jnp.float32) for at in (4, 5))
+    qkv_parts = put_slots(gather_seq(swapped[:, : quarter * 3]), seq_at)
+    qkv_cols = qkv_parts.reshape(4, 8, quarter, 3 * own).transpose(1, 0, 2, 3).reshape(width, 3 * own)
+
+    seq_tokens = gather_group(tokens).reshape(8 * rows, width)
+
+    out_half = gather_group(lax.dynamic_slice_in_dim(w_out, core_at * (own // 2), own // 2, 0))
+    out_parts = jnp.zeros((2,) + out_half.shape, low)
+    out_parts = lax.dynamic_update_slice_in_dim(out_parts, out_half[None], core_at, 0)
+    out_parts = lax.dynamic_update_slice_in_dim(
+        out_parts, lax.ppermute(out_half, "seq", CORE)[None], 1 - core_at, 0
+    )
+    out_full = out_parts.transpose(1, 0, 2, 3).reshape(width, width)
+
+    unit_rows = fc_in.shape[0] // 4
+    ffn_own = jnp.stack(
+        [
+            lax.dynamic_slice_in_dim(fc_in, seq_at * unit_rows, unit_rows, 0),
+            lax.dynamic_slice_in_dim(fc_out, seq_at * unit_rows, unit_rows, 0),
+        ]
+    )
+    ffn_weights = gather_group(ffn_own)
+    units = 8 * unit_rows
+    ffn_in = ffn_weights[:, 0].reshape(units, width)
+    ffn_out = ffn_weights[:, 1].reshape(units, width)
+    ffn_bias = lax.dynamic_index_in_dim(bias_all, seq_at, 1, keepdims=False).reshape(units).astype(jnp.float32)
+
+    projected = dot(seq_tokens, qkv_cols)
+    queries = ((projected[:, :own] + bias_query) * scale).astype(low)
+    keys = projected[:, own : 2 * own].astype(low)
+    values = (projected[:, 2 * own :] + bias_value).astype(low)
+    mixed, weights, inverse = attend(queries, keys, values)
+    context = lax.all_to_all(mixed.astype(low).reshape(8, rows, own), GROUP, 0, 0, tiled=True)
+    context = context.transpose(1, 0, 2).reshape(rows, width)
+
+    attn_out = dot(context, out_full) + bias_output
+    norm_one, scale_one = normalize(tokens.astype(jnp.float32) + attn_out)
+    middle = norm_one * gain_one + shift_one
+    middle_all = jnp.concatenate(gather_seq(middle.astype(low)), axis=0)
+    pre_act = dot_rows(middle_all, ffn_in) + ffn_bias
+    cdf = 0.5 * (1.0 + lax.erf(pre_act * (0.5**0.5)))
+    act = (pre_act * cdf).astype(low)
+    slope = cdf + pre_act * jnp.exp(-0.5 * pre_act * pre_act) * ((2.0 * math.pi) ** -0.5)
+    summed = scatter_seq(dot(act, ffn_out).reshape(4, rows, width))
+    norm_two, scale_two = normalize(middle + summed + bias_ffn)
+    layer_output = norm_two * gain_two + shift_two
+
+    cotangent = out_grad.astype(jnp.float32)
+    grad_two = normalize_back(cotangent, gain_two, norm_two, scale_two)
+    grad_ffn = grad_two.astype(low)
+    grad_ffn_all = jnp.concatenate(gather_seq(grad_ffn), axis=0)
+    grad_pre_float = dot_rows(grad_ffn_all, ffn_out) * slope
+    grad_pre = grad_pre_float.astype(low)
+    grad_mid = grad_two + scatter_seq(dot(grad_pre, ffn_in).reshape(4, rows, width))
+    grad_one = normalize_back(grad_mid, gain_one, norm_one, scale_one)
+    grad_attn = grad_one.astype(low)
+    grad_context = dot_rows(grad_attn, out_full).astype(low)
+    grad_context = lax.all_to_all(
+        grad_context.reshape(rows, 8, own).transpose(1, 0, 2), GROUP, 0, 0, tiled=True
+    ).reshape(8 * rows, own)
+    dq, dk, dv = attend_back(grad_context, mixed, inverse, queries, weights, keys, values)
+    grad_cols = jnp.concatenate([dq * low(scale), dk, dv], axis=1)
+    grad_proj = lax.all_to_all(grad_cols.reshape(8, rows, 3 * own), GROUP, 0, 0, tiled=True)
+    grad_proj = grad_proj.reshape(8, rows, 3, own).transpose(1, 2, 0, 3).reshape(rows, 3 * width)
+
+    qkv_quarter = gather_group(lax.dynamic_slice_in_dim(w_qkv, seq_at * quarter, quarter, 0))
+    qkv_full = put_slots(gather_seq(qkv_quarter), seq_at)
+    qkv_full = qkv_full.transpose(1, 0, 2, 3).reshape(width, 3 * width)
+    input_grad = grad_one + dot_rows(grad_proj, qkv_full)
+
+    ffn_terms = jnp.stack(
+        [
+            dot_cols(grad_pre, middle_all).reshape(8, unit_rows, width),
+            dot_cols(act, grad_ffn_all).reshape(8, unit_rows, width),
+        ],
+        axis=1,
+    )
+    ffn_grads = scatter_group(ffn_terms).astype(low)
+    moves = []
+    for seq_from in range(4):
+        for rank_from in range(8):
+            moves.append((seq_from * 8 + rank_from, rank_from * 4 + seq_from))
+    ffn_grads = lax.ppermute(ffn_grads, ("seq", "head", "blk"), moves).astype(jnp.float32)
+
+    context_parts = context.reshape(rows, 4, width // 4)
+    parts = [lax.dynamic_index_in_dim(context_parts, seq_at ^ at, 1, keepdims=False) for at in range(4)]
+    parts = [
+        parts[0],
+        lax.ppermute(parts[1], "seq", CORE),
+        lax.ppermute(parts[2], "seq", ACROSS),
+        lax.ppermute(parts[3], "seq", tuple((at, at ^ 3) for at in range(4))),
+    ]
+    grad_attn_all = jnp.concatenate(gather_seq(grad_attn), axis=0)
+    out_terms = dot_cols(jnp.concatenate(parts, axis=0), grad_attn_all)
+    grad_w_out = scatter_group(out_terms.reshape(8, quarter, width))
+
+    qkv_terms = dot_cols(seq_tokens, grad_cols).reshape(32, quarter * 3, own)
+    grad_cols_sum = jnp.sum(grad_cols.astype(jnp.float32), axis=0).reshape(3, own)
+    col_sums = lax.dynamic_update_slice(
+        jnp.zeros((2, width), jnp.float32),
+        jnp.stack([grad_cols_sum[0], grad_cols_sum[2]]),
+        (0, rank * own),
+    )
+    token_sums = jnp.stack(
+        [
+            jnp.sum(grad_mid * norm_one, axis=0),
+            jnp.sum(cotangent * norm_two, axis=0),
+            jnp.sum(grad_mid, axis=0),
+            jnp.sum(cotangent, axis=0),
+            col_sums[0],
+            col_sums[1],
+            jnp.sum(grad_attn.astype(jnp.float32), axis=0),
+            jnp.sum(grad_ffn.astype(jnp.float32), axis=0),
+        ]
+    )
+    token_sums = token_sums.reshape(8, 32, quarter).transpose(1, 0, 2).reshape(32, -1, own)
+    unit_sums = jnp.sum(grad_pre.astype(jnp.float32), axis=0).reshape(8, 1, unit_rows)
+    unit_sums = lax.dynamic_update_slice(
+        jnp.zeros((8, 4, unit_rows), jnp.float32), unit_sums, (0, seq_at, 0)
+    ).reshape(32, 1, unit_rows)
+    payload = jnp.concatenate([qkv_terms, token_sums, unit_sums], axis=1).reshape(4, 8, -1, own)
+    payload = scatter_seq([lax.dynamic_index_in_dim(payload, seq_at ^ at, 0, keepdims=False) for at in range(4)])
+    payload = lax.all_to_all(payload.astype(low), GROUP, 0, 0, tiled=True).astype(jnp.float32)
+    grad_w_qkv = payload[:, : quarter * 3].reshape(8, quarter, 3, own).transpose(1, 2, 0, 3).reshape(quarter, -1)
+    sums = jnp.sum(payload[:, quarter * 3 :], axis=0)
+    grad_vectors = sums[:2].reshape(8, quarter).T
+    grad_bias = sums[2]
+    return (
+        layer_output,
+        input_grad,
+        grad_w_qkv,
+        grad_w_out,
+        ffn_grads[0],
+        ffn_grads[1],
+        grad_bias,
+        grad_vectors,
+    )
+
+
 def solution(mesh):
+    sizes = tuple(mesh.shape[name] for name in ("seq", "head", "blk"))
     return jax.shard_map(
-        body,
+        grouped_body if sizes == (4, 2, 4) else general_body,
         mesh=mesh,
         in_specs=(
             P(("seq", "head", "blk"), None),

time: 1830 us -> 454 us (0.25)
  the two profiles are of different devices: /device:TPU:2 before, /device:TPU:6 now
where the time goes in v1:
time: 454 us; the launch traced here: 452 us
  waiting for transfers between devices  174 us (38%)
  starting transfers between devices  112 us (25%)
  local copies, waits for them, and re-layouts  75 us (17%)
  matrix products  40.6 us (9%)
  other arithmetic  36.4 us (8%)
  Pallas kernels  12.5 us (3%)
    ppermute x5, waiting for transfers between devices, gather_seq(): across = lax.ppermute(own, 'seq', ACROSS)  36.2 us
    ppermute x16, waiting for transfers between devices, gather_group(): slots = slots + [lax.ppermute(slot, 'head', FLIP) for slot in slots]  36.2 us
    ppermute x2, waiting for transfers between devices, scatter_group(): lax.ppermute(away, 'head', FLIP).astype(jnp.float32)  25 us
    dynamic_update_slice x23, local copies, waits for them, and re-layouts, gather_group(): whole = lax.dynamic_update_slice_in_dim(whole, slot[None], rank ^ at, 0)  23.2 us
    ppermute x4, waiting for transfers between devices, gather_blk(): third = lax.ppermute(second_in, 'blk', OUTER)  21.4 us
    ppermute x1, waiting for transfers between devices, grouped_body(): lax.ppermute(ffn_grads, ('seq', 'head', 'blk'), moves).astype(jnp.float32)  18.3 us
    dot_general x4, matrix products, dot_rows(): lax.dot_general(left, right, ROWS_DIMS, preferred_element_type=jnp.float32)  16.6 us
    dot_general x4, matrix products, dot_cols(): lax.dot_general(left, right, COLS_DIMS, preferred_element_type=jnp.float32)  15 us
  transfers between devices with their start and end apart: 79, of which 29 were waited for; matrix products, arithmetic and copies ran while one was open for 32% of the time, Pallas kernels for 3%

profile of v1, /device:TPU:6, one launch (start us, length us, event | category | flops | bytes accessed | tf_op | source)
XLA Modules:
  0.0 451.8 jit_solution(992570517612242700)
XLA Ops:
  5.3 4.4 collective-permute-start.12
  14.1 5.5 %all-to-all-start = ((bf16[8,108,128]{2,1,0:T(8,128)(2,1)}), bf16[8,108,128]{2,1,0:T(8,128)(2,1)S(1)}, u32[]{:S(2)}, u32[]{:S(2)}) async-start(bf16[8,108,128]{2,1,0:T(8,128)(2,1)} %copy.52), calls=%async_computation | async-start | bytes 458752 | tf_op jit(solution)/shard_map/all_to_all | solution.py:507
  35.6 4.9 %collective-permute-done.15 = bf16[64,1024]{1,0:T(8,128)(2,1)S(1)} collective-permute-done((bf16[64,1024]{1,0:T(8,128)(2,1)S(1)}, bf16[64,1024]{1,0:T(8,128)(2,1)S(1)}, u32[]{:S(2)}, u32[]{:S(2)}) %collective-permute-start.15) | collective-permute-done | bytes 131104 | tf_op jit(solution)/shard_map/ppermute | solution.py:299
  46.2 4.4 collective-permute-done.16
  52.3 4.4 collective-permute-done.18
  64.4 4.8 %collective-permute-done.44 = bf16[32,3072]{1,0:T(8,128)(2,1)S(1)} collective-permute-done((bf16[32,3072]{1,0:T(8,128)(2,1)S(1)}, bf16[32,3072]{1,0:T(8,128)(2,1)S(1)}, u32[]{:S(2)}, u32[]{:S(2)}) %collective-permute-start.44) | collective-permute-done | bytes 196640 | tf_op jit(solution)/shard_map/ppermute | solution.py:299
  71.3 4.3 collective-permute-done.20
  86.9 6.4 %collective-permute-done.10 = bf16[8,96,128]{2,1,0:T(8,128)(2,1)S(1)} collective-permute-done((bf16[8,96,128]{2,1,0:T(8,128)(2,1)S(1)}, bf16[8,96,128]{2,1,0:T(8,128)(2,1)S(1)}, u32[]{:S(2)}, u32[]{:S(2)}) %collective-permute-start.10) | collective-permute-done | bytes 196640 | tf_op jit(solution)/shard_map/ppermute | solution.py:334
  94.6 6.7 %collective-permute-done.45 = bf16[32,3072]{1,0:T(8,128)(2,1)S(1)} collective-permute-done((bf16[32,3072]{1,0:T(8,128)(2,1)S(1)}, bf16[32,3072]{1,0:T(8,128)(2,1)S(1)}, u32[]{:S(2)}, u32[]{:S(2)}) %collective-permute-start.45) | collective-permute-done | bytes 196640 | tf_op jit(solution)/shard_map/ppermute | solution.py:300
  121.0 6.6 %collective-permute-done.7 = bf16[128,1024]{1,0:T(8,128)(2,1)S(1)} collective-permute-done((bf16[128,1024]{1,0:T(8,128)(2,1)S(1)}, bf16[128,1024]{1,0:T(8,128)(2,1)S(1)}, u32[]{:S(2)}, u32[]{:S(2)}) %collective-permute-start.7) | collective-permute-done | bytes 262176 | tf_op jit(solution)/shard_map/ppermute | solution.py:307
  137.5 5.2 %shard_map.143 = (f32[1024,128]{1,0:T(8,128)S(1)}, bf16[2,1024,1024]{2,1,0:T(8,128)(2,1)S(1)}, f32[1024,128]{1,0:T(8,128)S(1)}) custom-call(bf16[1024,128]{1,0:T(8,128)(2,1)S(1)} %get-tuple-element.67.q_ref, bf16[1024,128]{1,0:T(8,128)(2,1)S(1)} %slice.269.k_ref, bf16[1024,128]{1,0:T(8,128)(2,1)S(1)} %get-tuple-element.66.v_ref), custom_call_target="tpu_custom_call" | custom-call | flops 536870912 | bytes 6291456 | tf_op jit(solution)/shard_map/pallas_call | solution.py:377
  145.5 6.3 %all-to-all-start.1 = ((bf16[8,128,128]{1,2,0:T(8,128)(2,1)}), bf16[8,128,128]{1,2,0:T(8,128)(2,1)S(1)}, u32[]{:S(2)}, u32[]{:S(2)}) async-start(bf16[8,128,128]{1,2,0:T(8,128)(2,1)} %copy.54), calls=%async_computation.1 | async-start | bytes 524288 | tf_op jit(solution)/shard_map/all_to_all | solution.py:544
  162.0 8.8 %collective-permute-done.29 = bf16[2,128,1024]{2,1,0:T(8,128)(2,1)S(1)} collective-permute-done((bf16[2,128,1024]{2,1,0:T(8,128)(2,1)}, bf16[2,128,1024]{2,1,0:T(8,128)(2,1)S(1)}, u32[]{:S(2)}, u32[]{:S(2)}) %collective-permute-start.29) | collective-permute-done | bytes 524320 | tf_op jit(solution)/shard_map/ppermute | solution.py:300
  180.5 6.0 %collective-permute-done.32 = bf16[2,128,1024]{2,1,0:T(8,128)(2,1)S(1)} collective-permute-done((bf16[2,128,1024]{2,1,0:T(8,128)(2,1)S(1)}, bf16[2,128,1024]{2,1,0:T(8,128)(2,1)S(1)}, u32[]{:S(2)}, u32[]{:S(2)}) %collective-permute-start.32) | collective-permute-done | bytes 524320 | tf_op jit(solution)/shard_map/ppermute | solution.py:307
  187.8 6.7 %collective-permute-done.33 = bf16[2,128,1024]{2,1,0:T(8,128)(2,1)S(1)} collective-permute-done((bf16[2,128,1024]{2,1,0:T(8,128)(2,1)S(1)}, bf16[2,128,1024]{2,1,0:T(8,128)(2,1)S(1)}, u32[]{:S(2)}, u32[]{:S(2)}) %collective-permute-start.33) | collective-permute-done | bytes 524320 | tf_op jit(solution)/shard_map/ppermute | solution.py:307
  209.4 5.5 %collective-permute-done.35 = bf16[128,1024]{1,0:T(8,128)(2,1)S(1)} collective-permute-done((bf16[128,1024]{1,0:T(8,128)(2,1)S(1)}, bf16[128,1024]{1,0:T(8,128)(2,1)S(1)}, u32[]{:S(2)}, u32[]{:S(2)}) %collective-permute-start.35) | collective-permute-done | bytes 262176 | tf_op jit(solution)/shard_map/ppermute | solution.py:343
  230.9 23.3 %collective-permute-done.37 = bf16[128,1024]{1,0:T(8,128)(2,1)} collective-permute-done((bf16[128,1024]{1,0:T(8,128)(2,1)}, bf16[128,1024]{1,0:T(8,128)(2,1)}, u32[]{:S(2)}, u32[]{:S(2)}) %collective-permute-start.37) | collective-permute-done | bytes 262176 | tf_op jit(solution)/shard_map/ppermute | solution.py:334
  257.0 4.5 convert_reduce_fusion
  268.4 4.8 %fusion.53 = f32[1024,1024]{1,0:T(8,128)} fusion(bf16[512,1024]{1,0:T(8,128)(2,1)} %copy-done.55, bf16[128,1024]{1,0:T(8,128)(2,1)} %copy-done.48, bf16[128,1024]{1,0:T(8,128)(2,1)} %copy-done.46, bf16[128,1024]{1,0:T(8,128)(2,1)} %copy-done.47, bf16[128,1024]{1,0:T(8,128)(2,1)S(1)} %copy-done.17), kind=kOutput, calls=%fused_computation.163 | convolution fusion | flops 1077936128 | bytes 6291456 | tf_op jit(solution)/shard_map/dot_general | solution.py:486
  274.9 4.3 fusion.52
  288.4 4.4 all-to-all-start.2
  297.9 6.5 %collective-permute-done.59 = bf16[128,1024]{1,0:T(8,128)(2,1)} collective-permute-done((bf16[128,1024]{1,0:T(8,128)(2,1)S(1)}, bf16[128,1024]{1,0:T(8,128)(2,1)}, u32[]{:S(2)}, u32[]{:S(2)}) %collective-permute-start.59) | collective-permute-done | bytes 262176 | tf_op jit(solution)/shard_map/ppermute | solution.py:334
  306.6 7.3 %shard_map.144 = (bf16[1024,128]{1,0:T(8,128)(2,1)S(1)}, bf16[1024,128]{1,0:T(8,128)(2,1)S(1)}, bf16[1024,128]{1,0:T(8,128)(2,1)S(1)}) custom-call(bf16[1024,128]{1,0:T(8,128)(2,1)S(1)} %bitcast.274, f32[1024,128]{1,0:T(8,128)S(1)} %get-tuple-element.14.mixed_ref, f32[1024,128]{1,0:T(8,128)S(1)} %get-tuple-element.15.inverse_ref, ...), custom_call_target="tpu_custom_call" | custom-call | flops 1073741824 | bytes 7340032 | tf_op jit(solution)/shard_map/pallas_call | solution.py:448
  324.7 25.0 %collective-permute-done.61 = bf16[4,32,1024]{2,1,0:T(8,128)(2,1)S(1)} collective-permute-done((bf16[4,32,1024]{2,1,0:T(8,128)(2,1)S(1)}, bf16[4,32,1024]{2,1,0:T(8,128)(2,1)S(1)}, u32[]{:S(2)}, u32[]{:S(2)}) %collective-permute-start.61) | collective-permute-done | bytes 262176 | tf_op jit(solution)/shard_map/ppermute | solution.py:319
  368.5 4.8 %all-to-all-start.4 = ((bf16[8,99,128]{2,1,0:T(8,128)(2,1)}), bf16[8,99,128]{2,1,0:T(8,128)(2,1)S(1)}, u32[]{:S(2)}, u32[]{:S(2)}) async-start(bf16[8,99,128]{2,1,0:T(8,128)(2,1)} %fusion.43), calls=%async_computation.4 | async-start | bytes 425984 | tf_op jit(solution)/shard_map/all_to_all | solution.py:634
  384.2 5.1 %all-to-all-start.3 = ((bf16[8,128,384]{1,2,0:T(8,128)(2,1)}), bf16[8,128,384]{1,2,0:T(8,128)(2,1)S(1)}, u32[]{:S(2)}, u32[]{:S(2)}) async-start(bf16[8,128,384]{1,2,0:T(8,128)(2,1)} %copy.57), calls=%async_computation.3 | async-start | bytes 1572864 | tf_op jit(solution)/shard_map/all_to_all | solution.py:574
  390.9 4.2 collective-permute-start.64
  397.9 9.3 %collective-permute-start.70 = (bf16[2,128,1024]{2,1,0:T(8,128)(2,1)S(1)}, bf16[2,128,1024]{2,1,0:T(8,128)(2,1)S(1)}, u32[]{:S(2)}, u32[]{:S(2)}) collective-permute-start(bf16[2,128,1024]{2,1,0:T(8,128)(2,1)S(1)} %get-tuple-element.58), channel_id=1, source_target_pairs={{0,1},{1,0},{2,3},{3,2},{4,5},{5,4},{6,7},{7,6},{8,9},{9,8},{10,11... | collective-permute-start | bytes 1572872 | tf_op jit(solution)/shard_map/ppermute | solution.py:330
  408.0 7.4 %collective-permute-done.70 = bf16[2,128,1024]{2,1,0:T(8,128)(2,1)S(1)} collective-permute-done((bf16[2,128,1024]{2,1,0:T(8,128)(2,1)S(1)}, bf16[2,128,1024]{2,1,0:T(8,128)(2,1)S(1)}, u32[]{:S(2)}, u32[]{:S(2)}) %collective-permute-start.70) | collective-permute-done | bytes 524320 | tf_op jit(solution)/shard_map/ppermute | solution.py:330
  416.9 7.5 %collective-permute-start.73 = (bf16[2,128,1024]{2,1,0:T(8,128)(2,1)S(1)}, bf16[2,128,1024]{2,1,0:T(8,128)(2,1)S(1)}, u32[]{:S(2)}, u32[]{:S(2)}) collective-permute-start(bf16[2,128,1024]{2,1,0:T(8,128)(2,1)S(1)} %fusion.24), channel_id=1, source_target_pairs={{0,0},{1,4},{2,8},{3,12},{4,16},{5,20},{6,24},{7,28},{8,1},{9,5},{... | collective-permute-start | bytes 1572872 | tf_op jit(solution)/shard_map/ppermute | solution.py:594
  426.5 5.8 %convolution_add_fusion.1 = f32[128,1024]{1,0:T(8,128)} fusion(f32[128,1024]{1,0:T(8,128)S(1)} %get-tuple-element.32, bf16[128,3072]{0,1:T(8,128)(2,1)S(1)} %bitcast.282, bf16[1024,3072]{1,0:T(8,128)(2,1)} %bitcast.88), kind=kOutput, calls=%fused_computation.26 | convolution fusion | flops 805437440 | bytes 8126464 | tf_op jit(solution)/shard_map/dot_general | solution.py:482
  432.3 18.3 %collective-permute-done.73 = bf16[2,128,1024]{2,1,0:T(8,128)(2,1)S(1)} collective-permute-done((bf16[2,128,1024]{2,1,0:T(8,128)(2,1)S(1)}, bf16[2,128,1024]{2,1,0:T(8,128)(2,1)S(1)}, u32[]{:S(2)}, u32[]{:S(2)}) %collective-permute-start.73) | collective-permute-done | bytes 524320 | tf_op jit(solution)/shard_map/ppermute | solution.py:594
  (401 shorter events, 216.6 us)
Async XLA Ops:
  0.7 41.1 %collective-permute-start = (bf16[128,1024]{1,0:T(8,128)(2,1)}, bf16[128,1024]{1,0:T(8,128)(2,1)}, u32[]{:S(2)}, u32[]{:S(2)}) collective-permute-start(bf16[128,1024]{1,0:T(8,128)(2,1)} %param.8), channel_id=1, source_target_pairs={{0,1},{1,0},{2,3},{3,2},{4,5},{5,4},{6,7},{7,6},{8,9},{9,8},{10,11... | collective-permute-start | bytes 786440 | tf_op jit(solution)/shard_map/ppermute | solution.py:296
  2.3 68.3 %collective-permute-start.2 = (bf16[128,1024]{1,0:T(8,128)(2,1)}, bf16[128,1024]{1,0:T(8,128)(2,1)S(1)}, u32[]{:S(2)}, u32[]{:S(2)}) collective-permute-start(bf16[128,1024]{1,0:T(8,128)(2,1)} %param.8), channel_id=1, source_target_pairs={{1,2},{2,1},{5,6},{6,5},{9,10},{10,9},{13,14},{14,13},{17,18},{18,... | collective-permute-start | bytes 786440 | tf_op jit(solution)/shard_map/ppermute | solution.py:297
  3.0 111.3 %collective-permute-start.5 = (bf16[128,1024]{1,0:T(8,128)(2,1)}, bf16[128,1024]{1,0:T(8,128)(2,1)}, u32[]{:S(2)}, u32[]{:S(2)}) collective-permute-start(bf16[128,1024]{1,0:T(8,128)(2,1)} %param.8), channel_id=1, source_target_pairs={{0,4},{4,0},{1,5},{5,1},{2,6},{6,2},{3,7},{7,3},{8,12},{12,8},{9,1... | collective-permute-start | bytes 786440 | tf_op jit(solution)/shard_map/ppermute | solution.py:307
  5.3 22.6 %collective-permute-start.12 = (bf16[64,1024]{1,0:T(8,128)(2,1)}, bf16[64,1024]{1,0:T(8,128)(2,1)S(1)}, u32[]{:S(2)}, u32[]{:S(2)}) collective-permute-start(bf16[64,1024]{1,0:T(8,128)(2,1)} %get-tuple-element.49), channel_id=1, source_target_pairs={{0,1},{1,0},{2,3},{3,2},{4,5},{5,4},{6,7},{7,6},{8,9},{9,8},{10,11... | collective-permute-start | bytes 393224 | tf_op jit(solution)/shard_map/ppermute | solution.py:296
  9.6 19.8 %collective-permute-start.14 = (bf16[64,1024]{1,0:T(8,128)(2,1)}, bf16[64,1024]{1,0:T(8,128)(2,1)S(1)}, u32[]{:S(2)}, u32[]{:S(2)}) collective-permute-start(bf16[64,1024]{1,0:T(8,128)(2,1)} %get-tuple-element.49), channel_id=1, source_target_pairs={{1,2},{2,1},{5,6},{6,5},{9,10},{10,9},{13,14},{14,13},{17,18},{18,... | collective-permute-start | bytes 393224 | tf_op jit(solution)/shard_map/ppermute | solution.py:297
  14.1 30.6 %all-to-all-start = ((bf16[8,108,128]{2,1,0:T(8,128)(2,1)}), bf16[8,108,128]{2,1,0:T(8,128)(2,1)S(1)}, u32[]{:S(2)}, u32[]{:S(2)}) async-start(bf16[8,108,128]{2,1,0:T(8,128)(2,1)} %copy.52), calls=%async_computation | async-start | bytes 458752 | tf_op jit(solution)/shard_map/all_to_all | solution.py:507
  50.7 28.9 %collective-permute-start.25 = (bf16[2,128,1024]{2,1,0:T(8,128)(2,1)}, bf16[2,128,1024]{2,1,0:T(8,128)(2,1)}, u32[]{:S(2)}, u32[]{:S(2)}) collective-permute-start(bf16[2,128,1024]{2,1,0:T(8,128)(2,1)} %pad_maximum_fusion.4), channel_id=1, source_target_pairs={{0,1},{1,0},{2,3},{3,2},{4,5},{5,4},{6,7},{7,6},{8,9},{9,8},{10,11... | collective-permute-start | bytes 1572872 | tf_op jit(solution)/shard_map/ppermute | solution.py:296
  63.0 65.4 %collective-permute-start.27 = (bf16[2,128,1024]{2,1,0:T(8,128)(2,1)}, bf16[2,128,1024]{2,1,0:T(8,128)(2,1)}, u32[]{:S(2)}, u32[]{:S(2)}) collective-permute-start(bf16[2,128,1024]{2,1,0:T(8,128)(2,1)} %pad_maximum_fusion.4), channel_id=1, source_target_pairs={{1,2},{2,1},{5,6},{6,5},{9,10},{10,9},{13,14},{14,13},{17,18},{18,... | collective-permute-start | bytes 1572872 | tf_op jit(solution)/shard_map/ppermute | solution.py:297
  79.6 94.7 %collective-permute-start.30 = (bf16[2,128,1024]{2,1,0:T(8,128)(2,1)}, bf16[2,128,1024]{2,1,0:T(8,128)(2,1)}, u32[]{:S(2)}, u32[]{:S(2)}) collective-permute-start(bf16[2,128,1024]{2,1,0:T(8,128)(2,1)} %pad_maximum_fusion.4), channel_id=1, source_target_pairs={{0,4},{4,0},{1,5},{5,1},{2,6},{6,2},{3,7},{7,3},{8,12},{12,8},{9,1... | collective-permute-start | bytes 1572872 | tf_op jit(solution)/shard_map/ppermute | solution.py:307
  82.0 21.5 %collective-permute-start.46 = (bf16[32,3072]{1,0:T(8,128)(2,1)S(1)}, bf16[32,3072]{1,0:T(8,128)(2,1)S(1)}, u32[]{:S(2)}, u32[]{:S(2)}) collective-permute-start(bf16[32,3072]{1,0:T(8,128)(2,1)S(1)} %get-tuple-element.40), channel_id=1, source_target_pairs={{0,4},{4,0},{1,5},{5,1},{2,6},{6,2},{3,7},{7,3},{8,12},{12,8},{9,1... | collective-permute-start | bytes 589832 | tf_op jit(solution)/shard_map/ppermute | solution.py:307
  111.9 91.7 %collective-permute-start.48 = (bf16[32,3072]{1,0:T(8,128)(2,1)}, bf16[32,3072]{1,0:T(8,128)(2,1)}, u32[]{:S(2)}, u32[]{:S(2)}) collective-permute-start(bf16[32,3072]{1,0:T(8,128)(2,1)} %get-tuple-element.38), channel_id=1, source_target_pairs={{0,4},{4,0},{1,5},{5,1},{2,6},{6,2},{3,7},{7,3},{8,12},{12,8},{9,1... | collective-permute-start | bytes 589832 | tf_op jit(solution)/shard_map/ppermute | solution.py:307
  127.6 28.6 %collective-permute-start.21 = (bf16[8,64,1024]{2,1,0:T(8,128)(2,1)S(1)}, bf16[8,64,1024]{2,1,0:T(8,128)(2,1)}, u32[]{:S(2)}, u32[]{:S(2)}) collective-permute-start(bf16[8,64,1024]{2,1,0:T(8,128)(2,1)S(1)} %bitcast_dynamic-update-slice_fusion.34), channel_id=1, source_target_pairs={{0,8},{8,0},{16,24},{24,16},{1,9},{9,1},{17,25},{25,17},{2,10},{10... | collective-permute-start | bytes 3145736 | tf_op jit(solution)/shard_map/ppermute | solution.py:522
  128.4 23.5 %collective-permute-start.26 = (bf16[2,128,1024]{2,1,0:T(8,128)(2,1)}, bf16[2,128,1024]{2,1,0:T(8,128)(2,1)}, u32[]{:S(2)}, u32[]{:S(2)}) collective-permute-start(bf16[2,128,1024]{2,1,0:T(8,128)(2,1)} %collective-permute-done.25), channel_id=1, source_target_pairs={{1,2},{2,1},{5,6},{6,5},{9,10},{10,9},{13,14},{14,13},{17,18},{18,... | collective-permute-start | bytes 1572872 | tf_op jit(solution)/shard_map/ppermute | solution.py:298
  151.9 26.1 %collective-permute-start.31 = (bf16[2,128,1024]{2,1,0:T(8,128)(2,1)}, bf16[2,128,1024]{2,1,0:T(8,128)(2,1)}, u32[]{:S(2)}, u32[]{:S(2)}) collective-permute-start(bf16[2,128,1024]{2,1,0:T(8,128)(2,1)} %collective-permute-done.25), channel_id=1, source_target_pairs={{0,4},{4,0},{1,5},{5,1},{2,6},{6,2},{3,7},{7,3},{8,12},{12,8},{9,1... | collective-permute-start | bytes 1572872 | tf_op jit(solution)/shard_map/ppermute | solution.py:307
  151.9 54.3 %collective-permute-start.49 = (bf16[32,3072]{1,0:T(8,128)(2,1)}, bf16[32,3072]{1,0:T(8,128)(2,1)}, u32[]{:S(2)}, u32[]{:S(2)}) collective-permute-start(bf16[32,3072]{1,0:T(8,128)(2,1)} %get-tuple-element.36), channel_id=1, source_target_pairs={{0,4},{4,0},{1,5},{5,1},{2,6},{6,2},{3,7},{7,3},{8,12},{12,8},{9,1... | collective-permute-start | bytes 589832 | tf_op jit(solution)/shard_map/ppermute | solution.py:307
  174.3 20.3 %collective-permute-start.33 = (bf16[2,128,1024]{2,1,0:T(8,128)(2,1)S(1)}, bf16[2,128,1024]{2,1,0:T(8,128)(2,1)S(1)}, u32[]{:S(2)}, u32[]{:S(2)}) collective-permute-start(bf16[2,128,1024]{2,1,0:T(8,128)(2,1)S(1)} %get-tuple-element.55), channel_id=1, source_target_pairs={{0,4},{4,0},{1,5},{5,1},{2,6},{6,2},{3,7},{7,3},{8,12},{12,8},{9,1... | collective-permute-start | bytes 1572872 | tf_op jit(solution)/shard_map/ppermute | solution.py:307
  207.9 22.6 %collective-permute-start.50 = (bf16[8,32,3072]{2,1,0:T(8,128)(2,1)}, bf16[8,32,3072]{2,1,0:T(8,128)(2,1)}, u32[]{:S(2)}, u32[]{:S(2)}) collective-permute-start(bf16[8,32,3072]{2,1,0:T(8,128)(2,1)} %bitcast_dynamic-update-slice_fusion.22), channel_id=1, source_target_pairs={{0,8},{8,0},{16,24},{24,16},{1,9},{9,1},{17,25},{25,17},{2,10},{10... | collective-permute-start | bytes 4718600 | tf_op jit(solution)/shard_map/ppermute | solution.py:335
  207.9 57.6 %collective-permute-start.51 = (bf16[8,32,3072]{2,1,0:T(8,128)(2,1)}, bf16[8,32,3072]{2,1,0:T(8,128)(2,1)}, u32[]{:S(2)}, u32[]{:S(2)}) collective-permute-start(bf16[8,32,3072]{2,1,0:T(8,128)(2,1)} %bitcast_dynamic-update-slice_fusion.22), channel_id=1, source_target_pairs={{0,16},{8,24},{16,0},{24,8},{1,17},{9,25},{17,1},{25,9},{2,18},{10... | collective-permute-start | bytes 4718600 | tf_op jit(solution)/shard_map/ppermute | solution.py:334
  217.7 36.5 %collective-permute-start.37 = (bf16[128,1024]{1,0:T(8,128)(2,1)}, bf16[128,1024]{1,0:T(8,128)(2,1)}, u32[]{:S(2)}, u32[]{:S(2)}) collective-permute-start(bf16[128,1024]{1,0:T(8,128)(2,1)} %get-tuple-element.29), channel_id=1, source_target_pairs={{0,16},{8,24},{16,0},{24,8},{1,17},{9,25},{17,1},{25,9},{2,18},{10... | collective-permute-start | bytes 786440 | tf_op jit(solution)/shard_map/ppermute | solution.py:334
  226.6 91.9 %collective-permute-start.57 = (bf16[128,256]{1,0:T(8,128)(2,1)}, bf16[128,256]{1,0:T(8,128)(2,1)}, u32[]{:S(2)}, u32[]{:S(2)}) collective-permute-start(bf16[128,256]{1,0:T(8,128)(2,1)} %bitcast.103), channel_id=1, source_target_pairs={{0,24},{8,16},{16,8},{24,0},{1,25},{9,17},{17,9},{25,1},{2,26},{10... | collective-permute-start | bytes 196616 | tf_op jit(solution)/shard_map/ppermute | solution.py:602
  228.1 92.6 %collective-permute-start.56 = (bf16[128,256]{1,0:T(8,128)(2,1)}, bf16[128,256]{1,0:T(8,128)(2,1)}, u32[]{:S(2)}, u32[]{:S(2)}) collective-permute-start(bf16[128,256]{1,0:T(8,128)(2,1)} %bitcast.102), channel_id=1, source_target_pairs={{0,16},{8,24},{16,0},{24,8},{1,17},{9,25},{17,1},{25,9},{2,18},{10... | collective-permute-start | bytes 196616 | tf_op jit(solution)/shard_map/ppermute | solution.py:601
  230.5 26.5 %collective-permute-start.36 = (bf16[128,1024]{1,0:T(8,128)(2,1)}, bf16[128,1024]{1,0:T(8,128)(2,1)S(1)}, u32[]{:S(2)}, u32[]{:S(2)}) collective-permute-start(bf16[128,1024]{1,0:T(8,128)(2,1)} %get-tuple-element.29), channel_id=1, source_target_pairs={{0,8},{8,0},{16,24},{24,16},{1,9},{9,1},{17,25},{25,17},{2,10},{10... | collective-permute-start | bytes 786440 | tf_op jit(solution)/shard_map/ppermute | solution.py:335
  296.7 57.9 %collective-permute-start.67 = (bf16[4,2,128,1024]{3,2,0,1:T(8,128)(2,1)}, bf16[4,2,128,1024]{3,2,0,1:T(8,128)(2,1)}, u32[]{:S(2)}, u32[]{:S(2)}) collective-permute-start(bf16[4,2,128,1024]{3,2,0,1:T(8,128)(2,1)} %fusion.1), channel_id=1, source_target_pairs={{0,4},{4,0},{1,5},{5,1},{2,6},{6,2},{3,7},{7,3},{8,12},{12,8},{9,1... | collective-permute-start | bytes 6291464 | tf_op jit(solution)/shard_map/ppermute | solution.py:319
  297.6 23.2 %collective-permute-start.58 = (bf16[128,1024]{1,0:T(8,128)(2,1)S(1)}, bf16[128,1024]{1,0:T(8,128)(2,1)}, u32[]{:S(2)}, u32[]{:S(2)}) collective-permute-start(bf16[128,1024]{1,0:T(8,128)(2,1)S(1)} %get-tuple-element.31), channel_id=1, source_target_pairs={{0,8},{8,0},{16,24},{24,16},{1,9},{9,1},{17,25},{25,17},{2,10},{10... | collective-permute-start | bytes 786440 | tf_op jit(solution)/shard_map/ppermute | solution.py:335
  320.7 59.7 %collective-permute-start.52 = (bf16[8,32,3072]{2,1,0:T(8,128)(2,1)}, bf16[8,32,3072]{2,1,0:T(8,128)(2,1)}, u32[]{:S(2)}, u32[]{:S(2)}) collective-permute-start(bf16[8,32,3072]{2,1,0:T(8,128)(2,1)} %collective-permute-done.51), channel_id=1, source_target_pairs={{0,8},{8,0},{16,24},{24,16},{1,9},{9,1},{17,25},{25,17},{2,10},{10... | collective-permute-start | bytes 4718600 | tf_op jit(solution)/shard_map/ppermute | solution.py:335
  322.7 27.0 %collective-permute-start.61 = (bf16[4,32,1024]{2,1,0:T(8,128)(2,1)S(1)}, bf16[4,32,1024]{2,1,0:T(8,128)(2,1)S(1)}, u32[]{:S(2)}, u32[]{:S(2)}) collective-permute-start(bf16[4,32,1024]{2,1,0:T(8,128)(2,1)S(1)} %dynamic-slice_convert_fusion), channel_id=1, source_target_pairs={{0,4},{4,0},{1,5},{5,1},{2,6},{6,2},{3,7},{7,3},{8,12},{12,8},{9,1... | collective-permute-start | bytes 786440 | tf_op jit(solution)/shard_map/ppermute | solution.py:319
  324.4 37.3 %collective-permute-start.53 = (bf16[2,8,99,128]{3,2,1,0:T(8,128)(2,1)S(1)}, bf16[2,8,99,128]{3,2,1,0:T(8,128)(2,1)S(1)}, u32[]{:S(2)}, u32[]{:S(2)}) collective-permute-start(bf16[2,8,99,128]{3,2,1,0:T(8,128)(2,1)S(1)} %pad_maximum_fusion.7), channel_id=1, source_target_pairs={{0,8},{8,0},{16,24},{24,16},{1,9},{9,1},{17,25},{25,17},{2,10},{10... | collective-permute-start | bytes 1216520 | tf_op jit(solution)/shard_map/ppermute | solution.py:340
  352.7 36.6 %collective-permute-start.65 = (bf16[32,1024]{1,0:T(8,128)(2,1)S(1)}, bf16[32,1024]{1,0:T(8,128)(2,1)}, u32[]{:S(2)}, u32[]{:S(2)}) collective-permute-start(bf16[32,1024]{1,0:T(8,128)(2,1)S(1)} %get-tuple-element.78), channel_id=1, source_target_pairs={{0,1},{3,2},{4,5},{7,6},{8,9},{11,10},{12,13},{15,14},{16,17},{19,... | collective-permute-start | bytes 196616 | tf_op jit(solution)/shard_map/ppermute | solution.py:324
  362.4 26.9 %collective-permute-start.63 = (bf16[32,1024]{1,0:T(8,128)(2,1)S(1)}, bf16[32,1024]{1,0:T(8,128)(2,1)}, u32[]{:S(2)}, u32[]{:S(2)}) collective-permute-start(bf16[32,1024]{1,0:T(8,128)(2,1)S(1)} %fusion.56), channel_id=1, source_target_pairs={{1,2},{2,1},{5,6},{6,5},{9,10},{10,9},{13,14},{14,13},{17,18},{18,... | collective-permute-start | bytes 196616 | tf_op jit(solution)/shard_map/ppermute | solution.py:327
  373.3 21.8 %collective-permute-start.71 = (bf16[2,128,1024]{2,1,0:T(8,128)(2,1)}, bf16[2,128,1024]{2,1,0:T(8,128)(2,1)S(1)}, u32[]{:S(2)}, u32[]{:S(2)}) collective-permute-start(bf16[2,128,1024]{2,1,0:T(8,128)(2,1)} %get-tuple-element.61), channel_id=1, source_target_pairs={{0,1},{3,2},{4,5},{7,6},{8,9},{11,10},{12,13},{15,14},{16,17},{19,... | collective-permute-start | bytes 1572872 | tf_op jit(solution)/shard_map/ppermute | solution.py:324
  384.2 42.2 %all-to-all-start.3 = ((bf16[8,128,384]{1,2,0:T(8,128)(2,1)}), bf16[8,128,384]{1,2,0:T(8,128)(2,1)S(1)}, u32[]{:S(2)}, u32[]{:S(2)}) async-start(bf16[8,128,384]{1,2,0:T(8,128)(2,1)} %copy.57), calls=%async_computation.3 | async-start | bytes 1572864 | tf_op jit(solution)/shard_map/all_to_all | solution.py:574
  416.9 33.7 %collective-permute-start.73 = (bf16[2,128,1024]{2,1,0:T(8,128)(2,1)S(1)}, bf16[2,128,1024]{2,1,0:T(8,128)(2,1)S(1)}, u32[]{:S(2)}, u32[]{:S(2)}) collective-permute-start(bf16[2,128,1024]{2,1,0:T(8,128)(2,1)S(1)} %fusion.24), channel_id=1, source_target_pairs={{0,0},{1,4},{2,8},{3,12},{4,16},{5,20},{6,24},{7,28},{8,1},{9,5},{... | collective-permute-start | bytes 1572872 | tf_op jit(solution)/shard_map/ppermute | solution.py:594
  (103 other events, 1027.5 us)

commit v2 on v0

--- a/solution.py
+++ b/solution.py
@@ -3,6 +3,8 @@
 import jax
 import jax.numpy as jnp
 from jax import lax
+from jax.experimental import pallas as pl
+from jax.experimental.pallas import tpu as pltpu
 from jax.sharding import PartitionSpec as P
 
 HEAD_DIM = 64
@@ -49,7 +51,7 @@
     )
 
 
-def body(tokens, out_grad, w_qkv, w_out, fc_in, fc_out, fc_in_bias, vectors):
+def general_body(tokens, out_grad, w_qkv, w_out, fc_in, fc_out, fc_in_bias, vectors):
     model_width = tokens.shape[1]
     hidden_units = fc_in.shape[0] * lax.axis_size(("head", "blk"))
     ratio = hidden_units // model_width
@@ -271,9 +273,788 @@
     )
 
 
+GROUP = ("head", "blk")
+FLIP = ((0, 1), (1, 0))
+PAIRS = ((0, 1), (1, 0), (2, 3), (3, 2))
+INNER = ((1, 2), (2, 1))
+OUTER = ((1, 0), (2, 3))
+INWARD = ((0, 1), (3, 2))
+TWO_ON = ((0, 2), (2, 0), (1, 3), (3, 1))
+CORE = tuple((at, at ^ 1) for at in range(4))
+ACROSS = tuple((at, at ^ 2) for at in range(4))
+LOW = jnp.bfloat16
+FULL = jnp.float32
+ROWS_DIMS = (((1,), (1,)), ((), ()))
+COLS_DIMS = (((0,), (0,)), ((), ()))
+
+
+def dot(left, right):
+    return jnp.dot(left, right, preferred_element_type=FULL)
+
+
+def dot_rows(left, right):
+    return lax.dot_general(left, right, ROWS_DIMS, preferred_element_type=FULL)
+
+
+def dot_cols(left, right):
+    return lax.dot_general(left, right, COLS_DIMS, preferred_element_type=FULL)
+
+
+def after(values, *others):
+    if not isinstance(values, (list, tuple)):
+        return lax.optimization_barrier((values,) + others)[0]
+    return lax.optimization_barrier(tuple(values) + others)[: len(values)]
+
+
+def inner_blk():
+    at = lax.axis_index("blk")
+    return (at == 1) | (at == 2)
+
+
+def flip_head(value):
+    return lax.ppermute(value, "head", FLIP)
+
+
+def scatter_group(near, away):
+    across_3 = flip_head(away[3])
+    third = near[3] + across_3.astype(FULL)
+    away_2 = after(away[2], across_3)
+    ends_third = lax.ppermute(third.astype(LOW), "blk", INWARD)
+    across_2 = flip_head(away_2)
+    second = near[2] + across_2.astype(FULL) + ends_third.astype(FULL)
+    second_low, away_1 = after((second.astype(LOW), away[1]), across_2)
+    ends_second = lax.ppermute(second_low, "blk", INWARD)
+    inner_second = lax.ppermute(second_low, "blk", INNER)
+    across_1 = flip_head(away_1)
+    third = third + ends_second.astype(FULL)
+    first = near[1] + across_1.astype(FULL) + inner_second.astype(FULL)
+    third_low, first_low, away_0 = after((third.astype(LOW), first.astype(LOW), away[0]))
+    inner_third = lax.ppermute(third_low, "blk", INNER)
+    last = lax.ppermute(first_low, "blk", PAIRS)
+    across_0 = flip_head(away_0)
+    return [near[0], across_0, inner_third, last]
+
+
+def gather_seq(own):
+    across = lax.ppermute(own, "seq", ACROSS)
+    return [own, lax.ppermute(own, "seq", CORE), across, lax.ppermute(across, "seq", CORE)]
+
+
+def gather_four(own):
+    across = flip_head(own)
+    beside = lax.ppermute(own, "blk", PAIRS)
+    return [own, beside, across, lax.ppermute(across, "blk", PAIRS)]
+
+
+def gather_cores(own):
+    across = flip_head(own)
+    return [own, lax.ppermute(own, "seq", CORE), across, lax.ppermute(across, "seq", CORE)]
+
+
+def shape_of(shape, dtype):
+    return jax.ShapeDtypeStruct(shape, dtype)
+
+
+def call(kernel, outs, place, *args, scratch=(), flops=0, vmem=28, far_in=0, far_out=0):
+    moved = sum(arg.size * arg.dtype.itemsize for arg in args)
+    moved += sum(math.prod(out.shape) * jnp.dtype(out.dtype).itemsize for out in outs)
+    near = pl.BlockSpec(memory_space=pltpu.VMEM)
+    far = pl.BlockSpec(memory_space=pltpu.HBM)
+    return pl.pallas_call(
+        kernel,
+        out_shape=outs,
+        in_specs=[pl.BlockSpec(memory_space=pltpu.SMEM)]
+        + [near] * (len(args) - far_in)
+        + [far] * far_in,
+        out_specs=[near] * (len(outs) - far_out) + [far] * far_out,
+        scratch_shapes=scratch,
+        compiler_params=pltpu.CompilerParams(vmem_limit_bytes=vmem * 2**20),
+        cost_estimate=pl.CostEstimate(flops=flops, bytes_accessed=moved, transcendentals=0),
+    )(place, *args)
+
+
+def fetch(sources, held, sems):
+    copies = [pltpu.make_async_copy(*both, sems.at[at]) for at, both in enumerate(zip(sources, held))]
+    for copy in copies:
+        copy.start()
+    return copies
+
+
+def put_columns(core, own_half, other_half, cols_ref):
+    half, own = own_half.shape[2:]
+    for at in range(8):
+        for side, half_ref in ((core, own_half), (1 - core, other_half)):
+            span = pl.ds(pl.multiple_of((2 * at + side) * half, half), half)
+            for which in range(3):
+                cols_ref[span, which * own : (which + 1) * own] = half_ref[at, which]
+
+
+def attend_kernel(place, *refs):
+    slots, refs = refs[:8], refs[8:]
+    own_half, other_half, bias_ref = refs[:3]
+    context_ref, kept, refs = refs[3], refs[4:10], refs[10:]
+    q_ref, k_ref, v_ref, mixed_ref, inverse_ref, weights_ref, cols_ref, sems = refs
+    rank, core = place[0], place[2]
+    half = own_half.shape[2]
+    width = q_ref.shape[1]
+    rows = slots[0].shape[0]
+    put_columns(core, own_half, other_half, cols_ref)
+    scale = HEAD_DIM ** (-0.5)
+    for pair in range(4):
+        span = slice(pair * 2 * rows, (pair + 1) * 2 * rows)
+        both = jnp.concatenate([slots[2 * pair][...], slots[2 * pair + 1][...]], axis=0)
+        projected = dot(both, cols_ref[...])
+        q_ref[span] = ((projected[:, :width] + bias_ref[0]) * scale).astype(LOW)
+        k_ref[span] = projected[:, width : 2 * width].astype(LOW)
+        v_ref[span] = (projected[:, 2 * width :] + bias_ref[1]).astype(LOW)
+
+    @pl.loop(0, 4)
+    def _(pair):
+        span = pl.ds(pl.multiple_of(pair * 2 * rows, 2 * rows), 2 * rows)
+        for at in range(width // HEAD_DIM):
+            cols = slice(at * HEAD_DIM, (at + 1) * HEAD_DIM)
+            scores = dot_rows(q_ref[span, cols], k_ref[:, cols])
+            weights = jnp.exp(scores - jnp.max(scores, axis=-1, keepdims=True))
+            inverse = 1.0 / jnp.sum(weights, axis=-1, keepdims=True)
+            weights = weights.astype(LOW)
+            weights_ref[at, span] = weights
+            mixed_ref[span, cols] = dot(weights, v_ref[:, cols]) * inverse
+            inverse_ref[span, cols] = jnp.broadcast_to(inverse, (2 * rows, HEAD_DIM))
+        first = lax.bitwise_xor(rank, 2 * pair)
+        mixed = mixed_ref[span].astype(LOW)
+        context_ref[first] = mixed[:rows]
+        context_ref[lax.bitwise_xor(first, 1)] = mixed[rows:]
+        pltpu.make_async_copy(
+            weights_ref.at[:, span], kept[5].at[:, span], sems.at[pair]
+        ).start()
+
+    copies = []
+    for at, ref in enumerate((q_ref, k_ref, v_ref, mixed_ref, inverse_ref)):
+        copies.append(pltpu.make_async_copy(ref, kept[at], sems.at[4 + at]))
+    for pair in range(4):
+        span = slice(pair * 2 * rows, (pair + 1) * 2 * rows)
+        copies.append(
+            pltpu.make_async_copy(weights_ref.at[:, span], kept[5].at[:, span], sems.at[pair])
+        )
+    for copy in copies[:5]:
+        copy.start()
+    for copy in copies:
+        copy.wait()
+
+
+def attend_back_kernel(place, grad_ref, own_half, other_half, *refs):
+    kept, refs = refs[:6], refs[6:]
+    out_ref, near_ref, away_ref, cols_ref, refs = refs[0], refs[1], refs[2], refs[3], refs[4:]
+    q_ref, k_ref, v_ref, mixed_ref, inverse_ref, weights_ref, dk_sum, dv_sum, sems = refs
+    rank = place[0]
+    rows, width = grad_ref.shape[1:]
+    scale = HEAD_DIM ** (-0.5)
+    copies = []
+    for at, ref in enumerate((q_ref, k_ref, v_ref, mixed_ref, inverse_ref)):
+        copies.append(pltpu.make_async_copy(kept[at], ref, sems.at[4 + at]))
+
+    def block_copy(pair, span):
+        return pltpu.make_async_copy(kept[5].at[:, span], weights_ref.at[:, span], sems.at[pair])
+
+    for copy in copies:
+        copy.start()
+    for pair in range(4):
+        block_copy(pair, slice(pair * 2 * rows, (pair + 1) * 2 * rows)).start()
+    dk_sum[...] = jnp.zeros_like(dk_sum)
+    dv_sum[...] = jnp.zeros_like(dv_sum)
+    for copy in copies:
+        copy.wait()
+
+    @pl.loop(0, 4)
+    def _(pair):
+        span = pl.ds(pl.multiple_of(pair * 2 * rows, 2 * rows), 2 * rows)
+        block_copy(pair, span).wait()
+        first = lax.bitwise_xor(rank, 2 * pair)
+        second = lax.bitwise_xor(first, 1)
+        grad_all = jnp.concatenate([grad_ref[first], grad_ref[second]], axis=0)
+        inverse = inverse_ref[span]
+        q_scaled = (q_ref[span].astype(FULL) * inverse).astype(LOW)
+        g_scaled = (grad_all.astype(FULL) * inverse).astype(LOW)
+        product = grad_all.astype(FULL) * mixed_ref[span]
+        for at in range(width // HEAD_DIM):
+            cols = slice(at * HEAD_DIM, (at + 1) * HEAD_DIM)
+            delta = jnp.sum(product[:, cols], axis=-1, keepdims=True)
+            weights = weights_ref[at, span]
+            dprobs = dot_rows(grad_all[:, cols], v_ref[:, cols])
+            dscores = (weights.astype(FULL) * (dprobs - delta)).astype(LOW)
+            dq = (dot(dscores, k_ref[:, cols]) * inverse[:, cols]).astype(LOW) * LOW(scale)
+            out_ref[first, :, cols] = dq[:rows]
+            out_ref[second, :, cols] = dq[rows:]
+            dk_sum[cols] += dot_cols(q_scaled[:, cols], dscores)
+            dv_sum[cols] += dot_cols(g_scaled[:, cols], weights)
+
+    dk = dk_sum[...].T.astype(LOW)
+    dv = dv_sum[...].T.astype(LOW)
+    for at in range(8):
+        whose = lax.bitwise_xor(rank, at)
+        out_ref[whose, :, width : 2 * width] = dk[at * rows : (at + 1) * rows]
+        out_ref[whose, :, 2 * width :] = dv[at * rows : (at + 1) * rows]
+    put_columns(place[2], own_half, other_half, cols_ref)
+    for pair in (2, 3, 0, 1):
+        left = [out_ref[lax.bitwise_xor(rank, 2 * pair + at)] for at in range(2)]
+        term = dot_rows(jnp.concatenate(left, axis=0), cols_ref[...])
+        for at in range(2):
+            if pair < 2:
+                near_ref[2 * pair + at] = term[at * rows : (at + 1) * rows]
+            else:
+                away_ref[2 * pair + at - 4] = term[at * rows : (at + 1) * rows].astype(LOW)
+
+
+def normalize(values):
+    center = values - jnp.mean(values, axis=-1, keepdims=True)
+    scale = lax.rsqrt(jnp.mean(center * center, axis=-1, keepdims=True) + 1e-05)
+    return center * scale, scale
+
+
+def normalize_back(cotangent, gain, normed, scale):
+    dn = cotangent * gain
+    inner = jnp.mean(dn, axis=-1, keepdims=True)
+    outer = jnp.mean(dn * normed, axis=-1, keepdims=True)
+    return scale * (dn - inner - normed * outer)
+
+
+def quarter_span(place, at, size):
+    return pl.ds(pl.multiple_of(lax.bitwise_xor(place[1], at) * size, size), size)
+
+
+def fetch_out(place, sources, held, sems):
+    own = held.shape[1]
+    copies = []
+    for at, source in enumerate(sources):
+        for part in range(2):
+            start = (2 * lax.bitwise_xor(place[1], at) + part) * own
+            span = pl.ds(pl.multiple_of(start, own), own)
+            copies.append(
+                pltpu.make_async_copy(
+                    source.at[:, part], held.at[:, :, span], sems.at[2 * at + part]
+                )
+            )
+    for copy in copies:
+        copy.start()
+    return copies
+
+
+def mix_kernel(
+    place, context_ref, tokens_ref, vec_ref, *refs
+):
+    sources, refs = refs[:4], refs[4:]
+    middle_ref, low_ref, norm_ref, scale_ref, left_ref, out_ref, sems = refs
+    copies = fetch_out(place, sources, out_ref, sems)
+    own = context_ref.shape[2]
+    for at in range(8):
+        left_ref[:, at * own : (at + 1) * own] = context_ref[at]
+    for copy in copies:
+        copy.wait()
+    attended = dot(left_ref[...], out_ref[...].reshape(8 * own, 8 * own))
+    norm, scale = normalize(tokens_ref[...].astype(FULL) + (attended + vec_ref[6:7]))
+    middle = norm * vec_ref[0:1] + vec_ref[2:3]
+    middle_ref[...] = middle
+    low_ref[...] = middle.astype(LOW)
+    norm_ref[...] = norm
+    scale_ref[...] = scale
+
+
+def fetch_units(place, sources, w_in, w_out, sems, first):
+    ins = [(sources[0], w_in.at[0])]
+    outs = [(sources[1], w_out.at[0])]
+    for at, source in enumerate(sources[2:]):
+        span = quarter_span(place, at, source.shape[1])
+        ins.append((source.at[0], w_in.at[1, span]))
+        outs.append((source.at[1], w_out.at[1, span]))
+    order = ins[:1] + outs[:1] + ins[1:] + outs[1:]
+    if first == 1:
+        order = outs[:1] + ins[:1] + outs[1:] + ins[1:]
+    copies = [pltpu.make_async_copy(*both, sems.at[at]) for at, both in enumerate(order)]
+    for copy in copies:
+        copy.start()
+
+    def wait(part, which):
+        if part % 2 == 0:
+            start = 2 + 4 * which if part else which
+            for copy in copies[start : start + 4] if part else copies[start : start + 1]:
+                copy.wait()
+
+    return wait
+
+
+def ffn_kernel(place, first_ref, second_ref, *refs):
+    bias_ref, sources, refs = refs[0], refs[1:7], refs[7:]
+    pre_ref, act_ref, near_ref, away_ref, sum_ref, w_in, w_out, sems = refs
+    wait = fetch_units(place, sources, w_in, w_out, sems, 0)
+    rows = first_ref.shape[0]
+    step = bias_ref.shape[2]
+    both = jnp.concatenate([first_ref[...], second_ref[...]], axis=0)
+    for part in range(4):
+        span = slice(part * 2 * step, (part + 1) * 2 * step)
+        shard, rows_of = part // 2, slice(part % 2 * 2 * step, (part % 2 + 1) * 2 * step)
+        whose = place[4] * 4 + lax.bitwise_xor(place[5], 2 * shard)
+        bias = [bias_ref[whose * 4 + part % 2 * 2 + at] for at in range(2)]
+        wait(part, 0)
+        pre = dot_rows(both, w_in[shard, rows_of]) + jnp.concatenate(bias, axis=1)
+        pre_ref[:, span] = pre
+        act = (pre * (0.5 * (1.0 + lax.erf(pre * (0.5**0.5))))).astype(LOW)
+        act_ref[:, span] = act
+        wait(part, 1)
+        term = dot(act, w_out[shard, rows_of])
+        if part == 0:
+            sum_ref[...] = term
+        else:
+            sum_ref[...] += term
+    near_ref[...] = sum_ref[:rows]
+    away_ref[...] = sum_ref[rows:].astype(LOW)
+
+
+def ffn_back_kernel(place, first_ref, second_ref, slope_ref, *refs):
+    sources, refs = refs[:6], refs[6:]
+    grad_ref, near_ref, away_ref, units_ref, sum_ref, w_in, w_out, sems = refs
+    wait = fetch_units(place, sources, w_in, w_out, sems, 1)
+    rows = first_ref.shape[0]
+    step = units_ref.shape[2]
+    both = jnp.concatenate([first_ref[...], second_ref[...]], axis=0)
+    for part in range(4):
+        span = slice(part * 2 * step, (part + 1) * 2 * step)
+        shard, rows_of = part // 2, slice(part % 2 * 2 * step, (part % 2 + 1) * 2 * step)
+        wait(part, 0)
+        grad = (dot_rows(both, w_out[shard, rows_of]) * slope_ref[:, span]).astype(LOW)
+        grad_ref[:, span] = grad
+        sums = jnp.sum(grad.astype(FULL), axis=0, keepdims=True)
+        for at in range(2):
+            half = lax.bitwise_xor(place[7], shard)
+            units_ref[half * 4 + part % 2 * 2 + at] = sums[:, at * step : (at + 1) * step]
+        wait(part, 1)
+        term = dot(grad, w_in[shard, rows_of])
+        if part == 0:
+            sum_ref[...] = term
+        else:
+            sum_ref[...] += term
+    near_ref[...] = sum_ref[:rows]
+    away_ref[...] = sum_ref[rows:].astype(LOW)
+
+
+def top_kernel(
+    place, near_ref, sent_ref, far_ref, middle_ref, vec_ref, cotangent_ref,
+    layer_ref, grad_ref, low_ref, sums_ref,
+):
+    summed = near_ref[...] + sent_ref[...].astype(FULL) + far_ref[...].astype(FULL)
+    norm, scale = normalize(middle_ref[...] + summed + vec_ref[7:8])
+    layer_ref[...] = norm * vec_ref[1:2] + vec_ref[3:4]
+    cotangent = cotangent_ref[...].astype(FULL)
+    grad = normalize_back(cotangent, vec_ref[1:2], norm, scale)
+    grad_ref[...] = grad
+    low_ref[...] = grad.astype(LOW)
+    sums_ref[0:1] = jnp.sum(cotangent * norm, axis=0, keepdims=True)
+    sums_ref[1:2] = jnp.sum(cotangent, axis=0, keepdims=True)
+    sums_ref[2:3] = jnp.sum(grad.astype(LOW).astype(FULL), axis=0, keepdims=True)
+
+
+def mix_back_kernel(
+    place, near_ref, sent_ref, far_ref, grad_two_ref, norm_ref, scale_ref, vec_ref, *refs
+):
+    sources, refs = refs[:4], refs[4:]
+    grad_ref, low_ref, context_ref, sums_ref, out_ref, sems = refs
+    copies = fetch_out(place, sources, out_ref, sems)
+    summed = near_ref[...] + sent_ref[...].astype(FULL) + far_ref[...].astype(FULL)
+    grad_mid = grad_two_ref[...] + summed
+    norm = norm_ref[...]
+    grad = normalize_back(grad_mid, vec_ref[0:1], norm, scale_ref[...])
+    grad_ref[...] = grad
+    low_ref[...] = grad.astype(LOW)
+    sums_ref[0:1] = jnp.sum(grad_mid * norm, axis=0, keepdims=True)
+    sums_ref[1:2] = jnp.sum(grad_mid, axis=0, keepdims=True)
+    sums_ref[2:3] = jnp.sum(grad.astype(LOW).astype(FULL), axis=0, keepdims=True)
+    own = context_ref.shape[2]
+    for copy in copies:
+        copy.wait()
+    total = dot_rows(low_ref[...], out_ref[...].reshape(8 * own, 8 * own)).astype(LOW)
+    own = context_ref.shape[2]
+    for at in range(8):
+        context_ref[at] = total[:, at * own : (at + 1) * own]
+
+
+def weight_grad_kernel(place, left_0, left_1, *refs):
+    right, near_ref, away_ref = refs[:4], refs[4], refs[5]
+    rows = near_ref.shape[1]
+    first = jnp.concatenate([right[0][...], right[1][...]], axis=0)
+    second = jnp.concatenate([right[2][...], right[3][...]], axis=0)
+    for stays in range(2):
+        shard = place[6] if stays else 1 - place[6]
+        for half in range(2):
+            span = pl.ds(pl.multiple_of((2 * shard + half) * 2 * rows, 2 * rows), 2 * rows)
+            both = dot_cols(left_0[:, span], first) + dot_cols(left_1[:, span], second)
+            for at in range(2):
+                part = both[at * rows : (at + 1) * rows]
+                slot = 2 * lax.bitwise_xor(place[3], at) + lax.bitwise_xor(place[7], half)
+                if stays:
+                    near_ref[slot] = part
+                else:
+                    away_ref[slot] = part.astype(LOW)
+
+
+def out_grad_kernel(place, *refs):
+    parts, grads, near_ref, away_ref = refs[:4], refs[4:8], refs[8], refs[9]
+    step = near_ref.shape[1]
+    right = jnp.concatenate([grad[...] for grad in grads], axis=0)
+    for stays in range(2):
+        which = place[3] if stays else 1 - place[3]
+        total = dot_cols(jnp.concatenate([part[which] for part in parts], axis=0), right)
+        for at in range(4):
+            if stays:
+                near_ref[at] = total[at * step : (at + 1) * step]
+            else:
+                away_ref[at] = total[at * step : (at + 1) * step].astype(LOW)
+
+
+def qkv_grad_kernel(place, *refs):
+    slots, refs = refs[:8], refs[8:]
+    grad_ref, top_ref, mid_ref, units_a, units_b = refs[:5]
+    near_ref, away_ref, total_ref, sums_ref = refs[5:]
+    rank, seq_at = place[0], place[1]
+    rows = slots[0].shape[0]
+    width = sums_ref.shape[1]
+    own = width // 8
+    quarter = width // 4
+    col_sum = 0.0
+    for pair in range(4):
+        grads = [grad_ref[lax.bitwise_xor(rank, 2 * pair + at)] for at in range(2)]
+        grads = jnp.concatenate(grads, axis=0)
+        both = jnp.concatenate([slots[2 * pair][...], slots[2 * pair + 1][...]], axis=0)
+        term = dot_cols(both, grads)
+        col_sum += jnp.sum(grads.astype(FULL), axis=0, keepdims=True)
+        if pair == 0:
+            total_ref[...] = term
+        else:
+            total_ref[...] += term
+    sums_ref[...] = jnp.zeros_like(sums_ref)
+    sums_ref[0:1] = mid_ref[0:1]
+    sums_ref[1:2] = top_ref[0:1]
+    sums_ref[2:3] = mid_ref[1:2]
+    sums_ref[3:4] = top_ref[1:2]
+    own_cols = pl.ds(pl.multiple_of(rank * own, own), own)
+    sums_ref[4:5, own_cols] = col_sum[:, :own]
+    sums_ref[5:6, own_cols] = col_sum[:, 2 * own :]
+    sums_ref[6:7] = mid_ref[2:3]
+    sums_ref[7:8] = top_ref[2:3]
+    row_at = lax.broadcasted_iota(jnp.int32, (8, own), 0)
+    for at in (1, 3, 0, 2):
+        whose = lax.bitwise_xor(seq_at, at)
+        part = total_ref[quarter_span(place, at, quarter)]
+        sums = sums_ref[:, quarter_span(place, at, quarter)]
+        here = lax.shift_right_logical(whose, 1) == place[4]
+        first = 4 * lax.bitwise_and(whose, 1)
+        units = [units_a[first + row] + units_b[first + row] for row in range(4)]
+        mine = (row_at >= 4 * place[8]) & (row_at < 4 * place[8] + 4)
+        units = jnp.where(mine & here, jnp.concatenate(units + units, axis=0), 0.0)
+        sums = jnp.concatenate([sums, units], axis=1)
+        sums = jnp.concatenate([sums, jnp.zeros_like(sums)], axis=0)
+        if at % 2:
+            away_ref[at // 2, :quarter] = part.astype(LOW)
+            away_ref[at // 2, quarter:] = sums.astype(LOW)
+        else:
+            near_ref[at // 2, :quarter] = part
+            near_ref[at // 2, quarter:] = sums
+
+
+def qkv_send_kernel(place, near_ref, far_ref, out_ref):
+    total = near_ref[...] + far_ref[...].astype(FULL)
+    rows = total.shape[0] - 16
+    step = rows // 8
+    sums = total[rows:].astype(LOW)
+    for at in range(8):
+        out_ref[at, :step] = total[at * step : (at + 1) * step].astype(LOW)
+        out_ref[at, step:] = sums
+
+
+def qkv_last_kernel(place, parts_ref, grad_ref, sums_ref):
+    step = grad_ref.shape[0]
+    own = parts_ref.shape[2] // 3
+    for at in range(8):
+        for which in range(3):
+            cols = slice((which * 8 + at) * own, (which * 8 + at + 1) * own)
+            grad_ref[:, cols] = parts_ref[at, :step, which * own : (which + 1) * own].astype(FULL)
+    sums = parts_ref[0, step:].astype(FULL)
+    for at in range(1, 8):
+        sums += parts_ref[at, step:].astype(FULL)
+    sums_ref[...] = sums
+
+
+def grouped_body(tokens, out_grad, w_qkv, w_out, fc_in, fc_out, fc_in_bias, vectors):
+    rows, width = tokens.shape
+    own = width // 8
+    seq_at = lax.axis_index("seq")
+    core_at, across_at = lax.rem(seq_at, 2), seq_at // 2
+    head_at, blk_at = lax.axis_index("head"), lax.axis_index("blk")
+    rank = head_at * 4 + blk_at
+    far_at, near_at = blk_at // 2, lax.rem(blk_at, 2)
+    place = jnp.stack(
+        [rank, seq_at, core_at, across_at, head_at, blk_at, far_at ^ core_at, far_at, near_at]
+    ).astype(jnp.int32)
+    unit_rows = fc_in.shape[0] // 4
+    units = 8 * unit_rows
+
+    half = own // 2
+    qkv_half = lax.dynamic_slice_in_dim(w_qkv, core_at * half, half, 0)
+    qkv_half = qkv_half.reshape(half, 3, 8, own).transpose(2, 1, 0, 3).reshape(8, 3 * half, own)
+    small = jnp.concatenate([vectors.T, fc_in_bias.reshape(-1, own)], axis=0)
+    small = jnp.broadcast_to(small[None], (8, 12, own))
+    out_quarter = lax.dynamic_slice_in_dim(w_out, seq_at * 2 * own, 2 * own, 1)
+    out_quarter = out_quarter.reshape(own, 2, own).transpose(1, 0, 2).reshape(1, 2 * own, own)
+    out_quarter = jnp.broadcast_to(out_quarter, (8, 2 * own, own))
+    to_swap = jnp.concatenate(
+        [qkv_half, out_quarter, small, jnp.zeros((8, 4, own), LOW)], axis=1
+    )
+    units_away = jnp.stack(
+        [lax.dynamic_slice_in_dim(w, seq_at * unit_rows, unit_rows, 0) for w in (fc_in, fc_out)]
+    )
+
+    inner = inner_blk()
+    first = lax.ppermute(tokens, "blk", PAIRS)
+    middle = lax.ppermute(tokens, "blk", INNER)
+    across_0 = flip_head(tokens)
+    first, middle, across_0, to_swap = after((first, middle, across_0, to_swap))
+    second_in = lax.ppermute(first, "blk", INNER)
+    second_out = lax.ppermute(middle, "blk", OUTER)
+    across_1 = flip_head(first)
+    swapped = lax.all_to_all(to_swap, GROUP, 0, 0, tiled=True)
+    second_in, second_out, across_1 = after((second_in, second_out, across_1))
+    third = lax.ppermute(second_in, "blk", OUTER)
+    second = jnp.where(inner, second_in, second_out)
+    across_2 = flip_head(second)
+    third, across_2, swapped, units_away = after((third, across_2, swapped, units_away))
+    third = jnp.where(inner, middle, third)
+    across_3 = flip_head(third)
+    own_half = swapped[:, : 3 * half].reshape(8, 3, half, own)
+    other_half = lax.ppermute(own_half, "seq", CORE)
+    out_quarter = swapped[:, 3 * half : 3 * half + 2 * own].reshape(8, 2, own, own)
+    small = swapped[:, 3 * half + 2 * own : 3 * half + 2 * own + 12].astype(FULL)
+    vec = small[:, :8].transpose(1, 0, 2).reshape(8, width)
+    bias_all = small[:, 8:].reshape(32, 1, own)
+    across_3, other_half = after((across_3, other_half))
+    slots = [tokens, first, second, third, across_0, across_1, across_2, across_3]
+
+    units_two_on = lax.ppermute(units_away, "blk", TWO_ON)
+    out_slots = gather_seq(out_quarter)
+
+    bias = vectors.T.reshape(8, 1, own)[4:6].astype(FULL)
+    seq_rows = 8 * rows
+    heads = own // HEAD_DIM
+    kept_shapes = [((seq_rows, own), LOW)] * 3 + [((seq_rows, own), FULL)] * 2
+    kept_shapes.append(((heads, seq_rows, seq_rows), LOW))
+    kept_scratch = [pltpu.VMEM(*shape) for shape in kept_shapes]
+    context, *kept = call(
+        attend_kernel,
+        [shape_of((8, rows, own), LOW)] + [shape_of(*shape) for shape in kept_shapes],
+        place, *slots, own_half, other_half, bias,
+        scratch=kept_scratch + [pltpu.VMEM((width, 3 * own), LOW), pltpu.SemaphoreType.DMA((9,))],
+        flops=8 * 10**9,
+        far_out=6,
+    )
+    context, units_two_on = after((context, units_two_on), *out_slots[1:])
+    context = lax.all_to_all(context, GROUP, 0, 0, tiled=True)
+    ffn_weights = [fc_in, fc_out] + gather_seq(units_two_on)
+    out_scratch = [pltpu.VMEM((8, own, width), LOW), pltpu.SemaphoreType.DMA((8,))]
+
+    per_row = shape_of((rows, width), FULL)
+    per_row_low = shape_of((rows, width), LOW)
+    middle, middle_low, norm_one, scale_one = call(
+        mix_kernel,
+        [per_row, per_row_low, per_row, shape_of((rows, 1), FULL)],
+        place, context, tokens, vec, *out_slots,
+        scratch=[pltpu.VMEM((rows, width), LOW)] + out_scratch,
+        flops=2 * 10**9,
+        far_in=4,
+    )
+
+    both_rows = shape_of((2 * rows, units), FULL)
+    both_rows_low = shape_of((2 * rows, units), LOW)
+    middle_slots = gather_four(middle_low)
+    ffn_scratch = [pltpu.VMEM((2 * rows, width), FULL)]
+    ffn_scratch += [pltpu.VMEM((2, 4 * unit_rows, width), LOW)] * 2
+    ffn_scratch += [pltpu.SemaphoreType.DMA((10,))]
+    ffn_parts = []
+    for at in (0, 2):
+        ffn_parts.append(
+            call(
+                ffn_kernel,
+                [both_rows, both_rows_low, per_row, per_row_low],
+                place, middle_slots[at], middle_slots[at + 1], bias_all, *ffn_weights,
+                scratch=ffn_scratch,
+                flops=3 * 10**9,
+                far_in=6,
+            )
+        )
+
+    def features_of(core, head):
+        both = lax.dynamic_index_in_dim(context.reshape(2, 2, 2, rows, own), core, 1, False)
+        return lax.dynamic_index_in_dim(both, head, 1, False)
+
+    diagonal = []
+    for seq in range(4):
+        for head in range(2):
+            diagonal.append((seq * 2 + head, (seq ^ 1) * 2 + 1 - head))
+    parts = [
+        features_of(core_at, head_at),
+        features_of(1 - core_at, head_at),
+        features_of(core_at, 1 - head_at),
+        features_of(1 - core_at, 1 - head_at),
+    ]
+    parts[1:] = after(parts[1:], ffn_parts[0][1])
+    parts = [
+        parts[0],
+        lax.ppermute(parts[1], "seq", CORE),
+        flip_head(parts[2]),
+        lax.ppermute(parts[3], ("seq", "head"), tuple(diagonal)),
+    ]
+
+    def scatter_parts(near_part, far_part):
+        sent_far = lax.ppermute(far_part[1], "blk", PAIRS).astype(FULL)
+        far = flip_head((far_part[0] + sent_far).astype(LOW))
+        return near_part[0], lax.ppermute(near_part[1], "blk", PAIRS), far
+
+    def scatter_units(near, away):
+        near = near + lax.ppermute(away, "seq", CORE).astype(FULL)
+        near = near[:2] + lax.ppermute(near[2:].astype(LOW), "seq", ACROSS).astype(FULL)
+        return near[0] + lax.ppermute(near[1].astype(LOW), "blk", TWO_ON).astype(FULL)
+
+    summed = scatter_parts(ffn_parts[0][2:4], ffn_parts[1][2:4])
+    three_sums = shape_of((3, width), FULL)
+    layer_output, grad_two, grad_ffn, top_sums = call(
+        top_kernel,
+        [per_row, per_row, per_row_low, three_sums],
+        place, *summed, middle, vec, out_grad,
+        flops=10**9,
+    )
+
+    grad_ffn_slots = gather_four(grad_ffn)
+    back_parts = []
+    for at in (0, 2):
+        pre = ffn_parts[at // 2][0]
+        cdf = 0.5 * (1.0 + lax.erf(pre * (0.5**0.5)))
+        slope = cdf + pre * jnp.exp(-0.5 * pre * pre) * ((2.0 * math.pi) ** -0.5)
+        back_parts.append(
+            call(
+                ffn_back_kernel,
+                [both_rows_low, per_row, per_row_low, shape_of((8, 1, unit_rows), FULL)],
+                place, grad_ffn_slots[at], grad_ffn_slots[at + 1], slope, *ffn_weights,
+                scratch=ffn_scratch,
+                flops=3 * 10**9,
+                far_in=6,
+            )
+        )
+    summed = scatter_parts(back_parts[0][1:3], back_parts[1][1:3])
+    terms = [shape_of((4, unit_rows, width), FULL), shape_of((4, unit_rows, width), LOW)]
+    out_near_grad, out_away_grad = call(
+        weight_grad_kernel, terms, place, ffn_parts[0][1], ffn_parts[1][1], *grad_ffn_slots,
+        flops=2 * 10**9,
+    )
+    grad_fc_out = scatter_units(out_near_grad, out_away_grad)
+    in_near_grad, in_away_grad = call(
+        weight_grad_kernel, terms, place, back_parts[0][0], back_parts[1][0], *middle_slots,
+        flops=2 * 10**9,
+    )
+    summed = after(summed, in_away_grad)
+    grad_one, grad_attn, grad_context, mid_sums = call(
+        mix_back_kernel,
+        [per_row, per_row_low, shape_of((8, rows, own), LOW), three_sums],
+        place, *summed, grad_two, norm_one, scale_one, vec, *out_slots,
+        scratch=out_scratch,
+        flops=2 * 10**9,
+        far_in=4,
+    )
+    grad_context = lax.all_to_all(grad_context, GROUP, 0, 0, tiled=True)
+    grad_fc_in = scatter_units(in_near_grad, in_away_grad)
+    grad_attn_slots = gather_cores(grad_attn)
+
+    grad_cols, near_terms, away_terms = call(
+        attend_back_kernel,
+        [
+            shape_of((8, rows, 3 * own), LOW),
+            shape_of((4, rows, width), FULL),
+            shape_of((4, rows, width), LOW),
+        ],
+        place, grad_context, own_half, other_half, *kept,
+        scratch=[pltpu.VMEM((width, 3 * own), LOW)]
+        + kept_scratch
+        + [pltpu.VMEM((own, seq_rows), FULL)] * 2
+        + [pltpu.SemaphoreType.DMA((9,))],
+        flops=8 * 10**9,
+        far_in=6,
+    )
+    terms = scatter_group(near_terms, away_terms)
+    input_grad = grad_one + terms[0]
+    for term in terms[1:]:
+        input_grad = input_grad + term.astype(FULL)
+
+    payload_rows = 2 * own + 16
+    near, away = call(
+        qkv_grad_kernel,
+        [shape_of((2, payload_rows, 3 * own), FULL), shape_of((2, payload_rows, 3 * own), LOW)],
+        place, *slots, grad_cols, top_sums, mid_sums, back_parts[0][3], back_parts[1][3],
+        scratch=[pltpu.VMEM((width, 3 * own), FULL), pltpu.VMEM((8, width), FULL)],
+        flops=2 * 10**9,
+    )
+    sent = lax.ppermute(away, "seq", CORE).astype(FULL)
+    far = lax.ppermute((near[1] + sent[1]).astype(LOW), "seq", ACROSS)
+
+    out_terms = [shape_of((4, own // 4, width), FULL), shape_of((4, own // 4, width), LOW)]
+    near_rows, away_rows = call(
+        out_grad_kernel, out_terms, place, *parts, *grad_attn_slots, flops=10**9
+    )
+    near_rows = near_rows + lax.ppermute(away_rows, "seq", ACROSS).astype(FULL)
+    grad_w_out = lax.all_to_all(near_rows.astype(LOW), "blk", 0, 0, tiled=True)
+    grad_w_out = jnp.sum(grad_w_out.astype(FULL), axis=0)
+
+    moves = []
+    for across in range(2):
+        for core in range(2):
+            for head in range(2):
+                for two_on in range(2):
+                    for near_by in range(2):
+                        start = (across * 2 + core) * 8 + head * 4 + two_on * 2 + near_by
+                        stop = (head * 2 + core) * 8 + near_by * 4 + two_on * 2 + across
+                        if start != stop:
+                            moves.append((start, stop))
+    stays = (across_at == head_at) & (head_at == near_at)
+
+    def to_owner(grad):
+        moved = lax.ppermute(grad.astype(LOW), ("seq", "head", "blk"), moves).astype(FULL)
+        return jnp.where(stays, grad, moved)
+
+    grad_fc_out, grad_fc_in = to_owner(grad_fc_out), to_owner(grad_fc_in)
+
+    (payload,) = call(
+        qkv_send_kernel,
+        [shape_of((8, own // 4 + 16, 3 * own), LOW)],
+        place, near[0] + sent[0], far,
+    )
+    payload = lax.all_to_all(payload, GROUP, 0, 0, tiled=True)
+    grad_w_qkv, sums = call(
+        qkv_last_kernel,
+        [shape_of((own // 4, 3 * width), FULL), shape_of((16, 3 * own), FULL)],
+        place, payload,
+    )
+    grad_vectors = lax.dynamic_slice(sums, (0, rank * (own // 4)), (8, own // 4)).T
+    grad_bias = lax.dynamic_slice(sums, (rank, 2 * own), (1, own)).reshape(own)
+    return (
+        layer_output,
+        input_grad,
+        grad_w_qkv,
+        grad_w_out,
+        grad_fc_in,
+        grad_fc_out,
+        grad_bias,
+        grad_vectors,
+    )
+
+
 def solution(mesh):
+    sizes = tuple(mesh.shape[name] for name in ("seq", "head", "blk"))
     return jax.shard_map(
-        body,
+        grouped_body if sizes == (4, 2, 4) else general_body,
         mesh=mesh,
         in_specs=(
             P(("seq", "head", "blk"), None),

time: 1830 us -> 324 us (0.18)
  waiting for transfers between devices: 1480 us -> 114 us
  matrix products: 82.4 us -> 0 us
  local copies, waits for them, and re-layouts: 122 us -> 45.6 us
  blocking collectives: 71.5 us -> 0 us
  starting transfers between devices: 21.5 us -> 85.6 us
  Pallas kernels: 0 us -> 47.6 us
    reduce_scatter x2 -> x0, waiting for transfers between devices: 1100 us -> none  [the longest x1 1080 us: body(): lax.psum_scatter(jnp.concatenate([ffn_block, attn_block.reshape(lax.axis_...]
    all_gather x7 -> x0, waiting for transfers between devices: 352 us -> none  [the longest x1 123 us: body(): part_in = lax.all_gather(fc_in, ('head', 'blk'), axis=0, tiled=True)]
    ppermute x0 -> x55, waiting for transfers between devices: none -> 105 us  [the longest x14 26.9 us: flip_head(): return lax.ppermute(value, 'head', FLIP)]
    dot_general x25 -> x0, matrix products: 82.4 us -> none  [the longest x1 11 us: body(): jnp.einsum('td,fd->tf', middle_low, part_in, preferred_element_type=jnp.f...]
    ppermute x0 -> x55, starting transfers between devices: none -> 63.7 us  [the longest x14 15.9 us: flip_head(): return lax.ppermute(value, 'head', FLIP)]
    concatenate x2 -> x1, local copies, waits for them, and re-layouts: 60.3 us -> 0.08 us  [grouped_body(): jnp.concatenate([qkv_half, out_quarter, small, jnp.zeros((8, 4, own), LOW...]
    all_gather x2 -> x0, blocking collectives: 54.9 us -> none  [the longest x1 27.7 us: body(): part_vec = lax.all_gather(vectors, ('head', 'blk'), axis=0, tiled=True)]
    pallas_call x0 -> x15, Pallas kernels: none -> 47.6 us  [call(): pl.pallas_call(kernel, out_shape=outs, in_specs=[pl.BlockSpec(memory_spac...]
  transfers between devices with their start and end apart: 15 -> 60, of which waited for: 12 -> 25; matrix products, arithmetic and copies ran while one was open for 11% -> 11% of each run, Pallas kernels for 0% -> 13%
where the time goes in v2:
time: 324 us; the launch traced here: 321 us
  waiting for transfers between devices  114 us (35%)
  starting transfers between devices  85.6 us (26%)
  Pallas kernels  47.6 us (15%)
  local copies, waits for them, and re-layouts  45.6 us (14%)
  other arithmetic  27.4 us (8%)
    pallas_call x15, Pallas kernels, call(): pl.pallas_call(kernel, out_shape=outs, in_specs=[pl.BlockSpec(memory_spac...  47.6 us
    unnamed x167, local copies, waits for them, and re-layouts  34.8 us
    ppermute x14, waiting for transfers between devices, flip_head(): return lax.ppermute(value, 'head', FLIP)  26.9 us
    ppermute x14, starting transfers between devices, flip_head(): return lax.ppermute(value, 'head', FLIP)  15.9 us
    ppermute x1, waiting for transfers between devices, grouped_body(): second_out = lax.ppermute(middle, 'blk', OUTER)  15.2 us
    ppermute x2, waiting for transfers between devices, to_owner(): lax.ppermute(grad.astype(LOW), ('seq', 'head', 'blk'), moves).astype(FULL)  14.9 us
    ppermute x2, waiting for transfers between devices, gather_four(): return [own, beside, across, lax.ppermute(across, 'blk', PAIRS)]  13.2 us
    ppermute x1, waiting for transfers between devices, grouped_body(): third = lax.ppermute(second_in, 'blk', OUTER)  9.11 us
  transfers between devices with their start and end apart: 60, of which 25 were waited for; matrix products, arithmetic and copies ran while one was open for 11% of the time, Pallas kernels for 13%

profile of v2, /device:TPU:2, one launch (start us, length us, event | category | flops | bytes accessed | tf_op | source)
XLA Modules:
  0.0 321.4 jit_solution(7052212011053442566)
XLA Ops:
  2.9 4.5 %collective-permute-start = (bf16[128,1024]{1,0:T(8,128)(2,1)}, bf16[128,1024]{1,0:T(8,128)(2,1)S(1)}, u32[]{:S(2)}, u32[]{:S(2)}) collective-permute-start(bf16[128,1024]{1,0:T(8,128)(2,1)} %refs_0_.7), channel_id=1, source_target_pairs={{0,1},{1,0},{2,3},{3,2},{4,5},{5,4},{6,7},{7,6},{8,9},{9,8},{10,11... | collective-permute-start | bytes 786440 | tf_op jit(solution)/shard_map/ppermute | solution.py:815
  10.8 2.6 collective-permute-done.refs_1_
  13.3 4.2 %all-to-all-start = ((bf16[8,464,128]{2,1,0:T(8,128)(2,1)}), bf16[8,464,128]{2,1,0:T(8,128)(2,1)}, u32[]{:S(2)}, u32[]{:S(2)}) async-start(bf16[8,464,128]{2,1,0:T(8,128)(2,1)} %maximum_maximum_fusion), calls=%async_computation | async-start | bytes 1900544 | tf_op jit(solution)/shard_map/all_to_all | solution.py:822
  21.5 15.2 %collective-permute-done.4 = bf16[128,1024]{1,0:T(8,128)(2,1)S(1)} collective-permute-done((bf16[128,1024]{1,0:T(8,128)(2,1)S(1)}, bf16[128,1024]{1,0:T(8,128)(2,1)S(1)}, u32[]{:S(2)}, u32[]{:S(2)}) %collective-permute-start.4) | collective-permute-done | bytes 262176 | tf_op jit(solution)/shard_map/ppermute | solution.py:820
  41.4 3.1 collective-permute-done.7.refs_6_
  44.5 9.1 %collective-permute-done.6 = bf16[128,1024]{1,0:T(8,128)(2,1)S(1)} collective-permute-done((bf16[128,1024]{1,0:T(8,128)(2,1)S(1)}, bf16[128,1024]{1,0:T(8,128)(2,1)S(1)}, u32[]{:S(2)}, u32[]{:S(2)}) %collective-permute-start.6) | collective-permute-done | bytes 262176 | tf_op jit(solution)/shard_map/ppermute | solution.py:824
  61.3 5.1 %collective-permute-done.8.refs_7_ = bf16[128,1024]{1,0:T(8,128)(2,1)} collective-permute-done((bf16[128,1024]{1,0:T(8,128)(2,1)S(1)}, bf16[128,1024]{1,0:T(8,128)(2,1)}, u32[]{:S(2)}, u32[]{:S(2)}) %collective-permute-start.8) | collective-permute-done | bytes 262176 | tf_op jit(solution)/shard_map/ppermute | solution.py:315
  71.5 8.8 %shard_map.143 = (bf16[8,128,128]{2,1,0:T(8,128)(2,1)}, bf16[1024,128]{1,0:T(8,128)(2,1)S(1)}, bf16[1024,128]{1,0:T(8,128)(2,1)S(1)}, bf16[1024,128]{1,0:T(8,128...) custom-call(s32[9]{0:T(128)S(1)} %stack.48.place, ...), custom_call_target="tpu_custom_call" | custom-call | flops 8000000000 | bytes 9176064 | tf_op jit(solution)/shard_map/pallas_call | solution.py:363
  88.5 5.9 %all-to-all-start.1 = ((bf16[8,128,128]{2,1,0:T(8,128)(2,1)}), bf16[8,128,128]{2,1,0:T(8,128)(2,1)S(1)}, u32[]{:S(2)}, u32[]{:S(2)}) async-start(bf16[8,128,128]{2,1,0:T(8,128)(2,1)} %get-tuple-element.97), calls=%async_computation.1 | async-start | bytes 524288 | tf_op jit(solution)/shard_map/all_to_all | solution.py:857
  95.8 8.8 %all-to-all-done.1.context_ref = bf16[8,128,128]{2,1,0:T(8,128)(2,1)S(1)} async-done(((bf16[8,128,128]{2,1,0:T(8,128)(2,1)}), bf16[8,128,128]{2,1,0:T(8,128)(2,1)S(1)}, u32[]{:S(2)}, u32[]{:S(2)}) %all-to-all-start.1) | async-done | bytes 262176 | tf_op jit(solution)/shard_map/all_to_all | solution.py:857
  111.4 6.0 %collective-permute-done.19.first_ref.refs_2_ = bf16[128,1024]{1,0:T(8,128)(2,1)S(1)} collective-permute-done((bf16[128,1024]{1,0:T(8,128)(2,1)S(1)}, bf16[128,1024]{1,0:T(8,128)(2,1)S(1)}, u32[]{:S(2)}, u32[]{:S(2)}) %collective-permute-start.19) | collective-permute-done | bytes 262176 | tf_op jit(solution)/shard_map/ppermute | solution.py:315
  119.4 6.5 %collective-permute-done.20.second_ref.refs_3_ = bf16[128,1024]{1,0:T(8,128)(2,1)S(1)} collective-permute-done((bf16[128,1024]{1,0:T(8,128)(2,1)S(1)}, bf16[128,1024]{1,0:T(8,128)(2,1)S(1)}, u32[]{:S(2)}, u32[]{:S(2)}) %collective-permute-start.20) | collective-permute-done | bytes 262176 | tf_op jit(solution)/shard_map/ppermute | solution.py:346
  125.9 3.3 %shard_map.146 = (f32[256,1024]{1,0:T(8,128)S(1)}, bf16[256,1024]{1,0:T(8,128)(2,1)S(1)}, f32[128,1024]{1,0:T(8,128)S(1)}, bf16[128,1024]{1,0:T(8,128)(2,1)S(1)}) custom-call(s32[9]{0:T(128)S(1)} %stack.48.place, bf16[128,1024]{1,0:T(8,128)(2,1)S(1)} %collective-permute-done.19.first_ref.refs_2_, ...), custom_call_target="tpu_custom_call" | custom-call | flops 3000000000 | bytes 7094272 | tf_op jit(solution)/shard_map/pallas_call | solution.py:363
  131.2 3.3 %shard_map.145 = (f32[256,1024]{1,0:T(8,128)S(1)}, bf16[256,1024]{1,0:T(8,128)(2,1)S(1)}, f32[128,1024]{1,0:T(8,128)S(1)}, bf16[128,1024]{1,0:T(8,128)(2,1)S(1)}) custom-call(s32[9]{0:T(128)S(1)} %stack.48.place, bf16[128,1024]{1,0:T(8,128)(2,1)S(1)} %get-tuple-element.98.first_ref.refs_0_, bf16[128,1024]{1,0:T(8,128)(2,1)S(1)} %collective-permute-done.14.second_ref.refs_1_, ...), custom_call_target="tpu_custom_call" | custom-call | flops 3000000000 | bytes 7094272 | tf_op jit(solution)/shard_map/pallas_call | solution.py:363
  139.0 2.7 collective-permute-done.18.sent_ref
  141.8 5.1 %collective-permute-done.22.far_ref = bf16[128,1024]{1,0:T(8,128)(2,1)S(1)} collective-permute-done((bf16[128,1024]{1,0:T(8,128)(2,1)S(1)}, bf16[128,1024]{1,0:T(8,128)(2,1)S(1)}, u32[]{:S(2)}, u32[]{:S(2)}) %collective-permute-start.22) | collective-permute-done | bytes 262176 | tf_op jit(solution)/shard_map/ppermute | solution.py:315
  149.8 5.2 %collective-permute-done.25.first_ref.refs_2_ = bf16[128,1024]{1,0:T(8,128)(2,1)S(1)} collective-permute-done((bf16[128,1024]{1,0:T(8,128)(2,1)S(1)}, bf16[128,1024]{1,0:T(8,128)(2,1)S(1)}, u32[]{:S(2)}, u32[]{:S(2)}) %collective-permute-start.25) | collective-permute-done | bytes 262176 | tf_op jit(solution)/shard_map/ppermute | solution.py:315
  157.4 6.7 %collective-permute-done.26.second_ref.refs_3_ = bf16[128,1024]{1,0:T(8,128)(2,1)S(1)} collective-permute-done((bf16[128,1024]{1,0:T(8,128)(2,1)S(1)}, bf16[128,1024]{1,0:T(8,128)(2,1)S(1)}, u32[]{:S(2)}, u32[]{:S(2)}) %collective-permute-start.26) | collective-permute-done | bytes 262176 | tf_op jit(solution)/shard_map/ppermute | solution.py:346
  164.1 3.3 %shard_map.149 = (bf16[256,1024]{1,0:T(8,128)(2,1)S(1)}, f32[128,1024]{1,0:T(8,128)S(1)}, bf16[128,1024]{1,0:T(8,128)(2,1)S(1)}, f32[8,1,128]{2,1,0:T(1,128)S(1)}) custom-call(s32[9]{0:T(128)S(1)} %stack.48.place, bf16[128,1024]{1,0:T(8,128)(2,1)S(1)} %collective-permute-done.25.first_ref.refs_2_, ...), custom_call_target="tpu_custom_call" | custom-call | flops 3000000000 | bytes 7081984 | tf_op jit(solution)/shard_map/pallas_call | solution.py:363
  169.7 3.5 %shard_map.148 = (bf16[256,1024]{1,0:T(8,128)(2,1)S(1)}, f32[128,1024]{1,0:T(8,128)S(1)}, bf16[128,1024]{1,0:T(8,128)(2,1)S(1)}, f32[8,1,128]{2,1,0:T(1,128)S(1)}) custom-call(s32[9]{0:T(128)S(1)} %stack.48.place, bf16[128,1024]{1,0:T(8,128)(2,1)S(1)} %get-tuple-element.106.first_ref.refs_0_, ...), custom_call_target="tpu_custom_call" | custom-call | flops 3000000000 | bytes 7081984 | tf_op jit(solution)/shard_map/pallas_call | solution.py:363
  181.1 3.2 shard_map.151
  184.3 3.4 %all-to-all-start.2 = ((bf16[8,128,128]{2,1,0:T(8,128)(2,1)}), bf16[8,128,128]{2,1,0:T(8,128)(2,1)S(1)}, u32[]{:S(2)}, u32[]{:S(2)}) async-start(bf16[8,128,128]{2,1,0:T(8,128)(2,1)} %get-tuple-element.123), calls=%async_computation.2 | async-start | bytes 524288 | tf_op jit(solution)/shard_map/all_to_all | solution.py:968
  207.8 6.9 %shard_map.152 = (bf16[8,128,384]{2,1,0:T(8,128)(2,1)S(1)}, f32[4,128,1024]{2,1,0:T(8,128)S(1)}, bf16[4,128,1024]{2,1,0:T(8,128)(2,1)S(1)}) custom-call(s32[9]{0:T(128)S(1)} %stack.48.place, bf16[8,128,128]{2,1,0:T(8,128)(2,1)S(1)} %all-to-all-done.2.grad_ref, bf16[8,3,64,128]{3,2,1,0:T(8,128)(2,1)S(1)} %bitcast.120, bf16[8,3,64,128]{3,2,1,0:T(8,128)(2,1)S(1)} %copy-done.27, ...), custom_call_target="tpu_custom_call" | custom-call | flops 8000000000 | bytes 11010048 | tf_op jit(solution)/shard_map/pallas_call | solution.py:363
  233.0 4.1 %collective-permute-start.31 = (bf16[128,1024]{1,0:T(8,128)(2,1)}, bf16[128,1024]{1,0:T(8,128)(2,1)}, u32[]{:S(2)}, u32[]{:S(2)}) collective-permute-start(bf16[128,1024]{1,0:T(8,128)(2,1)} %fusion.19), channel_id=1, source_target_pairs={{0,1},{3,2},{4,5},{7,6},{8,9},{11,10},{12,13},{15,14},{16,17},{19,... | collective-permute-start | bytes 786440 | tf_op jit(solution)/shard_map/ppermute | solution.py:322
  237.2 7.5 %collective-permute-done.46 = bf16[4,32,1024]{2,1,0:T(8,128)(2,1)S(1)} collective-permute-done((bf16[4,32,1024]{2,1,0:T(8,128)(2,1)S(1)}, bf16[4,32,1024]{2,1,0:T(8,128)(2,1)S(1)}, u32[]{:S(2)}, u32[]{:S(2)}) %collective-permute-start.46) | collective-permute-done | bytes 262176 | tf_op jit(solution)/shard_map/ppermute | solution.py:1007
  247.1 4.6 %all-to-all-start.4 = ((bf16[4,32,1024]{2,1,0:T(8,128)(2,1)}), bf16[4,32,1024]{2,1,0:T(8,128)(2,1)}, u32[]{:S(2)}, u32[]{:S(2)}) async-start(bf16[4,32,1024]{2,1,0:T(8,128)(2,1)} %add_convert_fusion), calls=%async_computation.4 | async-start | bytes 524288 | tf_op jit(solution)/shard_map/all_to_all | solution.py:1008
  258.0 6.6 %collective-permute-start.32 = (bf16[128,1024]{1,0:T(8,128)(2,1)}, bf16[128,1024]{1,0:T(8,128)(2,1)}, u32[]{:S(2)}, u32[]{:S(2)}) collective-permute-start(bf16[128,1024]{1,0:T(8,128)(2,1)} %fusion.13), channel_id=1, source_target_pairs={{0,1},{3,2},{4,5},{7,6},{8,9},{11,10},{12,13},{15,14},{16,17},{19,... | collective-permute-start | bytes 786440 | tf_op jit(solution)/shard_map/ppermute | solution.py:326
  269.3 2.9 collective-permute-start.49
  273.5 3.8 %all-to-all-start.3 = ((bf16[8,48,384]{2,1,0:T(8,128)(2,1)}), bf16[8,48,384]{2,1,0:T(8,128)(2,1)S(1)}, u32[]{:S(2)}, u32[]{:S(2)}) async-start(bf16[8,48,384]{2,1,0:T(8,128)(2,1)} %shard_map.154), calls=%async_computation.3 | async-start | bytes 589824 | tf_op jit(solution)/shard_map/all_to_all | solution.py:1034
  283.3 4.2 %collective-permute-start.37 = (bf16[128,1024]{1,0:T(8,128)(2,1)S(1)}, bf16[128,1024]{1,0:T(8,128)(2,1)S(1)}, u32[]{:S(2)}, u32[]{:S(2)}) collective-permute-start(bf16[128,1024]{1,0:T(8,128)(2,1)S(1)} %get-tuple-element.137), channel_id=1, source_target_pairs={{0,1},{1,0},{2,3},{3,2},{4,5},{5,4},{6,7},{7,6},{8,9},{9,8},{10,11... | collective-permute-start | bytes 786440 | tf_op jit(solution)/shard_map/ppermute | solution.py:333
  296.1 3.1 collective-permute-start.50
  300.4 13.4 %collective-permute-done.54 = bf16[128,1024]{1,0:T(8,128)(2,1)S(1)} collective-permute-done((bf16[128,1024]{1,0:T(8,128)(2,1)S(1)}, bf16[128,1024]{1,0:T(8,128)(2,1)S(1)}, u32[]{:S(2)}, u32[]{:S(2)}) %collective-permute-start.54) | collective-permute-done | bytes 262176 | tf_op jit(solution)/shard_map/ppermute | solution.py:1024
  (318 shorter events, 143.1 us)
Async XLA Ops:
  13.3 40.3 %all-to-all-start = ((bf16[8,464,128]{2,1,0:T(8,128)(2,1)}), bf16[8,464,128]{2,1,0:T(8,128)(2,1)}, u32[]{:S(2)}, u32[]{:S(2)}) async-start(bf16[8,464,128]{2,1,0:T(8,128)(2,1)} %maximum_maximum_fusion), calls=%async_computation | async-start | bytes 1900544 | tf_op jit(solution)/shard_map/all_to_all | solution.py:822
  17.6 19.2 %collective-permute-start.4 = (bf16[128,1024]{1,0:T(8,128)(2,1)S(1)}, bf16[128,1024]{1,0:T(8,128)(2,1)S(1)}, u32[]{:S(2)}, u32[]{:S(2)}) collective-permute-start(bf16[128,1024]{1,0:T(8,128)(2,1)S(1)} %collective-permute-done.1), channel_id=1, source_target_pairs={{1,0},{2,3},{5,4},{6,7},{9,8},{10,11},{13,12},{14,15},{17,16},{18,... | collective-permute-start | bytes 786440 | tf_op jit(solution)/shard_map/ppermute | solution.py:820
  18.9 17.9 %collective-permute-start.5 = (bf16[128,1024]{1,0:T(8,128)(2,1)S(1)}, bf16[128,1024]{1,0:T(8,128)(2,1)S(1)}, u32[]{:S(2)}, u32[]{:S(2)}) collective-permute-start(bf16[128,1024]{1,0:T(8,128)(2,1)S(1)} %collective-permute-done.refs_1_), channel_id=1, source_target_pairs={{0,4},{4,0},{1,5},{5,1},{2,6},{6,2},{3,7},{7,3},{8,12},{12,8},{9,1... | collective-permute-start | bytes 786440 | tf_op jit(solution)/shard_map/ppermute | solution.py:315
  20.8 15.9 %collective-permute-start.3 = (bf16[128,1024]{1,0:T(8,128)(2,1)S(1)}, bf16[128,1024]{1,0:T(8,128)(2,1)S(1)}, u32[]{:S(2)}, u32[]{:S(2)}) collective-permute-start(bf16[128,1024]{1,0:T(8,128)(2,1)S(1)} %collective-permute-done.refs_1_), channel_id=1, source_target_pairs={{1,2},{2,1},{5,6},{6,5},{9,10},{10,9},{13,14},{14,13},{17,18},{18,... | collective-permute-start | bytes 786440 | tf_op jit(solution)/shard_map/ppermute | solution.py:819
  58.9 27.2 %collective-permute-start.11 = (bf16[8,2,128,128]{3,2,1,0:T(8,128)(2,1)S(1)}, bf16[8,2,128,128]{3,2,1,0:T(8,128)(2,1)S(1)}, u32[]{:S(2)}, u32[]{:S(2)}) collective-permute-start(bf16[8,2,128,128]{3,2,1,0:T(8,128)(2,1)S(1)} %bitcast.115), channel_id=1, source_target_pairs={{0,8},{8,0},{16,24},{24,16},{1,9},{9,1},{17,25},{25,17},{2,10},{10... | collective-permute-start | bytes 1572872 | tf_op jit(solution)/shard_map/ppermute | solution.py:340
  59.1 27.8 %collective-permute-start.10 = (bf16[2,128,1024]{2,1,0:T(8,128)(2,1)}, bf16[2,128,1024]{2,1,0:T(8,128)(2,1)S(1)}, u32[]{:S(2)}, u32[]{:S(2)}) collective-permute-start(bf16[2,128,1024]{2,1,0:T(8,128)(2,1)} %pad_maximum_fusion), channel_id=1, source_target_pairs={{0,2},{2,0},{1,3},{3,1},{4,6},{6,4},{5,7},{7,5},{8,10},{10,8},{9,1... | collective-permute-start | bytes 1572872 | tf_op jit(solution)/shard_map/ppermute | solution.py:839
  66.4 20.4 %collective-permute-start.13 = (bf16[8,2,128,128]{3,2,1,0:T(8,128)(2,1)S(1)}, bf16[8,2,128,128]{3,2,1,0:T(8,128)(2,1)S(1)}, u32[]{:S(2)}, u32[]{:S(2)}) collective-permute-start(bf16[8,2,128,128]{3,2,1,0:T(8,128)(2,1)S(1)} %collective-permute-done.12.refs_2_), channel_id=1, source_target_pairs={{0,8},{8,0},{16,24},{24,16},{1,9},{9,1},{17,25},{25,17},{2,10},{10... | collective-permute-start | bytes 1572872 | tf_op jit(solution)/shard_map/ppermute | solution.py:340
  88.5 16.2 %all-to-all-start.1 = ((bf16[8,128,128]{2,1,0:T(8,128)(2,1)}), bf16[8,128,128]{2,1,0:T(8,128)(2,1)S(1)}, u32[]{:S(2)}, u32[]{:S(2)}) async-start(bf16[8,128,128]{2,1,0:T(8,128)(2,1)} %get-tuple-element.97), calls=%async_computation.1 | async-start | bytes 524288 | tf_op jit(solution)/shard_map/all_to_all | solution.py:857
  94.4 17.0 %collective-permute-start.16 = (bf16[2,128,1024]{2,1,0:T(8,128)(2,1)}, bf16[2,128,1024]{2,1,0:T(8,128)(2,1)}, u32[]{:S(2)}, u32[]{:S(2)}) collective-permute-start(bf16[2,128,1024]{2,1,0:T(8,128)(2,1)} %copy-done.24), channel_id=1, source_target_pairs={{0,16},{8,24},{16,0},{24,8},{1,17},{9,25},{17,1},{25,9},{2,18},{10... | collective-permute-start | bytes 1572872 | tf_op jit(solution)/shard_map/ppermute | solution.py:339
  95.7 23.7 %collective-permute-start.15 = (bf16[2,128,1024]{2,1,0:T(8,128)(2,1)}, bf16[2,128,1024]{2,1,0:T(8,128)(2,1)}, u32[]{:S(2)}, u32[]{:S(2)}) collective-permute-start(bf16[2,128,1024]{2,1,0:T(8,128)(2,1)} %copy-done.24), channel_id=1, source_target_pairs={{0,8},{8,0},{16,24},{24,16},{1,9},{9,1},{17,25},{25,17},{2,10},{10... | collective-permute-start | bytes 1572872 | tf_op jit(solution)/shard_map/ppermute | solution.py:340
  184.3 16.3 %all-to-all-start.2 = ((bf16[8,128,128]{2,1,0:T(8,128)(2,1)}), bf16[8,128,128]{2,1,0:T(8,128)(2,1)S(1)}, u32[]{:S(2)}, u32[]{:S(2)}) async-start(bf16[8,128,128]{2,1,0:T(8,128)(2,1)} %get-tuple-element.123), calls=%async_computation.2 | async-start | bytes 524288 | tf_op jit(solution)/shard_map/all_to_all | solution.py:968
  188.5 30.5 %collective-permute-start.40 = (bf16[2,128,128]{2,1,0:T(8,128)(2,1)}, bf16[2,128,128]{2,1,0:T(8,128)(2,1)}, u32[]{:S(2)}, u32[]{:S(2)}) collective-permute-start(bf16[2,128,128]{2,1,0:T(8,128)(2,1)} %get-tuple-element.147), channel_id=1, source_target_pairs={{0,8},{8,0},{16,24},{24,16},{1,9},{9,1},{17,25},{25,17},{2,10},{10... | collective-permute-start | bytes 196616 | tf_op jit(solution)/shard_map/ppermute | solution.py:908
  188.5 35.1 %collective-permute-start.41 = (bf16[2,128,128]{2,1,0:T(8,128)(2,1)}, bf16[2,128,128]{2,1,0:T(8,128)(2,1)}, u32[]{:S(2)}, u32[]{:S(2)}) collective-permute-start(bf16[2,128,128]{2,1,0:T(8,128)(2,1)} %get-tuple-element.148), channel_id=1, source_target_pairs={{0,4},{4,0},{1,5},{5,1},{2,6},{6,2},{3,7},{7,3},{8,12},{12,8},{9,1... | collective-permute-start | bytes 196616 | tf_op jit(solution)/shard_map/ppermute | solution.py:315
  190.4 37.5 %collective-permute-start.47 = (bf16[4,128,1024]{2,1,0:T(8,128)(2,1)}, bf16[4,128,1024]{2,1,0:T(8,128)(2,1)}, u32[]{:S(2)}, u32[]{:S(2)}) collective-permute-start(bf16[4,128,1024]{2,1,0:T(8,128)(2,1)} %get-tuple-element.115), channel_id=1, source_target_pairs={{0,8},{8,0},{16,24},{24,16},{1,9},{9,1},{17,25},{25,17},{2,10},{10... | collective-permute-start | bytes 3145736 | tf_op jit(solution)/shard_map/ppermute | solution.py:919
  200.2 20.7 %collective-permute-start.51 = (bf16[4,128,1024]{2,1,0:T(8,128)(2,1)}, bf16[4,128,1024]{2,1,0:T(8,128)(2,1)}, u32[]{:S(2)}, u32[]{:S(2)}) collective-permute-start(bf16[4,128,1024]{2,1,0:T(8,128)(2,1)} %get-tuple-element.156), channel_id=1, source_target_pairs={{0,8},{8,0},{16,24},{24,16},{1,9},{9,1},{17,25},{25,17},{2,10},{10... | collective-permute-start | bytes 3145736 | tf_op jit(solution)/shard_map/ppermute | solution.py:919
  200.5 19.9 %collective-permute-start.44 = (bf16[128,1024]{1,0:T(8,128)(2,1)}, bf16[128,1024]{1,0:T(8,128)(2,1)}, u32[]{:S(2)}, u32[]{:S(2)}) collective-permute-start(bf16[128,1024]{1,0:T(8,128)(2,1)} %get-tuple-element.150.refs_4_), channel_id=1, source_target_pairs={{0,4},{4,0},{1,5},{5,1},{2,6},{6,2},{3,7},{7,3},{8,12},{12,8},{9,1... | collective-permute-start | bytes 786440 | tf_op jit(solution)/shard_map/ppermute | solution.py:315
  224.0 27.7 %collective-permute-start.38 = (bf16[2,272,384]{2,1,0:T(8,128)(2,1)S(1)}, bf16[2,272,384]{2,1,0:T(8,128)(2,1)}, u32[]{:S(2)}, u32[]{:S(2)}) collective-permute-start(bf16[2,272,384]{2,1,0:T(8,128)(2,1)S(1)} %get-tuple-element.144), channel_id=1, source_target_pairs={{0,8},{8,0},{16,24},{24,16},{1,9},{9,1},{17,25},{25,17},{2,10},{10... | collective-permute-start | bytes 1253384 | tf_op jit(solution)/shard_map/ppermute | solution.py:1000
  224.1 40.5 %collective-permute-start.52 = (bf16[2,128,1024]{2,1,0:T(8,128)(2,1)}, bf16[2,128,1024]{2,1,0:T(8,128)(2,1)}, u32[]{:S(2)}, u32[]{:S(2)}) collective-permute-start(bf16[2,128,1024]{2,1,0:T(8,128)(2,1)} %slice.172), channel_id=1, source_target_pairs={{0,16},{8,24},{16,0},{24,8},{1,17},{9,25},{17,1},{25,9},{2,18},{10... | collective-permute-start | bytes 1572872 | tf_op jit(solution)/shard_map/ppermute | solution.py:920
  226.2 18.5 %collective-permute-start.46 = (bf16[4,32,1024]{2,1,0:T(8,128)(2,1)S(1)}, bf16[4,32,1024]{2,1,0:T(8,128)(2,1)S(1)}, u32[]{:S(2)}, u32[]{:S(2)}) collective-permute-start(bf16[4,32,1024]{2,1,0:T(8,128)(2,1)S(1)} %get-tuple-element.152), channel_id=1, source_target_pairs={{0,16},{8,24},{16,0},{24,8},{1,17},{9,25},{17,1},{25,9},{2,18},{10... | collective-permute-start | bytes 786440 | tf_op jit(solution)/shard_map/ppermute | solution.py:1007
  230.3 36.9 %collective-permute-start.48 = (bf16[2,128,1024]{2,1,0:T(8,128)(2,1)}, bf16[2,128,1024]{2,1,0:T(8,128)(2,1)}, u32[]{:S(2)}, u32[]{:S(2)}) collective-permute-start(bf16[2,128,1024]{2,1,0:T(8,128)(2,1)} %slice.173), channel_id=1, source_target_pairs={{0,16},{8,24},{16,0},{24,8},{1,17},{9,25},{17,1},{25,9},{2,18},{10... | collective-permute-start | bytes 1572872 | tf_op jit(solution)/shard_map/ppermute | solution.py:920
  233.0 21.7 %collective-permute-start.31 = (bf16[128,1024]{1,0:T(8,128)(2,1)}, bf16[128,1024]{1,0:T(8,128)(2,1)}, u32[]{:S(2)}, u32[]{:S(2)}) collective-permute-start(bf16[128,1024]{1,0:T(8,128)(2,1)} %fusion.19), channel_id=1, source_target_pairs={{0,1},{3,2},{4,5},{7,6},{8,9},{11,10},{12,13},{15,14},{16,17},{19,... | collective-permute-start | bytes 786440 | tf_op jit(solution)/shard_map/ppermute | solution.py:322
  247.1 26.4 %all-to-all-start.4 = ((bf16[4,32,1024]{2,1,0:T(8,128)(2,1)}), bf16[4,32,1024]{2,1,0:T(8,128)(2,1)}, u32[]{:S(2)}, u32[]{:S(2)}) async-start(bf16[4,32,1024]{2,1,0:T(8,128)(2,1)} %add_convert_fusion), calls=%async_computation.4 | async-start | bytes 524288 | tf_op jit(solution)/shard_map/all_to_all | solution.py:1008
  256.6 22.4 %collective-permute-start.34 = (bf16[128,1024]{1,0:T(8,128)(2,1)}, bf16[128,1024]{1,0:T(8,128)(2,1)}, u32[]{:S(2)}, u32[]{:S(2)}) collective-permute-start(bf16[128,1024]{1,0:T(8,128)(2,1)} %fusion.13), channel_id=1, source_target_pairs={{1,2},{2,1},{5,6},{6,5},{9,10},{10,9},{13,14},{14,13},{17,18},{18,... | collective-permute-start | bytes 786440 | tf_op jit(solution)/shard_map/ppermute | solution.py:327
  258.0 21.1 %collective-permute-start.32 = (bf16[128,1024]{1,0:T(8,128)(2,1)}, bf16[128,1024]{1,0:T(8,128)(2,1)}, u32[]{:S(2)}, u32[]{:S(2)}) collective-permute-start(bf16[128,1024]{1,0:T(8,128)(2,1)} %fusion.13), channel_id=1, source_target_pairs={{0,1},{3,2},{4,5},{7,6},{8,9},{11,10},{12,13},{15,14},{16,17},{19,... | collective-permute-start | bytes 786440 | tf_op jit(solution)/shard_map/ppermute | solution.py:326
  267.2 22.3 %collective-permute-start.53 = (bf16[128,1024]{1,0:T(8,128)(2,1)}, bf16[128,1024]{1,0:T(8,128)(2,1)}, u32[]{:S(2)}, u32[]{:S(2)}) collective-permute-start(bf16[128,1024]{1,0:T(8,128)(2,1)} %fusion.23), channel_id=1, source_target_pairs={{0,2},{2,0},{1,3},{3,1},{4,6},{6,4},{5,7},{7,5},{8,10},{10,8},{9,1... | collective-permute-start | bytes 786440 | tf_op jit(solution)/shard_map/ppermute | solution.py:921
  269.3 25.8 %collective-permute-start.49 = (bf16[128,1024]{1,0:T(8,128)(2,1)}, bf16[128,1024]{1,0:T(8,128)(2,1)}, u32[]{:S(2)}, u32[]{:S(2)}) collective-permute-start(bf16[128,1024]{1,0:T(8,128)(2,1)} %fusion.22), channel_id=1, source_target_pairs={{0,2},{2,0},{1,3},{3,1},{4,6},{6,4},{5,7},{7,5},{8,10},{10,8},{9,1... | collective-permute-start | bytes 786440 | tf_op jit(solution)/shard_map/ppermute | solution.py:921
  273.5 45.4 %all-to-all-start.3 = ((bf16[8,48,384]{2,1,0:T(8,128)(2,1)}), bf16[8,48,384]{2,1,0:T(8,128)(2,1)S(1)}, u32[]{:S(2)}, u32[]{:S(2)}) async-start(bf16[8,48,384]{2,1,0:T(8,128)(2,1)} %shard_map.154), calls=%async_computation.3 | async-start | bytes 589824 | tf_op jit(solution)/shard_map/all_to_all | solution.py:1034
  280.5 18.7 %collective-permute-start.35 = (bf16[128,1024]{1,0:T(8,128)(2,1)S(1)}, bf16[128,1024]{1,0:T(8,128)(2,1)S(1)}, u32[]{:S(2)}, u32[]{:S(2)}) collective-permute-start(bf16[128,1024]{1,0:T(8,128)(2,1)S(1)} %copy-done.80), channel_id=1, source_target_pairs={{0,4},{4,0},{1,5},{5,1},{2,6},{6,2},{3,7},{7,3},{8,12},{12,8},{9,1... | collective-permute-start | bytes 786440 | tf_op jit(solution)/shard_map/ppermute | solution.py:315
  282.6 16.7 %collective-permute-start.36 = (bf16[128,1024]{1,0:T(8,128)(2,1)S(1)}, bf16[128,1024]{1,0:T(8,128)(2,1)S(1)}, u32[]{:S(2)}, u32[]{:S(2)}) collective-permute-start(bf16[128,1024]{1,0:T(8,128)(2,1)S(1)} %get-tuple-element.136), channel_id=1, source_target_pairs={{1,2},{2,1},{5,6},{6,5},{9,10},{10,9},{13,14},{14,13},{17,18},{18,... | collective-permute-start | bytes 786440 | tf_op jit(solution)/shard_map/ppermute | solution.py:332
  283.3 16.1 %collective-permute-start.37 = (bf16[128,1024]{1,0:T(8,128)(2,1)S(1)}, bf16[128,1024]{1,0:T(8,128)(2,1)S(1)}, u32[]{:S(2)}, u32[]{:S(2)}) collective-permute-start(bf16[128,1024]{1,0:T(8,128)(2,1)S(1)} %get-tuple-element.137), channel_id=1, source_target_pairs={{0,1},{1,0},{2,3},{3,2},{4,5},{5,4},{6,7},{7,6},{8,9},{9,8},{10,11... | collective-permute-start | bytes 786440 | tf_op jit(solution)/shard_map/ppermute | solution.py:333
  290.7 23.1 %collective-permute-start.54 = (bf16[128,1024]{1,0:T(8,128)(2,1)S(1)}, bf16[128,1024]{1,0:T(8,128)(2,1)S(1)}, u32[]{:S(2)}, u32[]{:S(2)}) collective-permute-start(bf16[128,1024]{1,0:T(8,128)(2,1)S(1)} %fusion.21), channel_id=1, source_target_pairs={{1,4},{3,6},{4,16},{5,20},{6,18},{7,22},{9,12},{11,14},{12,24},{13... | collective-permute-start | bytes 786440 | tf_op jit(solution)/shard_map/ppermute | solution.py:1024
  296.1 21.0 %collective-permute-start.50 = (bf16[128,1024]{1,0:T(8,128)(2,1)S(1)}, bf16[128,1024]{1,0:T(8,128)(2,1)S(1)}, u32[]{:S(2)}, u32[]{:S(2)}) collective-permute-start(bf16[128,1024]{1,0:T(8,128)(2,1)S(1)} %fusion.20), channel_id=1, source_target_pairs={{1,4},{3,6},{4,16},{5,20},{6,18},{7,22},{9,12},{11,14},{12,24},{13... | collective-permute-start | bytes 786440 | tf_op jit(solution)/shard_map/ppermute | solution.py:1024
  (110 other events, 869.7 us)

commit v3 on v2

--- a/solution.py
+++ b/solution.py
@@ -315,26 +315,6 @@
     return lax.ppermute(value, "head", FLIP)
 
 
-def scatter_group(near, away):
-    across_3 = flip_head(away[3])
-    third = near[3] + across_3.astype(FULL)
-    away_2 = after(away[2], across_3)
-    ends_third = lax.ppermute(third.astype(LOW), "blk", INWARD)
-    across_2 = flip_head(away_2)
-    second = near[2] + across_2.astype(FULL) + ends_third.astype(FULL)
-    second_low, away_1 = after((second.astype(LOW), away[1]), across_2)
-    ends_second = lax.ppermute(second_low, "blk", INWARD)
-    inner_second = lax.ppermute(second_low, "blk", INNER)
-    across_1 = flip_head(away_1)
-    third = third + ends_second.astype(FULL)
-    first = near[1] + across_1.astype(FULL) + inner_second.astype(FULL)
-    third_low, first_low, away_0 = after((third.astype(LOW), first.astype(LOW), away[0]))
-    inner_third = lax.ppermute(third_low, "blk", INNER)
-    last = lax.ppermute(first_low, "blk", PAIRS)
-    across_0 = flip_head(away_0)
-    return [near[0], across_0, inner_third, last]
-
-
 def gather_seq(own):
     across = lax.ppermute(own, "seq", ACROSS)
     return [own, lax.ppermute(own, "seq", CORE), across, lax.ppermute(across, "seq", CORE)]
@@ -369,7 +349,7 @@
         out_specs=[near] * (len(outs) - far_out) + [far] * far_out,
         scratch_shapes=scratch,
         compiler_params=pltpu.CompilerParams(vmem_limit_bytes=vmem * 2**20),
-        cost_estimate=pl.CostEstimate(flops=flops, bytes_accessed=moved, transcendentals=0),
+        cost_estimate=pl.CostEstimate(flops=flops // 2, bytes_accessed=moved, transcendentals=0),
     )(place, *args)
 
 
@@ -380,33 +360,56 @@
     return copies
 
 
-def put_columns(core, own_half, other_half, cols_ref):
-    half, own = own_half.shape[2:]
+def put_columns(place, parts, cols_ref):
+    step, width = parts.shape[3:]
     for at in range(8):
-        for side, half_ref in ((core, own_half), (1 - core, other_half)):
-            span = pl.ds(pl.multiple_of((2 * at + side) * half, half), half)
+        for part in range(4):
+            start = (4 * at + lax.bitwise_xor(place[1], part)) * step
+            span = pl.ds(pl.multiple_of(start, step), step)
             for which in range(3):
-                cols_ref[span, which * own : (which + 1) * own] = half_ref[at, which]
+                cols_ref[span, which * width : (which + 1) * width] = parts[part, at, which]
 
 
 def attend_kernel(place, *refs):
-    slots, refs = refs[:8], refs[8:]
-    own_half, other_half, bias_ref = refs[:3]
-    context_ref, kept, refs = refs[3], refs[4:10], refs[10:]
-    q_ref, k_ref, v_ref, mixed_ref, inverse_ref, weights_ref, cols_ref, sems = refs
-    rank, core = place[0], place[2]
-    half = own_half.shape[2]
+    bias_ref, refs = refs[0], refs[1:]
+    quarters, slots, refs = refs[:4], refs[4:12], refs[12:]
+    context_ref, kept, refs = refs[0], refs[1:8], refs[8:]
+    q_ref, k_ref, v_ref, mixed_ref, inverse_ref, cols_ref, weights_ref, tokens_ref = refs[:8]
+    parts, sems, slot_sems = refs[8], refs[9], refs[10]
+    rank = place[0]
     width = q_ref.shape[1]
-    rows = slots[0].shape[0]
-    put_columns(core, own_half, other_half, cols_ref)
+    rows = context_ref.shape[1]
+    step = parts.shape[3]
+    spans = [slice(pair * 2 * rows, (pair + 1) * 2 * rows) for pair in range(4)]
+    fetched = fetch(quarters, [parts.at[at] for at in range(4)], slot_sems)
+    held = [tokens_ref.at[at * rows : (at + 1) * rows] for at in range(8)]
+    fetched_slots = fetch(slots, held, slot_sems.at[4:12])
+    for copy in fetched:
+        copy.wait()
+    put_columns(place, parts, cols_ref)
     scale = HEAD_DIM ** (-0.5)
-    for pair in range(4):
-        span = slice(pair * 2 * rows, (pair + 1) * 2 * rows)
-        both = jnp.concatenate([slots[2 * pair][...], slots[2 * pair + 1][...]], axis=0)
-        projected = dot(both, cols_ref[...])
+    for pair, span in enumerate(spans):
+        fetched_slots[2 * pair].wait()
+        fetched_slots[2 * pair + 1].wait()
+        projected = dot(tokens_ref[span], cols_ref[...])
         q_ref[span] = ((projected[:, :width] + bias_ref[0]) * scale).astype(LOW)
         k_ref[span] = projected[:, width : 2 * width].astype(LOW)
         v_ref[span] = (projected[:, 2 * width :] + bias_ref[1]).astype(LOW)
+    copies = []
+    for at, ref in enumerate((q_ref, k_ref, v_ref, cols_ref)):
+        copies.append(pltpu.make_async_copy(ref, kept[at + 2 * (at == 3)], sems.at[12 + at]))
+    for copy in copies:
+        copy.start()
+
+    def block_copies(pair, span):
+        pairs = (
+            (mixed_ref.at[span], kept[3].at[span]),
+            (inverse_ref.at[span], kept[4].at[span]),
+            (weights_ref.at[:, span], kept[6].at[:, span]),
+        )
+        return [
+            pltpu.make_async_copy(*both, sems.at[pair + 4 * at]) for at, both in enumerate(pairs)
+        ]
 
     @pl.loop(0, 4)
     def _(pair):
@@ -424,28 +427,19 @@
         mixed = mixed_ref[span].astype(LOW)
         context_ref[first] = mixed[:rows]
         context_ref[lax.bitwise_xor(first, 1)] = mixed[rows:]
-        pltpu.make_async_copy(
-            weights_ref.at[:, span], kept[5].at[:, span], sems.at[pair]
-        ).start()
-
-    copies = []
-    for at, ref in enumerate((q_ref, k_ref, v_ref, mixed_ref, inverse_ref)):
-        copies.append(pltpu.make_async_copy(ref, kept[at], sems.at[4 + at]))
-    for pair in range(4):
-        span = slice(pair * 2 * rows, (pair + 1) * 2 * rows)
-        copies.append(
-            pltpu.make_async_copy(weights_ref.at[:, span], kept[5].at[:, span], sems.at[pair])
-        )
-    for copy in copies[:5]:
-        copy.start()
+        for copy in block_copies(pair, span):
+            copy.start()
+
+    for pair, span in enumerate(spans):
+        copies += block_copies(pair, span)
     for copy in copies:
         copy.wait()
 
 
-def attend_back_kernel(place, grad_ref, own_half, other_half, *refs):
+def attend_back_kernel(place, grad_ref, *refs):
     kept, refs = refs[:6], refs[6:]
-    out_ref, near_ref, away_ref, cols_ref, refs = refs[0], refs[1], refs[2], refs[3], refs[4:]
-    q_ref, k_ref, v_ref, mixed_ref, inverse_ref, weights_ref, dk_sum, dv_sum, sems = refs
+    out_ref, q_ref, k_ref, v_ref, mixed_ref, inverse_ref, weights_ref = refs[:7]
+    dk_sum, dv_sum, sems = refs[7:]
     rank = place[0]
     rows, width = grad_ref.shape[1:]
     scale = HEAD_DIM ** (-0.5)
@@ -494,15 +488,6 @@
         whose = lax.bitwise_xor(rank, at)
         out_ref[whose, :, width : 2 * width] = dk[at * rows : (at + 1) * rows]
         out_ref[whose, :, 2 * width :] = dv[at * rows : (at + 1) * rows]
-    put_columns(place[2], own_half, other_half, cols_ref)
-    for pair in (2, 3, 0, 1):
-        left = [out_ref[lax.bitwise_xor(rank, 2 * pair + at)] for at in range(2)]
-        term = dot_rows(jnp.concatenate(left, axis=0), cols_ref[...])
-        for at in range(2):
-            if pair < 2:
-                near_ref[2 * pair + at] = term[at * rows : (at + 1) * rows]
-            else:
-                away_ref[2 * pair + at - 4] = term[at * rows : (at + 1) * rows].astype(LOW)
 
 
 def normalize(values):
@@ -678,14 +663,17 @@
 
 def weight_grad_kernel(place, left_0, left_1, *refs):
     right, near_ref, away_ref = refs[:4], refs[4], refs[5]
+    held_0, held_1, first, second, sems = refs[6:]
     rows = near_ref.shape[1]
-    first = jnp.concatenate([right[0][...], right[1][...]], axis=0)
-    second = jnp.concatenate([right[2][...], right[3][...]], axis=0)
+    parts = [side.at[at * rows : (at + 1) * rows] for side in (first, second) for at in range(2)]
+    for copy in fetch((left_0, left_1) + tuple(right), [held_0, held_1] + parts, sems):
+        copy.wait()
     for stays in range(2):
         shard = place[6] if stays else 1 - place[6]
         for half in range(2):
             span = pl.ds(pl.multiple_of((2 * shard + half) * 2 * rows, 2 * rows), 2 * rows)
-            both = dot_cols(left_0[:, span], first) + dot_cols(left_1[:, span], second)
+            both = dot_cols(held_0[:, span], first[...])
+            both += dot_cols(held_1[:, span], second[...])
             for at in range(2):
                 part = both[at * rows : (at + 1) * rows]
                 slot = 2 * lax.bitwise_xor(place[3], at) + lax.bitwise_xor(place[7], half)
@@ -696,25 +684,32 @@
 
 
 def out_grad_kernel(place, *refs):
-    parts, grads, near_ref, away_ref = refs[:4], refs[4:8], refs[8], refs[9]
+    parts, grads, near_ref, away_ref, held, right, sems = refs[:4], refs[4:8], *refs[8:]
     step = near_ref.shape[1]
-    right = jnp.concatenate([grad[...] for grad in grads], axis=0)
+    rows = held.shape[2]
+    sides = [right.at[at * rows : (at + 1) * rows] for at in range(4)]
+    for copy in fetch(parts + grads, [held.at[at] for at in range(4)] + sides, sems):
+        copy.wait()
     for stays in range(2):
         which = place[3] if stays else 1 - place[3]
-        total = dot_cols(jnp.concatenate([part[which] for part in parts], axis=0), right)
+        left = jnp.concatenate([held[at, which] for at in range(4)], axis=0)
+        total = dot_cols(left, right[...])
         for at in range(4):
+            slot = lax.bitwise_xor(place[5], at)
             if stays:
-                near_ref[at] = total[at * step : (at + 1) * step]
+                near_ref[slot] = total[at * step : (at + 1) * step]
             else:
-                away_ref[at] = total[at * step : (at + 1) * step].astype(LOW)
+                away_ref[slot] = total[at * step : (at + 1) * step].astype(LOW)
 
 
 def qkv_grad_kernel(place, *refs):
-    slots, refs = refs[:8], refs[8:]
     grad_ref, top_ref, mid_ref, units_a, units_b = refs[:5]
-    near_ref, away_ref, total_ref, sums_ref = refs[5:]
+    slots, refs = refs[5:13], refs[13:]
+    near_ref, away_ref, total_ref, sums_ref, tokens_ref, sems = refs
+    rows = grad_ref.shape[1]
+    held = [tokens_ref.at[at * rows : (at + 1) * rows] for at in range(8)]
+    copies = fetch(slots, held, sems)
     rank, seq_at = place[0], place[1]
-    rows = slots[0].shape[0]
     width = sums_ref.shape[1]
     own = width // 8
     quarter = width // 4
@@ -722,8 +717,9 @@
     for pair in range(4):
         grads = [grad_ref[lax.bitwise_xor(rank, 2 * pair + at)] for at in range(2)]
         grads = jnp.concatenate(grads, axis=0)
-        both = jnp.concatenate([slots[2 * pair][...], slots[2 * pair + 1][...]], axis=0)
-        term = dot_cols(both, grads)
+        copies[2 * pair].wait()
+        copies[2 * pair + 1].wait()
+        term = dot_cols(tokens_ref[2 * pair * rows : 2 * (pair + 1) * rows], grads)
         col_sum += jnp.sum(grads.astype(FULL), axis=0, keepdims=True)
         if pair == 0:
             total_ref[...] = term
@@ -759,6 +755,28 @@
             near_ref[at // 2, quarter:] = sums
 
 
+def input_terms_kernel(place, across_ref, own_ref, *refs):
+    sources, refs = refs[:5], refs[5:]
+    near_ref, away_ref, cols_ref, beyond_ref, parts, sems = refs
+    copies = fetch(sources, [cols_ref] + [parts.at[at] for at in range(4)], sems)
+    rows = own_ref.shape[1]
+    for copy in copies:
+        copy.wait()
+    put_columns(place, parts, beyond_ref)
+    for slots in ((1, 3), (0, 2)):
+        whose = [lax.bitwise_xor(place[5], slot) for slot in slots]
+        left = jnp.concatenate([own_ref[place[4] * 4 + at] for at in whose], axis=0)
+        term = dot_rows(left, cols_ref[...])
+        left = jnp.concatenate([across_ref[at] for at in whose], axis=0)
+        term += dot_rows(left, beyond_ref[...])
+        for at, slot in enumerate(slots):
+            part = term[at * rows : (at + 1) * rows]
+            if slot % 2:
+                away_ref[at] = part.astype(LOW)
+            else:
+                near_ref[at] = part
+
+
 def qkv_send_kernel(place, near_ref, far_ref, out_ref):
     total = near_ref[...] + far_ref[...].astype(FULL)
     rows = total.shape[0] - 16
@@ -796,17 +814,16 @@
     unit_rows = fc_in.shape[0] // 4
     units = 8 * unit_rows
 
-    half = own // 2
-    qkv_half = lax.dynamic_slice_in_dim(w_qkv, core_at * half, half, 0)
-    qkv_half = qkv_half.reshape(half, 3, 8, own).transpose(2, 1, 0, 3).reshape(8, 3 * half, own)
+    quarter = own // 4
+    qkv_rows = lax.dynamic_slice_in_dim(w_qkv, seq_at * quarter, quarter, 0)
+    qkv_rows = qkv_rows.reshape(quarter, 3, 8, own).transpose(2, 1, 0, 3)
+    qkv_rows = qkv_rows.reshape(8, 3 * quarter, own)
     small = jnp.concatenate([vectors.T, fc_in_bias.reshape(-1, own)], axis=0)
     small = jnp.broadcast_to(small[None], (8, 12, own))
+    to_swap = jnp.concatenate([qkv_rows, small, jnp.zeros((8, 4, own), LOW)], axis=1)
     out_quarter = lax.dynamic_slice_in_dim(w_out, seq_at * 2 * own, 2 * own, 1)
     out_quarter = out_quarter.reshape(own, 2, own).transpose(1, 0, 2).reshape(1, 2 * own, own)
     out_quarter = jnp.broadcast_to(out_quarter, (8, 2 * own, own))
-    to_swap = jnp.concatenate(
-        [qkv_half, out_quarter, small, jnp.zeros((8, 4, own), LOW)], axis=1
-    )
     units_away = jnp.stack(
         [lax.dynamic_slice_in_dim(w, seq_at * unit_rows, unit_rows, 0) for w in (fc_in, fc_out)]
     )
@@ -820,41 +837,58 @@
     second_out = lax.ppermute(middle, "blk", OUTER)
     across_1 = flip_head(first)
     swapped = lax.all_to_all(to_swap, GROUP, 0, 0, tiled=True)
-    second_in, second_out, across_1 = after((second_in, second_out, across_1))
+    second_in, second_out, across_1, swapped, out_quarter = after(
+        (second_in, second_out, across_1, swapped, out_quarter)
+    )
+    out_quarter = lax.all_to_all(out_quarter, GROUP, 0, 0, tiled=True).reshape(8, 2, own, own)
     third = lax.ppermute(second_in, "blk", OUTER)
     second = jnp.where(inner, second_in, second_out)
     across_2 = flip_head(second)
-    third, across_2, swapped, units_away = after((third, across_2, swapped, units_away))
+    qkv_own = swapped[:, : 3 * quarter].reshape(8, 3, quarter, own)
+    qkv_across = lax.ppermute(qkv_own, "seq", ACROSS)
+    small = swapped[:, 3 * quarter : 3 * quarter + 12].astype(FULL)
+    vec = small[:, :8].transpose(1, 0, 2).reshape(8, width)
+    bias_all = small[:, 8:].reshape(32, 1, own)
+    third, across_2, qkv_own, qkv_across = after((third, across_2, qkv_own, qkv_across))
     third = jnp.where(inner, middle, third)
     across_3 = flip_head(third)
-    own_half = swapped[:, : 3 * half].reshape(8, 3, half, own)
-    other_half = lax.ppermute(own_half, "seq", CORE)
-    out_quarter = swapped[:, 3 * half : 3 * half + 2 * own].reshape(8, 2, own, own)
-    small = swapped[:, 3 * half + 2 * own : 3 * half + 2 * own + 12].astype(FULL)
-    vec = small[:, :8].transpose(1, 0, 2).reshape(8, width)
-    bias_all = small[:, 8:].reshape(32, 1, own)
-    across_3, other_half = after((across_3, other_half))
+    qkv_quarters = [qkv_own, lax.ppermute(qkv_own, "seq", CORE)]
+    qkv_quarters += [qkv_across, lax.ppermute(qkv_across, "seq", CORE)]
+    across_3, out_quarter, units_away, *qkv_quarters = after(
+        [across_3, out_quarter, units_away] + qkv_quarters
+    )
+    beyond = flip_head(qkv_quarters[0])
     slots = [tokens, first, second, third, across_0, across_1, across_2, across_3]
 
     units_two_on = lax.ppermute(units_away, "blk", TWO_ON)
-    out_slots = gather_seq(out_quarter)
-
     bias = vectors.T.reshape(8, 1, own)[4:6].astype(FULL)
     seq_rows = 8 * rows
     heads = own // HEAD_DIM
     kept_shapes = [((seq_rows, own), LOW)] * 3 + [((seq_rows, own), FULL)] * 2
+    kept_shapes.append(((width, 3 * own), LOW))
     kept_shapes.append(((heads, seq_rows, seq_rows), LOW))
     kept_scratch = [pltpu.VMEM(*shape) for shape in kept_shapes]
     context, *kept = call(
         attend_kernel,
         [shape_of((8, rows, own), LOW)] + [shape_of(*shape) for shape in kept_shapes],
-        place, *slots, own_half, other_half, bias,
-        scratch=kept_scratch + [pltpu.VMEM((width, 3 * own), LOW), pltpu.SemaphoreType.DMA((9,))],
+        place, bias, *qkv_quarters, *slots,
+        scratch=kept_scratch
+        + [pltpu.VMEM((seq_rows, width), LOW), pltpu.VMEM((4, 8, 3, quarter, own), LOW)]
+        + [pltpu.SemaphoreType.DMA((16,)), pltpu.SemaphoreType.DMA((12,))],
         flops=8 * 10**9,
-        far_out=6,
-    )
-    context, units_two_on = after((context, units_two_on), *out_slots[1:])
+        far_in=12,
+        far_out=7,
+        vmem=56,
+    )
+    out_across = lax.ppermute(out_quarter, "seq", ACROSS)
+    context, out_across, out_quarter = after((context, out_across, out_quarter))
+    out_slots = [out_quarter, lax.ppermute(out_quarter, "seq", CORE)]
+    out_slots += [out_across, lax.ppermute(out_across, "seq", CORE)]
     context = lax.all_to_all(context, GROUP, 0, 0, tiled=True)
+    beyond = after(beyond, *out_slots[1:])
+    beyond_across = lax.ppermute(beyond, "seq", ACROSS)
+    beyond_quarters = [beyond, lax.ppermute(beyond, "seq", CORE)]
+    beyond_quarters += [beyond_across, lax.ppermute(beyond_across, "seq", CORE)]
     ffn_weights = [fc_in, fc_out] + gather_seq(units_two_on)
     out_scratch = [pltpu.VMEM((8, own, width), LOW), pltpu.SemaphoreType.DMA((8,))]
 
@@ -915,10 +949,18 @@
         far = flip_head((far_part[0] + sent_far).astype(LOW))
         return near_part[0], lax.ppermute(near_part[1], "blk", PAIRS), far
 
-    def scatter_units(near, away):
-        near = near + lax.ppermute(away, "seq", CORE).astype(FULL)
-        near = near[:2] + lax.ppermute(near[2:].astype(LOW), "seq", ACROSS).astype(FULL)
-        return near[0] + lax.ppermute(near[1].astype(LOW), "blk", TWO_ON).astype(FULL)
+    weight_scratch = [pltpu.VMEM((2 * rows, units), LOW)] * 2
+    weight_scratch += [pltpu.VMEM((2 * rows, width), LOW)] * 2 + [pltpu.SemaphoreType.DMA((6,))]
+    terms = [shape_of((4, unit_rows, width), FULL), shape_of((4, unit_rows, width), LOW)]
+
+    def weight_grads(lefts, rights):
+        return call(
+            weight_grad_kernel, terms, place, *lefts, *rights,
+            scratch=weight_scratch, flops=2 * 10**9, far_in=6,
+        )
+
+    def add_low(near, sent):
+        return near + sent.astype(FULL)
 
     summed = scatter_parts(ffn_parts[0][2:4], ffn_parts[1][2:4])
     three_sums = shape_of((3, width), FULL)
@@ -946,17 +988,11 @@
             )
         )
     summed = scatter_parts(back_parts[0][1:3], back_parts[1][1:3])
-    terms = [shape_of((4, unit_rows, width), FULL), shape_of((4, unit_rows, width), LOW)]
-    out_near_grad, out_away_grad = call(
-        weight_grad_kernel, terms, place, ffn_parts[0][1], ffn_parts[1][1], *grad_ffn_slots,
-        flops=2 * 10**9,
-    )
-    grad_fc_out = scatter_units(out_near_grad, out_away_grad)
-    in_near_grad, in_away_grad = call(
-        weight_grad_kernel, terms, place, back_parts[0][0], back_parts[1][0], *middle_slots,
-        flops=2 * 10**9,
-    )
-    summed = after(summed, in_away_grad)
+    summed = after(summed, *beyond_quarters)
+    acts = after((ffn_parts[0][1], ffn_parts[1][1]), back_parts[1][0])
+    out_near_grad, out_away_grad = weight_grads(acts, grad_ffn_slots)
+    out_sent = lax.ppermute(out_away_grad, "seq", CORE)
+    summed = after(summed, out_sent)
     grad_one, grad_attn, grad_context, mid_sums = call(
         mix_back_kernel,
         [per_row, per_row_low, shape_of((8, rows, own), LOW), three_sums],
@@ -966,47 +1002,96 @@
         far_in=4,
     )
     grad_context = lax.all_to_all(grad_context, GROUP, 0, 0, tiled=True)
-    grad_fc_in = scatter_units(in_near_grad, in_away_grad)
-    grad_attn_slots = gather_cores(grad_attn)
-
-    grad_cols, near_terms, away_terms = call(
+    out_across = lax.ppermute(
+        add_low(out_near_grad[2:], out_sent[2:]).astype(LOW), "seq", ACROSS
+    )
+    in_near_grad, in_away_grad = weight_grads((back_parts[0][0], back_parts[1][0]), middle_slots)
+    in_sent = lax.ppermute(in_away_grad, "seq", CORE)
+    attn_across = flip_head(grad_attn)
+
+    def kept_here(near, sent, across, at):
+        return add_low(near[at] + sent[at].astype(FULL), across[at])
+
+    in_across = add_low(in_near_grad[2:], in_sent[2:]).astype(LOW)
+    out_last = kept_here(out_near_grad, out_sent, out_across, 1).astype(LOW)
+    grad_context, in_across, out_last, attn_across = after(
+        (grad_context, in_across, out_last, attn_across)
+    )
+    in_across = lax.ppermute(in_across, "seq", ACROSS)
+    out_last = lax.ppermute(out_last, "blk", TWO_ON)
+    grad_attn_slots = [grad_attn, lax.ppermute(grad_attn, "seq", CORE)]
+    grad_attn_slots += [attn_across, lax.ppermute(attn_across, "seq", CORE)]
+    (grad_cols,) = call(
         attend_back_kernel,
-        [
-            shape_of((8, rows, 3 * own), LOW),
-            shape_of((4, rows, width), FULL),
-            shape_of((4, rows, width), LOW),
-        ],
-        place, grad_context, own_half, other_half, *kept,
-        scratch=[pltpu.VMEM((width, 3 * own), LOW)]
-        + kept_scratch
+        [shape_of((8, rows, 3 * own), LOW)],
+        place, grad_context, *kept[:5], kept[6],
+        scratch=kept_scratch[:5]
+        + kept_scratch[6:]
         + [pltpu.VMEM((own, seq_rows), FULL)] * 2
         + [pltpu.SemaphoreType.DMA((9,))],
         flops=8 * 10**9,
         far_in=6,
-    )
-    terms = scatter_group(near_terms, away_terms)
-    input_grad = grad_one + terms[0]
-    for term in terms[1:]:
-        input_grad = input_grad + term.astype(FULL)
-
+        vmem=56,
+    )
+
+    cols_sent = lax.dynamic_slice_in_dim(grad_cols, (1 - head_at) * 4, 4, 0)
+    cols_sent = flip_head(cols_sent)
+    in_last = kept_here(in_near_grad, in_sent, in_across, 1).astype(LOW)
+    in_last = lax.ppermute(in_last, "blk", TWO_ON)
     payload_rows = 2 * own + 16
     near, away = call(
         qkv_grad_kernel,
         [shape_of((2, payload_rows, 3 * own), FULL), shape_of((2, payload_rows, 3 * own), LOW)],
-        place, *slots, grad_cols, top_sums, mid_sums, back_parts[0][3], back_parts[1][3],
-        scratch=[pltpu.VMEM((width, 3 * own), FULL), pltpu.VMEM((8, width), FULL)],
+        place, grad_cols, top_sums, mid_sums, back_parts[0][3], back_parts[1][3], *slots,
+        scratch=[pltpu.VMEM((width, 3 * own), FULL), pltpu.VMEM((8, width), FULL)]
+        + [pltpu.VMEM((seq_rows, width), LOW), pltpu.SemaphoreType.DMA((8,))],
         flops=2 * 10**9,
-    )
-    sent = lax.ppermute(away, "seq", CORE).astype(FULL)
-    far = lax.ppermute((near[1] + sent[1]).astype(LOW), "seq", ACROSS)
-
+        far_in=8,
+    )
+    sent = lax.ppermute(away, "seq", CORE)
+    near_terms, away_terms = call(
+        input_terms_kernel,
+        [
+            shape_of((2, rows, width), FULL),
+            shape_of((2, rows, width), LOW),
+        ],
+        place, cols_sent, grad_cols, kept[5], *beyond_quarters,
+        scratch=[pltpu.VMEM((width, 3 * own), LOW)] * 2
+        + [pltpu.VMEM((4, 8, 3, quarter, own), LOW), pltpu.SemaphoreType.DMA((5,))],
+        flops=2 * 10**9,
+        far_in=5,
+    )
+    sent_terms = lax.ppermute(away_terms, "blk", PAIRS)
     out_terms = [shape_of((4, own // 4, width), FULL), shape_of((4, own // 4, width), LOW)]
     near_rows, away_rows = call(
-        out_grad_kernel, out_terms, place, *parts, *grad_attn_slots, flops=10**9
-    )
-    near_rows = near_rows + lax.ppermute(away_rows, "seq", ACROSS).astype(FULL)
-    grad_w_out = lax.all_to_all(near_rows.astype(LOW), "blk", 0, 0, tiled=True)
-    grad_w_out = jnp.sum(grad_w_out.astype(FULL), axis=0)
+        out_grad_kernel, out_terms, place, *parts, *after(grad_attn_slots, away_terms),
+        scratch=[pltpu.VMEM((4, 2, rows, own), LOW), pltpu.VMEM((4 * rows, width), LOW)]
+        + [pltpu.SemaphoreType.DMA((8,))],
+        flops=10**9,
+        far_in=8,
+    )
+    sent_rows = lax.ppermute(away_rows, "seq", ACROSS)
+
+    last_terms = after(add_low(near_terms[1], sent_terms[1]).astype(LOW), in_last)
+    last_terms = lax.ppermute(last_terms, "blk", TWO_ON)
+    out_rows = add_low(near_rows, sent_rows)
+    sent_rows = lax.ppermute(out_rows.reshape(2, 2, -1, width)[:, 1].astype(LOW), "blk", PAIRS)
+    last_rows = lax.ppermute(add_low(out_rows[2], sent_rows[1]).astype(LOW), "blk", TWO_ON)
+    grad_w_out = add_low(add_low(out_rows[0], sent_rows[0]), last_rows)
+    far = lax.ppermute(add_low(near[1], sent[1]).astype(LOW), "seq", ACROSS)
+    unit_grads = jnp.stack(
+        [
+            add_low(kept_here(in_near_grad, in_sent, in_across, 0), in_last),
+            add_low(kept_here(out_near_grad, out_sent, out_across, 0), out_last),
+        ]
+    )
+    (payload,) = call(
+        qkv_send_kernel,
+        [shape_of((8, own // 4 + 16, 3 * own), LOW)],
+        place, add_low(near[0], sent[0]), far,
+    )
+    payload = lax.all_to_all(payload, GROUP, 0, 0, tiled=True)
+    input_grad = grad_one + add_low(add_low(near_terms[0], sent_terms[0]), last_terms)
 
     moves = []
     for across in range(2):
@@ -1020,18 +1105,9 @@
                             moves.append((start, stop))
     stays = (across_at == head_at) & (head_at == near_at)
 
-    def to_owner(grad):
-        moved = lax.ppermute(grad.astype(LOW), ("seq", "head", "blk"), moves).astype(FULL)
-        return jnp.where(stays, grad, moved)
-
-    grad_fc_out, grad_fc_in = to_owner(grad_fc_out), to_owner(grad_fc_in)
-
-    (payload,) = call(
-        qkv_send_kernel,
-        [shape_of((8, own // 4 + 16, 3 * own), LOW)],
-        place, near[0] + sent[0], far,
-    )
-    payload = lax.all_to_all(payload, GROUP, 0, 0, tiled=True)
+    moved = lax.ppermute(unit_grads.astype(LOW), ("seq", "head", "blk"), moves).astype(FULL)
+    grad_fc_in, grad_fc_out = jnp.where(stays, unit_grads, moved)
+
     grad_w_qkv, sums = call(
         qkv_last_kernel,
         [shape_of((own // 4, 3 * width), FULL), shape_of((16, 3 * own), FULL)],

time: 324 us -> 281 us (0.87)
  local copies, waits for them, and re-layouts: 45.6 us -> 15.2 us
  waiting for transfers between devices: 114 us -> 101 us
  Pallas kernels: 47.6 us -> 57.3 us
  starting transfers between devices: 85.6 us -> 78.7 us
    unnamed x167 -> x121, local copies, waits for them, and re-layouts: 34.8 us -> 8.4 us
    pallas_call x15 -> x16, Pallas kernels: 47.6 us -> 57.3 us  [call(): pl.pallas_call(kernel, out_shape=outs, in_specs=[pl.BlockSpec(memory_spac...]
    ppermute x1, waiting for transfers between devices: 9.11 us -> 0.01 us  [grouped_body(): third = lax.ppermute(second_in, 'blk', OUTER)]
    ppermute x1, waiting for transfers between devices: 15.2 us -> 6.15 us  [grouped_body(): second_out = lax.ppermute(middle, 'blk', OUTER)]
    ppermute x19 -> x25, starting transfers between devices: 29.3 us -> 22.9 us  [the longest x1 2.98 us: grouped_body(): lax.ppermute(unit_grads.astype(LOW), ('seq', 'head', 'blk'), moves)]
    ppermute x19 -> x25, waiting for transfers between devices: 27.1 us -> 33.3 us  [the longest x1 8.08 us: grouped_body(): lax.ppermute(add_low(out_rows[2], sent_rows[1]).astype(LOW), 'blk', TWO_ON)]
    another operation x0 -> x3, other arithmetic: none -> 4.63 us  [the longest x2 3.39 us: grouped_body(): jnp.stack([add_low(kept_here(in_near_grad, in_sent, in_across, 0), in_las...]
    slice x4 -> x1, local copies, waits for them, and re-layouts: 4.15 us -> 0.01 us  [grouped_body(): qkv_own = swapped[:, :3 * quarter].reshape(8, 3, quarter, own)]
  transfers between devices with their start and end apart: 60 -> 61, of which waited for: 25 -> 27; matrix products, arithmetic and copies ran while one was open for 11% -> 10% of each run, Pallas kernels for 13% -> 19%
where the time goes in v3:
time: 281 us; the launch traced here: 279 us
  waiting for transfers between devices  101 us (36%)
  starting transfers between devices  78.7 us (28%)
  Pallas kernels  57.3 us (20%)
  other arithmetic  25.3 us (9%)
  local copies, waits for them, and re-layouts  15.2 us (5%)
    pallas_call x16, Pallas kernels, call(): pl.pallas_call(kernel, out_shape=outs, in_specs=[pl.BlockSpec(memory_spac...  57.3 us
    ppermute x12, waiting for transfers between devices, flip_head(): return lax.ppermute(value, 'head', FLIP)  30.7 us
    ppermute x12, starting transfers between devices, flip_head(): return lax.ppermute(value, 'head', FLIP)  15.5 us
    ppermute x2, waiting for transfers between devices, gather_four(): return [own, beside, across, lax.ppermute(across, 'blk', PAIRS)]  12.1 us
    unnamed x121, local copies, waits for them, and re-layouts  8.4 us
    ppermute x1, waiting for transfers between devices, grouped_body(): lax.ppermute(add_low(out_rows[2], sent_rows[1]).astype(LOW), 'blk', TWO_ON)  8.08 us
    ppermute x1, waiting for transfers between devices, grouped_body(): far = lax.ppermute(add_low(near[1], sent[1]).astype(LOW), 'seq', ACROSS)  7.66 us
    all_to_all x1, starting transfers between devices, grouped_body(): swapped = lax.all_to_all(to_swap, GROUP, 0, 0, tiled=True)  6.34 us
  transfers between devices with their start and end apart: 61, of which 27 were waited for; matrix products, arithmetic and copies ran while one was open for 10% of the time, Pallas kernels for 19%

profile of v3, /device:TPU:2, one launch (start us, length us, event | category | flops | bytes accessed | tf_op | source)
XLA Modules:
  0.0 278.9 jit_solution(5090419642305717960)
XLA Ops:
  6.2 2.7 collective-permute-done.refs_6_
  11.7 6.3 %all-to-all-start = ((bf16[8,112,128]{2,1,0:T(8,128)(2,1)}), bf16[8,112,128]{2,1,0:T(8,128)(2,1)S(1)}, u32[]{:S(2)}, u32[]{:S(2)}) async-start(bf16[8,112,128]{2,1,0:T(8,128)(2,1)} %maximum_maximum_fusion), calls=%async_computation | async-start | bytes 458752 | tf_op jit(solution)/shard_map/all_to_all | solution.py:839
  24.0 6.1 %collective-permute-done.4 = bf16[128,1024]{1,0:T(8,128)(2,1)} collective-permute-done((bf16[128,1024]{1,0:T(8,128)(2,1)S(1)}, bf16[128,1024]{1,0:T(8,128)(2,1)}, u32[]{:S(2)}, u32[]{:S(2)}) %collective-permute-start.4) | collective-permute-done | bytes 262176 | tf_op jit(solution)/shard_map/ppermute | solution.py:837
  32.4 5.7 %all-to-all-start.1 = ((bf16[8,256,128]{2,1,0:T(8,128)(2,1)}), bf16[8,256,128]{2,1,0:T(8,128)(2,1)}, u32[]{:S(2)}, u32[]{:S(2)}) async-start(bf16[8,256,128]{2,1,0:T(8,128)(2,1)} %broadcast_in_dim.19), calls=%async_computation.1 | async-start | bytes 1048576 | tf_op jit(solution)/shard_map/all_to_all | solution.py:843
  41.9 5.1 %collective-permute-done.8.refs_3_ = bf16[8,3,32,128]{3,2,1,0:T(8,128)(2,1)S(1)} collective-permute-done((bf16[8,3,32,128]{3,2,1,0:T(8,128)(2,1)S(1)}, bf16[8,3,32,128]{3,2,1,0:T(8,128)(2,1)S(1)}, u32[]{:S(2)}, u32[]{:S(2)}) %collective-permute-start.8) | collective-permute-done | bytes 196640 | tf_op jit(solution)/shard_map/ppermute | solution.py:848
  54.0 2.8 collective-permute-done.9.refs_12_
  57.3 3.3 %collective-permute-start.16 = (bf16[2,128,1024]{2,1,0:T(8,128)(2,1)}, bf16[2,128,1024]{2,1,0:T(8,128)(2,1)S(1)}, u32[]{:S(2)}, u32[]{:S(2)}) collective-permute-start(bf16[2,128,1024]{2,1,0:T(8,128)(2,1)} %pad_maximum_fusion.1), channel_id=1, source_target_pairs={{0,2},{2,0},{1,3},{3,1},{4,6},{6,4},{5,7},{7,5},{8,10},{10,8},{9,1... | collective-permute-start | bytes 1572872 | tf_op jit(solution)/shard_map/ppermute | solution.py:863
  62.4 11.1 %shard_map.143 = (bf16[8,128,128]{2,1,0:T(8,128)(2,1)}, bf16[1024,128]{1,0:T(8,128)(2,1)}, bf16[1024,128]{1,0:T(8,128)(2,1)}, bf16[1024,128]{1,0:T(8,128)(2,1)},...) custom-call(s32[9]{0:T(128)} %stack.57.place, ...), custom_call_target="tpu_custom_call" | custom-call | flops 4000000000 | bytes 9962496 | tf_op jit(solution)/shard_map/pallas_call | solution.py:343
  74.1 4.0 %all-to-all-start.2 = ((bf16[8,128,128]{2,1,0:T(8,128)(2,1)}), bf16[8,128,128]{2,1,0:T(8,128)(2,1)S(1)}, u32[]{:S(2)}, u32[]{:S(2)}) async-start(bf16[8,128,128]{2,1,0:T(8,128)(2,1)} %get-tuple-element.120), calls=%async_computation.2 | async-start | bytes 524288 | tf_op jit(solution)/shard_map/all_to_all | solution.py:887
  83.1 4.9 %all-to-all-done.2.context_ref = bf16[8,128,128]{2,1,0:T(8,128)(2,1)S(1)} async-done(((bf16[8,128,128]{2,1,0:T(8,128)(2,1)}), bf16[8,128,128]{2,1,0:T(8,128)(2,1)S(1)}, u32[]{:S(2)}, u32[]{:S(2)}) %all-to-all-start.2) | async-done | bytes 262176 | tf_op jit(solution)/shard_map/all_to_all | solution.py:887
  89.1 2.8 %shard_map.144 = (f32[128,1024]{1,0:T(8,128)S(1)}, bf16[128,1024]{1,0:T(8,128)(2,1)S(1)}, f32[128,1024]{1,0:T(8,128)S(1)}, f32[128,1]{1,0:T(8,128)S(1)}) custom-call(s32[9]{0:T(128)S(1)} %copy-done.22, bf16[8,128,128]{2,1,0:T(8,128)(2,1)S(1)} %all-to-all-done.2.context_ref, bf16[128,1024]{1,0:T(8,128)(2,1)S(1)} %copy-done.24, ...), custom_call_target="tpu_custom_call" | custom-call | flops 1000000000 | bytes 3965440 | tf_op jit(solution)/shard_map/pallas_call | solution.py:343
  92.5 5.8 %collective-permute-done.21.first_ref.refs_2_ = bf16[128,1024]{1,0:T(8,128)(2,1)S(1)} collective-permute-done((bf16[128,1024]{1,0:T(8,128)(2,1)S(1)}, bf16[128,1024]{1,0:T(8,128)(2,1)S(1)}, u32[]{:S(2)}, u32[]{:S(2)}) %collective-permute-start.21) | collective-permute-done | bytes 262176 | tf_op jit(solution)/shard_map/ppermute | solution.py:315
  101.1 6.2 %collective-permute-done.22.second_ref.refs_3_ = bf16[128,1024]{1,0:T(8,128)(2,1)S(1)} collective-permute-done((bf16[128,1024]{1,0:T(8,128)(2,1)S(1)}, bf16[128,1024]{1,0:T(8,128)(2,1)S(1)}, u32[]{:S(2)}, u32[]{:S(2)}) %collective-permute-start.22) | collective-permute-done | bytes 262176 | tf_op jit(solution)/shard_map/ppermute | solution.py:326
  107.3 3.4 %shard_map.146 = (f32[256,1024]{1,0:T(8,128)S(1)}, bf16[256,1024]{1,0:T(8,128)(2,1)S(1)}, f32[128,1024]{1,0:T(8,128)S(1)}, bf16[128,1024]{1,0:T(8,128)(2,1)S(1)}) custom-call(s32[9]{0:T(128)S(1)} %copy-done.22, bf16[128,1024]{1,0:T(8,128)(2,1)S(1)} %collective-permute-done.21.first_ref.refs_2_, ...), custom_call_target="tpu_custom_call" | custom-call | flops 1500000000 | bytes 7094272 | tf_op jit(solution)/shard_map/pallas_call | solution.py:343
  111.7 3.4 %shard_map.145 = (f32[256,1024]{1,0:T(8,128)S(1)}, bf16[256,1024]{1,0:T(8,128)(2,1)S(1)}, f32[128,1024]{1,0:T(8,128)S(1)}, bf16[128,1024]{1,0:T(8,128)(2,1)S(1)}) custom-call(s32[9]{0:T(128)S(1)} %copy-done.22, bf16[128,1024]{1,0:T(8,128)(2,1)S(1)} %get-tuple-element.123.first_ref.refs_0_, bf16[128,1024]{1,0:T(8,128)(2,1)S(1)} %collective-permute-done.15.second_ref.refs_1_, ...), custom_call_target="tpu_custom_call" | custom-call | flops 1500000000 | bytes 7094272 | tf_op jit(solution)/shard_map/pallas_call | solution.py:343
  116.7 3.2 %collective-permute-done.23 = bf16[128,1024]{1,0:T(8,128)(2,1)S(1)} collective-permute-done((bf16[128,1024]{1,0:T(8,128)(2,1)S(1)}, bf16[128,1024]{1,0:T(8,128)(2,1)S(1)}, u32[]{:S(2)}, u32[]{:S(2)}) %collective-permute-start.23) | collective-permute-done | bytes 262176 | tf_op jit(solution)/shard_map/ppermute | solution.py:948
  122.7 5.9 %collective-permute-done.24.far_ref = bf16[128,1024]{1,0:T(8,128)(2,1)S(1)} collective-permute-done((bf16[128,1024]{1,0:T(8,128)(2,1)S(1)}, bf16[128,1024]{1,0:T(8,128)(2,1)S(1)}, u32[]{:S(2)}, u32[]{:S(2)}) %collective-permute-start.24) | collective-permute-done | bytes 262176 | tf_op jit(solution)/shard_map/ppermute | solution.py:315
  130.3 6.4 %collective-permute-done.27.first_ref.refs_2_ = bf16[128,1024]{1,0:T(8,128)(2,1)S(1)} collective-permute-done((bf16[128,1024]{1,0:T(8,128)(2,1)S(1)}, bf16[128,1024]{1,0:T(8,128)(2,1)S(1)}, u32[]{:S(2)}, u32[]{:S(2)}) %collective-permute-start.27) | collective-permute-done | bytes 262176 | tf_op jit(solution)/shard_map/ppermute | solution.py:315
  137.0 6.0 %collective-permute-done.28.second_ref.refs_3_ = bf16[128,1024]{1,0:T(8,128)(2,1)S(1)} collective-permute-done((bf16[128,1024]{1,0:T(8,128)(2,1)S(1)}, bf16[128,1024]{1,0:T(8,128)(2,1)S(1)}, u32[]{:S(2)}, u32[]{:S(2)}) %collective-permute-start.28) | collective-permute-done | bytes 262176 | tf_op jit(solution)/shard_map/ppermute | solution.py:326
  143.0 3.3 %shard_map.149 = (bf16[256,1024]{1,0:T(8,128)(2,1)S(1)}, f32[128,1024]{1,0:T(8,128)S(1)}, bf16[128,1024]{1,0:T(8,128)(2,1)S(1)}, f32[8,1,128]{2,1,0:T(1,128)S(1)}) custom-call(s32[9]{0:T(128)S(1)} %copy-done.22, bf16[128,1024]{1,0:T(8,128)(2,1)S(1)} %collective-permute-done.27.first_ref.refs_2_, ...), custom_call_target="tpu_custom_call" | custom-call | flops 1500000000 | bytes 7081984 | tf_op jit(solution)/shard_map/pallas_call | solution.py:343
  149.1 4.0 %shard_map.148 = (bf16[256,1024]{1,0:T(8,128)(2,1)S(1)}, f32[128,1024]{1,0:T(8,128)S(1)}, bf16[128,1024]{1,0:T(8,128)(2,1)}, f32[8,1,128]{2,1,0:T(1,128)S(1)}) custom-call(s32[9]{0:T(128)S(1)} %copy-done.22, bf16[128,1024]{1,0:T(8,128)(2,1)S(1)} %get-tuple-element.131.first_ref.refs_0_, bf16[128,1024]{1,0:T(8,128)(2,1)S(1)} %collective-permute-done.25.second_ref.refs_1_, ...), custom_call_target="tpu_custom_call" | custom-call | flops 1500000000 | bytes 7081984 | tf_op jit(solution)/shard_map/pallas_call | solution.py:343
  157.9 5.5 %collective-permute-done.33.refs_3_ = bf16[8,3,32,128]{3,2,1,0:T(8,128)(2,1)} collective-permute-done((bf16[8,3,32,128]{3,2,1,0:T(8,128)(2,1)S(1)}, bf16[8,3,32,128]{3,2,1,0:T(8,128)(2,1)}, u32[]{:S(2)}, u32[]{:S(2)}) %collective-permute-start.33) | collective-permute-done | bytes 196640 | tf_op jit(solution)/shard_map/ppermute | solution.py:889
  176.0 3.5 %shard_map.151 = (f32[128,1024]{1,0:T(8,128)S(1)}, bf16[128,1024]{1,0:T(8,128)(2,1)S(1)}, bf16[8,128,128]{2,1,0:T(8,128)(2,1)S(1)}, f32[3,1024]{1,0:T(4,128)S(1)}) custom-call(s32[9]{0:T(128)S(1)} %copy-done.22, f32[128,1024]{1,0:T(8,128)S(1)} %copy-done.10, bf16[128,1024]{1,0:T(8,128)(2,1)} %collective-permute-done.26.sent_ref, ...), custom_call_target="tpu_custom_call" | custom-call | flops 1000000000 | bytes 5288448 | tf_op jit(solution)/shard_map/pallas_call | solution.py:343
  181.7 3.5 %all-to-all-start.3 = ((bf16[8,128,128]{2,1,0:T(8,128)(2,1)}), bf16[8,128,128]{2,1,0:T(8,128)(2,1)S(1)}, u32[]{:S(2)}, u32[]{:S(2)}) async-start(bf16[8,128,128]{2,1,0:T(8,128)(2,1)} %copy-done.14), calls=%async_computation.3 | async-start | bytes 524288 | tf_op jit(solution)/shard_map/all_to_all | solution.py:1004
  191.2 4.7 %collective-permute-done.38.refs_6_ = bf16[128,1024]{1,0:T(8,128)(2,1)S(1)} collective-permute-done((bf16[128,1024]{1,0:T(8,128)(2,1)}, bf16[128,1024]{1,0:T(8,128)(2,1)S(1)}, u32[]{:S(2)}, u32[]{:S(2)}) %collective-permute-start.38) | collective-permute-done | bytes 262176 | tf_op jit(solution)/shard_map/ppermute | solution.py:315
  198.5 8.3 %shard_map.153.own_ref.refs_0_ = bf16[8,128,384]{2,1,0:T(8,128)(2,1)} custom-call(s32[9]{0:T(128)} %stack.57.place, bf16[8,128,128]{2,1,0:T(8,128)(2,1)} %copy-done.51, bf16[1024,128]{1,0:T(8,128)(2,1)} %get-tuple-element.162.refs_0_, bf16[1024,128]{1,0:T(8,128)(2,1)} %get-tuple-element.163.refs_1_, bf16[1024,128]{1,0:T(8,128)(2,1)} %get-tuple-element.164.refs_2_, ...), custom_call_target="tpu_custom_call" | custom-call | flops 4000000000 | bytes 7077888 | tf_op jit(solution)/shard_map/pallas_call | solution.py:343
  218.9 3.9 %shard_map.154 = (f32[2,128,1024]{2,1,0:T(8,128)S(1)}, bf16[2,128,1024]{2,1,0:T(8,128)(2,1)}) custom-call(s32[9]{0:T(128)S(1)} %copy-done.23, bf16[4,128,384]{2,1,0:T(8,128)(2,1)S(1)} %collective-permute-done.39.across_ref, bf16[8,128,384]{2,1,0:T(8,128)(2,1)S(1)} %copy-done.21, bf16[1024,384]{1,0:T(8,128)(2,1)S(1)} %copy-done.42, ...), custom_call_target="tpu_custom_call" | custom-call | flops 1000000000 | bytes 4325376 | tf_op jit(solution)/shard_map/pallas_call | solution.py:343
  231.6 7.7 %collective-permute-done.45.far_ref = bf16[272,384]{1,0:T(8,128)(2,1)S(1)} collective-permute-done((bf16[272,384]{1,0:T(8,128)(2,1)S(1)}, bf16[272,384]{1,0:T(8,128)(2,1)S(1)}, u32[]{:S(2)}, u32[]{:S(2)}) %collective-permute-start.45) | collective-permute-done | bytes 208928 | tf_op jit(solution)/shard_map/ppermute | solution.py:1081
  240.5 3.4 %all-to-all-start.4 = ((bf16[8,48,384]{2,1,0:T(8,128)(2,1)}), bf16[8,48,384]{2,1,0:T(8,128)(2,1)S(1)}, u32[]{:S(2)}, u32[]{:S(2)}) async-start(bf16[8,48,384]{2,1,0:T(8,128)(2,1)} %shard_map.156), calls=%async_computation.4 | async-start | bytes 589824 | tf_op jit(solution)/shard_map/all_to_all | solution.py:1093
  249.4 3.0 %collective-permute-start.55 = (bf16[2,128,1024]{2,1,0:T(8,128)(2,1)}, bf16[2,128,1024]{2,1,0:T(8,128)(2,1)}, u32[]{:S(2)}, u32[]{:S(2)}) collective-permute-start(bf16[2,128,1024]{2,1,0:T(8,128)(2,1)} %fusion.8), channel_id=1, source_target_pairs={{1,4},{3,6},{4,16},{5,20},{6,18},{7,22},{9,12},{11,14},{12,24},{13... | collective-permute-start | bytes 1572872 | tf_op jit(solution)/shard_map/ppermute | solution.py:1108
  258.3 8.1 %collective-permute-done.53 = bf16[32,1024]{1,0:T(8,128)(2,1)S(1)} collective-permute-done((bf16[32,1024]{1,0:T(8,128)(2,1)S(1)}, bf16[32,1024]{1,0:T(8,128)(2,1)S(1)}, u32[]{:S(2)}, u32[]{:S(2)}) %collective-permute-start.53) | collective-permute-done | bytes 65568 | tf_op jit(solution)/shard_map/ppermute | solution.py:1079
  273.6 3.0 %collective-permute-done.55 = bf16[2,128,1024]{2,1,0:T(8,128)(2,1)} collective-permute-done((bf16[2,128,1024]{2,1,0:T(8,128)(2,1)}, bf16[2,128,1024]{2,1,0:T(8,128)(2,1)}, u32[]{:S(2)}, u32[]{:S(2)}) %collective-permute-start.55) | collective-permute-done | bytes 524320 | tf_op jit(solution)/shard_map/ppermute | solution.py:1108
  (270 shorter events, 120.4 us)
Async XLA Ops:
  11.7 18.5 %all-to-all-start = ((bf16[8,112,128]{2,1,0:T(8,128)(2,1)}), bf16[8,112,128]{2,1,0:T(8,128)(2,1)S(1)}, u32[]{:S(2)}, u32[]{:S(2)}) async-start(bf16[8,112,128]{2,1,0:T(8,128)(2,1)} %maximum_maximum_fusion), calls=%async_computation | async-start | bytes 458752 | tf_op jit(solution)/shard_map/all_to_all | solution.py:839
  19.6 10.6 %collective-permute-start.4 = (bf16[128,1024]{1,0:T(8,128)(2,1)S(1)}, bf16[128,1024]{1,0:T(8,128)(2,1)}, u32[]{:S(2)}, u32[]{:S(2)}) collective-permute-start(bf16[128,1024]{1,0:T(8,128)(2,1)S(1)} %collective-permute-done.1), channel_id=1, source_target_pairs={{1,0},{2,3},{5,4},{6,7},{9,8},{10,11},{13,12},{14,15},{17,16},{18,... | collective-permute-start | bytes 786440 | tf_op jit(solution)/shard_map/ppermute | solution.py:837
  31.1 15.9 %collective-permute-start.6 = (bf16[128,1024]{1,0:T(8,128)(2,1)}, bf16[128,1024]{1,0:T(8,128)(2,1)}, u32[]{:S(2)}, u32[]{:S(2)}) collective-permute-start(bf16[128,1024]{1,0:T(8,128)(2,1)} %collective-permute-done.3), channel_id=1, source_target_pairs={{1,0},{2,3},{5,4},{6,7},{9,8},{10,11},{13,12},{14,15},{17,16},{18,... | collective-permute-start | bytes 786440 | tf_op jit(solution)/shard_map/ppermute | solution.py:844
  32.4 24.3 %all-to-all-start.1 = ((bf16[8,256,128]{2,1,0:T(8,128)(2,1)}), bf16[8,256,128]{2,1,0:T(8,128)(2,1)}, u32[]{:S(2)}, u32[]{:S(2)}) async-start(bf16[8,256,128]{2,1,0:T(8,128)(2,1)} %broadcast_in_dim.19), calls=%async_computation.1 | async-start | bytes 1048576 | tf_op jit(solution)/shard_map/all_to_all | solution.py:843
  56.7 16.8 %collective-permute-start.12 = (bf16[8,2,128,128]{3,2,1,0:T(8,128)(2,1)}, bf16[8,2,128,128]{3,2,1,0:T(8,128)(2,1)}, u32[]{:S(2)}, u32[]{:S(2)}) collective-permute-start(bf16[8,2,128,128]{3,2,1,0:T(8,128)(2,1)} %bitcast.18.refs_0_), channel_id=1, source_target_pairs={{0,16},{8,24},{16,0},{24,8},{1,17},{9,25},{17,1},{25,9},{2,18},{10... | collective-permute-start | bytes 1572872 | tf_op jit(solution)/shard_map/ppermute | solution.py:883
  57.3 23.5 %collective-permute-start.16 = (bf16[2,128,1024]{2,1,0:T(8,128)(2,1)}, bf16[2,128,1024]{2,1,0:T(8,128)(2,1)S(1)}, u32[]{:S(2)}, u32[]{:S(2)}) collective-permute-start(bf16[2,128,1024]{2,1,0:T(8,128)(2,1)} %pad_maximum_fusion.1), channel_id=1, source_target_pairs={{0,2},{2,0},{1,3},{3,1},{4,6},{6,4},{5,7},{7,5},{8,10},{10,8},{9,1... | collective-permute-start | bytes 1572872 | tf_op jit(solution)/shard_map/ppermute | solution.py:863
  73.5 14.6 %collective-permute-start.13 = (bf16[8,2,128,128]{3,2,1,0:T(8,128)(2,1)}, bf16[8,2,128,128]{3,2,1,0:T(8,128)(2,1)}, u32[]{:S(2)}, u32[]{:S(2)}) collective-permute-start(bf16[8,2,128,128]{3,2,1,0:T(8,128)(2,1)} %bitcast.18.refs_0_), channel_id=1, source_target_pairs={{0,8},{8,0},{16,24},{24,16},{1,9},{9,1},{17,25},{25,17},{2,10},{10... | collective-permute-start | bytes 1572872 | tf_op jit(solution)/shard_map/ppermute | solution.py:885
  73.6 14.5 %collective-permute-start.14 = (bf16[8,2,128,128]{3,2,1,0:T(8,128)(2,1)}, bf16[8,2,128,128]{3,2,1,0:T(8,128)(2,1)}, u32[]{:S(2)}, u32[]{:S(2)}) collective-permute-start(bf16[8,2,128,128]{3,2,1,0:T(8,128)(2,1)} %collective-permute-done.12.refs_2_), channel_id=1, source_target_pairs={{0,8},{8,0},{16,24},{24,16},{1,9},{9,1},{17,25},{25,17},{2,10},{10... | collective-permute-start | bytes 1572872 | tf_op jit(solution)/shard_map/ppermute | solution.py:886
  74.1 14.0 %all-to-all-start.2 = ((bf16[8,128,128]{2,1,0:T(8,128)(2,1)}), bf16[8,128,128]{2,1,0:T(8,128)(2,1)S(1)}, u32[]{:S(2)}, u32[]{:S(2)}) async-start(bf16[8,128,128]{2,1,0:T(8,128)(2,1)} %get-tuple-element.120), calls=%async_computation.2 | async-start | bytes 524288 | tf_op jit(solution)/shard_map/all_to_all | solution.py:887
  80.8 11.7 %collective-permute-start.18 = (bf16[2,128,1024]{2,1,0:T(8,128)(2,1)S(1)}, bf16[2,128,1024]{2,1,0:T(8,128)(2,1)S(1)}, u32[]{:S(2)}, u32[]{:S(2)}) collective-permute-start(bf16[2,128,1024]{2,1,0:T(8,128)(2,1)S(1)} %collective-permute-done.16.refs_3_.refs_2_), channel_id=1, source_target_pairs={{0,16},{8,24},{16,0},{24,8},{1,17},{9,25},{17,1},{25,9},{2,18},{10... | collective-permute-start | bytes 1572872 | tf_op jit(solution)/shard_map/ppermute | solution.py:319
  83.1 18.1 %collective-permute-start.17 = (bf16[2,128,1024]{2,1,0:T(8,128)(2,1)S(1)}, bf16[2,128,1024]{2,1,0:T(8,128)(2,1)}, u32[]{:S(2)}, u32[]{:S(2)}) collective-permute-start(bf16[2,128,1024]{2,1,0:T(8,128)(2,1)S(1)} %collective-permute-done.16.refs_3_.refs_2_), channel_id=1, source_target_pairs={{0,8},{8,0},{16,24},{24,16},{1,9},{9,1},{17,25},{25,17},{2,10},{10... | collective-permute-start | bytes 1572872 | tf_op jit(solution)/shard_map/ppermute | solution.py:320
  92.5 14.8 %collective-permute-start.19 = (bf16[2,128,1024]{2,1,0:T(8,128)(2,1)S(1)}, bf16[2,128,1024]{2,1,0:T(8,128)(2,1)S(1)}, u32[]{:S(2)}, u32[]{:S(2)}) collective-permute-start(bf16[2,128,1024]{2,1,0:T(8,128)(2,1)S(1)} %collective-permute-done.18.refs_5_.refs_4_), channel_id=1, source_target_pairs={{0,8},{8,0},{16,24},{24,16},{1,9},{9,1},{17,25},{25,17},{2,10},{10... | collective-permute-start | bytes 1572872 | tf_op jit(solution)/shard_map/ppermute | solution.py:320
  99.7 12.0 %collective-permute-start.15 = (bf16[128,1024]{1,0:T(8,128)(2,1)S(1)}, bf16[128,1024]{1,0:T(8,128)(2,1)S(1)}, u32[]{:S(2)}, u32[]{:S(2)}) collective-permute-start(bf16[128,1024]{1,0:T(8,128)(2,1)S(1)} %get-tuple-element.123.first_ref.refs_0_), channel_id=1, source_target_pairs={{0,1},{1,0},{2,3},{3,2},{4,5},{5,4},{6,7},{7,6},{8,9},{9,8},{10,11... | collective-permute-start | bytes 786440 | tf_op jit(solution)/shard_map/ppermute | solution.py:325
  130.3 16.1 %collective-permute-start.25 = (bf16[128,1024]{1,0:T(8,128)(2,1)S(1)}, bf16[128,1024]{1,0:T(8,128)(2,1)S(1)}, u32[]{:S(2)}, u32[]{:S(2)}) collective-permute-start(bf16[128,1024]{1,0:T(8,128)(2,1)S(1)} %get-tuple-element.131.first_ref.refs_0_), channel_id=1, source_target_pairs={{0,1},{1,0},{2,3},{3,2},{4,5},{5,4},{6,7},{7,6},{8,9},{9,8},{10,11... | collective-permute-start | bytes 786440 | tf_op jit(solution)/shard_map/ppermute | solution.py:325
  148.5 17.4 %collective-permute-start.35 = (bf16[4,128,1024]{2,1,0:T(8,128)(2,1)S(1)}, bf16[4,128,1024]{2,1,0:T(8,128)(2,1)S(1)}, u32[]{:S(2)}, u32[]{:S(2)}) collective-permute-start(bf16[4,128,1024]{2,1,0:T(8,128)(2,1)S(1)} %get-tuple-element.147), channel_id=1, source_target_pairs={{0,8},{8,0},{16,24},{24,16},{1,9},{9,1},{17,25},{25,17},{2,10},{10... | collective-permute-start | bytes 3145736 | tf_op jit(solution)/shard_map/ppermute | solution.py:994
  155.9 31.4 %collective-permute-start.36 = (bf16[4,128,1024]{2,1,0:T(8,128)(2,1)}, bf16[4,128,1024]{2,1,0:T(8,128)(2,1)}, u32[]{:S(2)}, u32[]{:S(2)}) collective-permute-start(bf16[4,128,1024]{2,1,0:T(8,128)(2,1)} %get-tuple-element.158), channel_id=1, source_target_pairs={{0,8},{8,0},{16,24},{24,16},{1,9},{9,1},{17,25},{25,17},{2,10},{10... | collective-permute-start | bytes 3145736 | tf_op jit(solution)/shard_map/ppermute | solution.py:1009
  157.9 11.0 %collective-permute-start.32 = (bf16[8,3,32,128]{3,2,1,0:T(8,128)(2,1)S(1)}, bf16[8,3,32,128]{3,2,1,0:T(8,128)(2,1)S(1)}, u32[]{:S(2)}, u32[]{:S(2)}) collective-permute-start(bf16[8,3,32,128]{3,2,1,0:T(8,128)(2,1)S(1)} %collective-permute-done.31.refs_1_), channel_id=1, source_target_pairs={{0,8},{8,0},{16,24},{24,16},{1,9},{9,1},{17,25},{25,17},{2,10},{10... | collective-permute-start | bytes 589832 | tf_op jit(solution)/shard_map/ppermute | solution.py:890
  169.6 19.6 %collective-permute-start.37 = (bf16[2,128,1024]{2,1,0:T(8,128)(2,1)}, bf16[2,128,1024]{2,1,0:T(8,128)(2,1)}, u32[]{:S(2)}, u32[]{:S(2)}) collective-permute-start(bf16[2,128,1024]{2,1,0:T(8,128)(2,1)} %add_convert_fusion), channel_id=1, source_target_pairs={{0,16},{8,24},{16,0},{24,8},{1,17},{9,25},{17,1},{25,9},{2,18},{10... | collective-permute-start | bytes 1572872 | tf_op jit(solution)/shard_map/ppermute | solution.py:1005
  181.7 14.3 %all-to-all-start.3 = ((bf16[8,128,128]{2,1,0:T(8,128)(2,1)}), bf16[8,128,128]{2,1,0:T(8,128)(2,1)S(1)}, u32[]{:S(2)}, u32[]{:S(2)}) async-start(bf16[8,128,128]{2,1,0:T(8,128)(2,1)} %copy-done.14), calls=%async_computation.3 | async-start | bytes 524288 | tf_op jit(solution)/shard_map/all_to_all | solution.py:1004
  185.2 10.8 %collective-permute-start.38 = (bf16[128,1024]{1,0:T(8,128)(2,1)}, bf16[128,1024]{1,0:T(8,128)(2,1)S(1)}, u32[]{:S(2)}, u32[]{:S(2)}) collective-permute-start(bf16[128,1024]{1,0:T(8,128)(2,1)} %copy-done.34), channel_id=1, source_target_pairs={{0,4},{4,0},{1,5},{5,1},{2,6},{6,2},{3,7},{7,3},{8,12},{12,8},{9,1... | collective-permute-start | bytes 786440 | tf_op jit(solution)/shard_map/ppermute | solution.py:315
  196.0 18.9 %collective-permute-start.54 = (bf16[128,1024]{1,0:T(8,128)(2,1)}, bf16[128,1024]{1,0:T(8,128)(2,1)S(1)}, u32[]{:S(2)}, u32[]{:S(2)}) collective-permute-start(bf16[128,1024]{1,0:T(8,128)(2,1)} %fusion.12), channel_id=1, source_target_pairs={{0,2},{2,0},{1,3},{3,1},{4,6},{6,4},{5,7},{7,5},{8,10},{10,8},{9,1... | collective-permute-start | bytes 786440 | tf_op jit(solution)/shard_map/ppermute | solution.py:1021
  207.9 10.6 %collective-permute-start.39 = (bf16[4,128,384]{2,1,0:T(8,128)(2,1)S(1)}, bf16[4,128,384]{2,1,0:T(8,128)(2,1)S(1)}, u32[]{:S(2)}, u32[]{:S(2)}) collective-permute-start(bf16[4,128,384]{2,1,0:T(8,128)(2,1)S(1)} %constant_dynamic-slice_fusion), channel_id=1, source_target_pairs={{0,4},{4,0},{1,5},{5,1},{2,6},{6,2},{3,7},{7,3},{8,12},{12,8},{9,1... | collective-permute-start | bytes 1179656 | tf_op jit(solution)/shard_map/ppermute | solution.py:315
  212.7 14.7 %collective-permute-start.44 = (bf16[2,272,384]{2,1,0:T(8,128)(2,1)S(1)}, bf16[2,272,384]{2,1,0:T(8,128)(2,1)S(1)}, u32[]{:S(2)}, u32[]{:S(2)}) collective-permute-start(bf16[2,272,384]{2,1,0:T(8,128)(2,1)S(1)} %get-tuple-element.178), channel_id=1, source_target_pairs={{0,8},{8,0},{16,24},{24,16},{1,9},{9,1},{17,25},{25,17},{2,10},{10... | collective-permute-start | bytes 1253384 | tf_op jit(solution)/shard_map/ppermute | solution.py:1051
  213.3 14.9 %collective-permute-start.41 = (bf16[2,128,1024]{2,1,0:T(8,128)(2,1)S(1)}, bf16[2,128,1024]{2,1,0:T(8,128)(2,1)S(1)}, u32[]{:S(2)}, u32[]{:S(2)}) collective-permute-start(bf16[2,128,1024]{2,1,0:T(8,128)(2,1)S(1)} %copy-done.50), channel_id=1, source_target_pairs={{0,16},{8,24},{16,0},{24,8},{1,17},{9,25},{17,1},{25,9},{2,18},{10... | collective-permute-start | bytes 1572872 | tf_op jit(solution)/shard_map/ppermute | solution.py:1020
  222.8 33.4 %collective-permute-start.40 = (bf16[2,128,1024]{2,1,0:T(8,128)(2,1)}, bf16[2,128,1024]{2,1,0:T(8,128)(2,1)}, u32[]{:S(2)}, u32[]{:S(2)}) collective-permute-start(bf16[2,128,1024]{2,1,0:T(8,128)(2,1)} %get-tuple-element.170), channel_id=1, source_target_pairs={{0,1},{1,0},{2,3},{3,2},{4,5},{5,4},{6,7},{7,6},{8,9},{9,8},{10,11... | collective-permute-start | bytes 1572872 | tf_op jit(solution)/shard_map/ppermute | solution.py:1064
  226.0 17.9 %collective-permute-start.51 = (bf16[4,32,1024]{2,1,0:T(8,128)(2,1)}, bf16[4,32,1024]{2,1,0:T(8,128)(2,1)}, u32[]{:S(2)}, u32[]{:S(2)}) collective-permute-start(bf16[4,32,1024]{2,1,0:T(8,128)(2,1)} %get-tuple-element.189), channel_id=1, source_target_pairs={{0,16},{8,24},{16,0},{24,8},{1,17},{9,25},{17,1},{25,9},{2,18},{10... | collective-permute-start | bytes 786440 | tf_op jit(solution)/shard_map/ppermute | solution.py:1073
  227.5 11.8 %collective-permute-start.45 = (bf16[272,384]{1,0:T(8,128)(2,1)S(1)}, bf16[272,384]{1,0:T(8,128)(2,1)S(1)}, u32[]{:S(2)}, u32[]{:S(2)}) collective-permute-start(bf16[272,384]{1,0:T(8,128)(2,1)S(1)} %get-tuple-element.194), channel_id=1, source_target_pairs={{0,16},{8,24},{16,0},{24,8},{1,17},{9,25},{17,1},{25,9},{2,18},{10... | collective-permute-start | bytes 626696 | tf_op jit(solution)/shard_map/ppermute | solution.py:1081
  230.2 17.0 %collective-permute-start.42 = (bf16[128,1024]{1,0:T(8,128)(2,1)}, bf16[128,1024]{1,0:T(8,128)(2,1)}, u32[]{:S(2)}, u32[]{:S(2)}) collective-permute-start(bf16[128,1024]{1,0:T(8,128)(2,1)} %fusion.14), channel_id=1, source_target_pairs={{0,2},{2,0},{1,3},{3,1},{4,6},{6,4},{5,7},{7,5},{8,10},{10,8},{9,1... | collective-permute-start | bytes 786440 | tf_op jit(solution)/shard_map/ppermute | solution.py:1040
  240.5 26.5 %all-to-all-start.4 = ((bf16[8,48,384]{2,1,0:T(8,128)(2,1)}), bf16[8,48,384]{2,1,0:T(8,128)(2,1)S(1)}, u32[]{:S(2)}, u32[]{:S(2)}) async-start(bf16[8,48,384]{2,1,0:T(8,128)(2,1)} %shard_map.156), calls=%async_computation.4 | async-start | bytes 589824 | tf_op jit(solution)/shard_map/all_to_all | solution.py:1093
  249.4 27.3 %collective-permute-start.55 = (bf16[2,128,1024]{2,1,0:T(8,128)(2,1)}, bf16[2,128,1024]{2,1,0:T(8,128)(2,1)}, u32[]{:S(2)}, u32[]{:S(2)}) collective-permute-start(bf16[2,128,1024]{2,1,0:T(8,128)(2,1)} %fusion.8), channel_id=1, source_target_pairs={{1,4},{3,6},{4,16},{5,20},{6,18},{7,22},{9,12},{11,14},{12,24},{13... | collective-permute-start | bytes 1572872 | tf_op jit(solution)/shard_map/ppermute | solution.py:1108
  254.2 12.2 %collective-permute-start.53 = (bf16[32,1024]{1,0:T(8,128)(2,1)S(1)}, bf16[32,1024]{1,0:T(8,128)(2,1)S(1)}, u32[]{:S(2)}, u32[]{:S(2)}) collective-permute-start(bf16[32,1024]{1,0:T(8,128)(2,1)S(1)} %fusion.19), channel_id=1, source_target_pairs={{0,2},{2,0},{1,3},{3,1},{4,6},{6,4},{5,7},{7,5},{8,10},{10,8},{9,1... | collective-permute-start | bytes 196616 | tf_op jit(solution)/shard_map/ppermute | solution.py:1079
  257.2 13.7 %collective-permute-start.43 = (bf16[128,1024]{1,0:T(8,128)(2,1)S(1)}, bf16[128,1024]{1,0:T(8,128)(2,1)S(1)}, u32[]{:S(2)}, u32[]{:S(2)}) collective-permute-start(bf16[128,1024]{1,0:T(8,128)(2,1)S(1)} %fusion.13), channel_id=1, source_target_pairs={{0,2},{2,0},{1,3},{3,1},{4,6},{6,4},{5,7},{7,5},{8,10},{10,8},{9,1... | collective-permute-start | bytes 786440 | tf_op jit(solution)/shard_map/ppermute | solution.py:1076
  (88 other events, 840.8 us)

commit v4 on v3

--- a/solution.py
+++ b/solution.py
@@ -963,6 +963,7 @@
         return near + sent.astype(FULL)
 
     summed = scatter_parts(ffn_parts[0][2:4], ffn_parts[1][2:4])
+    summed = after(summed, *beyond_quarters)
     three_sums = shape_of((3, width), FULL)
     layer_output, grad_two, grad_ffn, top_sums = call(
         top_kernel,
@@ -988,7 +989,6 @@
             )
         )
     summed = scatter_parts(back_parts[0][1:3], back_parts[1][1:3])
-    summed = after(summed, *beyond_quarters)
     acts = after((ffn_parts[0][1], ffn_parts[1][1]), back_parts[1][0])
     out_near_grad, out_away_grad = weight_grads(acts, grad_ffn_slots)
     out_sent = lax.ppermute(out_away_grad, "seq", CORE)

time: 281 us -> 275 us (0.979)
  starting transfers between devices: 78.7 us -> 73.3 us
    ppermute x12, waiting for transfers between devices: 30.7 us -> 21.6 us  [flip_head(): return lax.ppermute(value, 'head', FLIP)]
    ppermute x2, waiting for transfers between devices: 4.43 us -> 10.3 us  [scatter_parts(): sent_far = lax.ppermute(far_part[1], 'blk', PAIRS).astype(FULL)]
    ppermute x1, waiting for transfers between devices: 5.54 us -> 0.01 us  [grouped_body(): beyond_across = lax.ppermute(beyond, 'seq', ACROSS)]
    ppermute x1, waiting for transfers between devices: 0.01 us -> 3.2 us  [grouped_body(): third = lax.ppermute(second_in, 'blk', OUTER)]
    all_to_all x1, starting transfers between devices: 6.34 us -> 3.4 us  [grouped_body(): swapped = lax.all_to_all(to_swap, GROUP, 0, 0, tiled=True)]
    ppermute x1, waiting for transfers between devices: 0.01 us -> 2.85 us  [gather_seq(): across = lax.ppermute(own, 'seq', ACROSS)]
    unnamed x121 -> x127, local copies, waits for them, and re-layouts: 8.4 us -> 8.49 us
  transfers between devices with their start and end apart: 61 -> 61, of which waited for: 27 -> 31; matrix products, arithmetic and copies ran while one was open for 10% -> 11% of each run, Pallas kernels for 19% -> 19%
where the time goes in v4:
time: 275 us; the launch traced here: 274 us
  waiting for transfers between devices  101 us (37%)
  starting transfers between devices  73.3 us (27%)
  Pallas kernels  56.9 us (21%)
  other arithmetic  24.4 us (9%)
  local copies, waits for them, and re-layouts  16.2 us (6%)
    pallas_call x16, Pallas kernels, call(): pl.pallas_call(kernel, out_shape=outs, in_specs=[pl.BlockSpec(memory_spac...  56.9 us
    ppermute x12, waiting for transfers between devices, flip_head(): return lax.ppermute(value, 'head', FLIP)  21.6 us
    ppermute x12, starting transfers between devices, flip_head(): return lax.ppermute(value, 'head', FLIP)  17 us
    ppermute x2, waiting for transfers between devices, gather_four(): return [own, beside, across, lax.ppermute(across, 'blk', PAIRS)]  11.1 us
    ppermute x2, waiting for transfers between devices, scatter_parts(): sent_far = lax.ppermute(far_part[1], 'blk', PAIRS).astype(FULL)  10.3 us
    unnamed x127, local copies, waits for them, and re-layouts  8.49 us
    ppermute x1, waiting for transfers between devices, grouped_body(): lax.ppermute(add_low(out_rows[2], sent_rows[1]).astype(LOW), 'blk', TWO_ON)  7.86 us
    ppermute x1, waiting for transfers between devices, grouped_body(): far = lax.ppermute(add_low(near[1], sent[1]).astype(LOW), 'seq', ACROSS)  7.29 us
  transfers between devices with their start and end apart: 61, of which 31 were waited for; matrix products, arithmetic and copies ran while one was open for 11% of the time, Pallas kernels for 19%

profile of v4, /device:TPU:2, one launch (start us, length us, event | category | flops | bytes accessed | tf_op | source)
XLA Modules:
  0.0 273.6 jit_solution(12440187202497024822)
XLA Ops:
  3.6 3.8 %collective-permute-start = (bf16[128,1024]{1,0:T(8,128)(2,1)}, bf16[128,1024]{1,0:T(8,128)(2,1)S(1)}, u32[]{:S(2)}, u32[]{:S(2)}) collective-permute-start(bf16[128,1024]{1,0:T(8,128)(2,1)} %refs_5_.3), channel_id=1, source_target_pairs={{0,1},{1,0},{2,3},{3,2},{4,5},{5,4},{6,7},{7,6},{8,9},{9,8},{10,11... | collective-permute-start | bytes 786440 | tf_op jit(solution)/shard_map/ppermute | solution.py:832
  9.1 4.3 %collective-permute-done.refs_6_ = bf16[128,1024]{1,0:T(8,128)(2,1)S(1)} collective-permute-done((bf16[128,1024]{1,0:T(8,128)(2,1)}, bf16[128,1024]{1,0:T(8,128)(2,1)S(1)}, u32[]{:S(2)}, u32[]{:S(2)}) %collective-permute-start) | collective-permute-done | bytes 262176 | tf_op jit(solution)/shard_map/ppermute | solution.py:832
  13.3 3.4 %all-to-all-start = ((bf16[8,112,128]{2,1,0:T(8,128)(2,1)}), bf16[8,112,128]{2,1,0:T(8,128)(2,1)S(1)}, u32[]{:S(2)}, u32[]{:S(2)}) async-start(bf16[8,112,128]{2,1,0:T(8,128)(2,1)} %maximum_maximum_fusion), calls=%async_computation | async-start | bytes 458752 | tf_op jit(solution)/shard_map/all_to_all | solution.py:839
  22.6 5.8 %collective-permute-done.4 = bf16[128,1024]{1,0:T(8,128)(2,1)} collective-permute-done((bf16[128,1024]{1,0:T(8,128)(2,1)}, bf16[128,1024]{1,0:T(8,128)(2,1)}, u32[]{:S(2)}, u32[]{:S(2)}) %collective-permute-start.4) | collective-permute-done | bytes 262176 | tf_op jit(solution)/shard_map/ppermute | solution.py:837
  29.4 6.4 %all-to-all-start.1 = ((bf16[8,256,128]{2,1,0:T(8,128)(2,1)}), bf16[8,256,128]{2,1,0:T(8,128)(2,1)}, u32[]{:S(2)}, u32[]{:S(2)}) async-start(bf16[8,256,128]{2,1,0:T(8,128)(2,1)} %broadcast_in_dim.19), calls=%async_computation.1 | async-start | bytes 1048576 | tf_op jit(solution)/shard_map/all_to_all | solution.py:843
  41.7 5.1 %collective-permute-done.8.refs_3_ = bf16[8,3,32,128]{3,2,1,0:T(8,128)(2,1)S(1)} collective-permute-done((bf16[8,3,32,128]{3,2,1,0:T(8,128)(2,1)S(1)}, bf16[8,3,32,128]{3,2,1,0:T(8,128)(2,1)S(1)}, u32[]{:S(2)}, u32[]{:S(2)}) %collective-permute-start.8) | collective-permute-done | bytes 196640 | tf_op jit(solution)/shard_map/ppermute | solution.py:848
  48.2 3.2 %collective-permute-done.6 = bf16[128,1024]{1,0:T(8,128)(2,1)S(1)} collective-permute-done((bf16[128,1024]{1,0:T(8,128)(2,1)}, bf16[128,1024]{1,0:T(8,128)(2,1)S(1)}, u32[]{:S(2)}, u32[]{:S(2)}) %collective-permute-start.6) | collective-permute-done | bytes 262176 | tf_op jit(solution)/shard_map/ppermute | solution.py:844
  53.9 4.6 %collective-permute-done.9.refs_12_ = bf16[128,1024]{1,0:T(8,128)(2,1)} collective-permute-done((bf16[128,1024]{1,0:T(8,128)(2,1)S(1)}, bf16[128,1024]{1,0:T(8,128)(2,1)}, u32[]{:S(2)}, u32[]{:S(2)}) %collective-permute-start.9) | collective-permute-done | bytes 262176 | tf_op jit(solution)/shard_map/ppermute | solution.py:315
  62.7 11.1 %shard_map.143 = (bf16[8,128,128]{2,1,0:T(8,128)(2,1)}, bf16[1024,128]{1,0:T(8,128)(2,1)}, bf16[1024,128]{1,0:T(8,128)(2,1)}, bf16[1024,128]{1,0:T(8,128)(2,1)},...) custom-call(s32[9]{0:T(128)} %stack.57.place, ...), custom_call_target="tpu_custom_call" | custom-call | flops 4000000000 | bytes 9962496 | tf_op jit(solution)/shard_map/pallas_call | solution.py:343
  74.4 3.6 %all-to-all-start.2 = ((bf16[8,128,128]{2,1,0:T(8,128)(2,1)}), bf16[8,128,128]{2,1,0:T(8,128)(2,1)S(1)}, u32[]{:S(2)}, u32[]{:S(2)}) async-start(bf16[8,128,128]{2,1,0:T(8,128)(2,1)} %get-tuple-element.120), calls=%async_computation.2 | async-start | bytes 524288 | tf_op jit(solution)/shard_map/all_to_all | solution.py:887
  78.0 4.7 %collective-permute-done.16.refs_3_.refs_2_ = bf16[2,128,1024]{2,1,0:T(8,128)(2,1)S(1)} collective-permute-done((bf16[2,128,1024]{2,1,0:T(8,128)(2,1)}, bf16[2,128,1024]{2,1,0:T(8,128)(2,1)S(1)}, u32[]{:S(2)}, u32[]{:S(2)}) %collective-permute-start.16) | collective-permute-done | bytes 524320 | tf_op jit(solution)/shard_map/ppermute | solution.py:863
  84.0 4.0 %all-to-all-done.2.context_ref = bf16[8,128,128]{2,1,0:T(8,128)(2,1)S(1)} async-done(((bf16[8,128,128]{2,1,0:T(8,128)(2,1)}), bf16[8,128,128]{2,1,0:T(8,128)(2,1)S(1)}, u32[]{:S(2)}, u32[]{:S(2)}) %all-to-all-start.2) | async-done | bytes 262176 | tf_op jit(solution)/shard_map/all_to_all | solution.py:887
  96.4 3.6 %collective-permute-done.21.first_ref.refs_2_ = bf16[128,1024]{1,0:T(8,128)(2,1)S(1)} collective-permute-done((bf16[128,1024]{1,0:T(8,128)(2,1)S(1)}, bf16[128,1024]{1,0:T(8,128)(2,1)S(1)}, u32[]{:S(2)}, u32[]{:S(2)}) %collective-permute-start.21) | collective-permute-done | bytes 262176 | tf_op jit(solution)/shard_map/ppermute | solution.py:315
  104.5 4.7 %collective-permute-done.22.second_ref.refs_3_ = bf16[128,1024]{1,0:T(8,128)(2,1)S(1)} collective-permute-done((bf16[128,1024]{1,0:T(8,128)(2,1)S(1)}, bf16[128,1024]{1,0:T(8,128)(2,1)S(1)}, u32[]{:S(2)}, u32[]{:S(2)}) %collective-permute-start.22) | collective-permute-done | bytes 262176 | tf_op jit(solution)/shard_map/ppermute | solution.py:326
  109.2 3.4 %shard_map.146 = (f32[256,1024]{1,0:T(8,128)S(1)}, bf16[256,1024]{1,0:T(8,128)(2,1)S(1)}, f32[128,1024]{1,0:T(8,128)S(1)}, bf16[128,1024]{1,0:T(8,128)(2,1)S(1)}) custom-call(s32[9]{0:T(128)S(1)} %copy-done.22, bf16[128,1024]{1,0:T(8,128)(2,1)S(1)} %collective-permute-done.21.first_ref.refs_2_, ...), custom_call_target="tpu_custom_call" | custom-call | flops 1500000000 | bytes 7094272 | tf_op jit(solution)/shard_map/pallas_call | solution.py:343
  114.2 3.4 %shard_map.145 = (f32[256,1024]{1,0:T(8,128)S(1)}, bf16[256,1024]{1,0:T(8,128)(2,1)S(1)}, f32[128,1024]{1,0:T(8,128)S(1)}, bf16[128,1024]{1,0:T(8,128)(2,1)S(1)}) custom-call(s32[9]{0:T(128)S(1)} %copy-done.22, bf16[128,1024]{1,0:T(8,128)(2,1)S(1)} %get-tuple-element.123.first_ref.refs_0_, bf16[128,1024]{1,0:T(8,128)(2,1)S(1)} %collective-permute-done.15.second_ref.refs_1_, ...), custom_call_target="tpu_custom_call" | custom-call | flops 1500000000 | bytes 7094272 | tf_op jit(solution)/shard_map/pallas_call | solution.py:343
  118.1 3.2 %collective-permute-done.23 = bf16[128,1024]{1,0:T(8,128)(2,1)S(1)} collective-permute-done((bf16[128,1024]{1,0:T(8,128)(2,1)S(1)}, bf16[128,1024]{1,0:T(8,128)(2,1)S(1)}, u32[]{:S(2)}, u32[]{:S(2)}) %collective-permute-start.23) | collective-permute-done | bytes 262176 | tf_op jit(solution)/shard_map/ppermute | solution.py:948
  124.7 3.2 %collective-permute-done.24.far_ref = bf16[128,1024]{1,0:T(8,128)(2,1)S(1)} collective-permute-done((bf16[128,1024]{1,0:T(8,128)(2,1)S(1)}, bf16[128,1024]{1,0:T(8,128)(2,1)S(1)}, u32[]{:S(2)}, u32[]{:S(2)}) %collective-permute-start.24) | collective-permute-done | bytes 262176 | tf_op jit(solution)/shard_map/ppermute | solution.py:315
  130.9 5.0 %collective-permute-done.31.first_ref.refs_2_ = bf16[128,1024]{1,0:T(8,128)(2,1)S(1)} collective-permute-done((bf16[128,1024]{1,0:T(8,128)(2,1)S(1)}, bf16[128,1024]{1,0:T(8,128)(2,1)S(1)}, u32[]{:S(2)}, u32[]{:S(2)}) %collective-permute-start.31) | collective-permute-done | bytes 262176 | tf_op jit(solution)/shard_map/ppermute | solution.py:315
  136.3 6.4 %collective-permute-done.32.second_ref.refs_3_ = bf16[128,1024]{1,0:T(8,128)(2,1)S(1)} collective-permute-done((bf16[128,1024]{1,0:T(8,128)(2,1)S(1)}, bf16[128,1024]{1,0:T(8,128)(2,1)S(1)}, u32[]{:S(2)}, u32[]{:S(2)}) %collective-permute-start.32) | collective-permute-done | bytes 262176 | tf_op jit(solution)/shard_map/ppermute | solution.py:326
  142.7 3.3 %shard_map.149 = (bf16[256,1024]{1,0:T(8,128)(2,1)S(1)}, f32[128,1024]{1,0:T(8,128)S(1)}, bf16[128,1024]{1,0:T(8,128)(2,1)S(1)}, f32[8,1,128]{2,1,0:T(1,128)S(1)}) custom-call(s32[9]{0:T(128)S(1)} %copy-done.22, bf16[128,1024]{1,0:T(8,128)(2,1)S(1)} %collective-permute-done.31.first_ref.refs_2_, ...), custom_call_target="tpu_custom_call" | custom-call | flops 1500000000 | bytes 7081984 | tf_op jit(solution)/shard_map/pallas_call | solution.py:343
  148.7 4.3 %shard_map.148 = (bf16[256,1024]{1,0:T(8,128)(2,1)S(1)}, f32[128,1024]{1,0:T(8,128)S(1)}, bf16[128,1024]{1,0:T(8,128)(2,1)}, f32[8,1,128]{2,1,0:T(1,128)S(1)}) custom-call(s32[9]{0:T(128)S(1)} %copy-done.22, bf16[128,1024]{1,0:T(8,128)(2,1)S(1)} %get-tuple-element.135.first_ref.refs_0_, bf16[128,1024]{1,0:T(8,128)(2,1)S(1)} %collective-permute-done.29.second_ref.refs_1_, ...), custom_call_target="tpu_custom_call" | custom-call | flops 1500000000 | bytes 7081984 | tf_op jit(solution)/shard_map/pallas_call | solution.py:343
  158.1 7.1 %collective-permute-done.33 = bf16[128,1024]{1,0:T(8,128)(2,1)S(1)} collective-permute-done((bf16[128,1024]{1,0:T(8,128)(2,1)S(1)}, bf16[128,1024]{1,0:T(8,128)(2,1)S(1)}, u32[]{:S(2)}, u32[]{:S(2)}) %collective-permute-start.33) | collective-permute-done | bytes 262176 | tf_op jit(solution)/shard_map/ppermute | solution.py:948
  173.9 3.5 %shard_map.151 = (f32[128,1024]{1,0:T(8,128)S(1)}, bf16[128,1024]{1,0:T(8,128)(2,1)S(1)}, bf16[8,128,128]{2,1,0:T(8,128)(2,1)S(1)}, f32[3,1024]{1,0:T(4,128)S(1)}) custom-call(s32[9]{0:T(128)S(1)} %copy-done.22, f32[128,1024]{1,0:T(8,128)S(1)} %copy-done.10, bf16[128,1024]{1,0:T(8,128)(2,1)} %collective-permute-done.30.sent_ref, ...), custom_call_target="tpu_custom_call" | custom-call | flops 1000000000 | bytes 5288448 | tf_op jit(solution)/shard_map/pallas_call | solution.py:343
  179.6 3.4 %all-to-all-start.3 = ((bf16[8,128,128]{2,1,0:T(8,128)(2,1)}), bf16[8,128,128]{2,1,0:T(8,128)(2,1)S(1)}, u32[]{:S(2)}, u32[]{:S(2)}) async-start(bf16[8,128,128]{2,1,0:T(8,128)(2,1)} %copy-done.14), calls=%async_computation.3 | async-start | bytes 524288 | tf_op jit(solution)/shard_map/all_to_all | solution.py:1004
  194.1 8.3 %shard_map.153.own_ref.refs_0_ = bf16[8,128,384]{2,1,0:T(8,128)(2,1)} custom-call(s32[9]{0:T(128)} %stack.57.place, bf16[8,128,128]{2,1,0:T(8,128)(2,1)} %copy-done.55, bf16[1024,128]{1,0:T(8,128)(2,1)} %get-tuple-element.162.refs_0_, bf16[1024,128]{1,0:T(8,128)(2,1)} %get-tuple-element.163.refs_1_, bf16[1024,128]{1,0:T(8,128)(2,1)} %get-tuple-element.164.refs_2_, ...), custom_call_target="tpu_custom_call" | custom-call | flops 4000000000 | bytes 7077888 | tf_op jit(solution)/shard_map/pallas_call | solution.py:343
  213.2 3.3 %shard_map.154 = (f32[2,128,1024]{2,1,0:T(8,128)S(1)}, bf16[2,128,1024]{2,1,0:T(8,128)(2,1)}) custom-call(s32[9]{0:T(128)S(1)} %copy-done.23, bf16[4,128,384]{2,1,0:T(8,128)(2,1)S(1)} %collective-permute-done.39.across_ref, bf16[8,128,384]{2,1,0:T(8,128)(2,1)S(1)} %copy-done.21, bf16[1024,384]{1,0:T(8,128)(2,1)S(1)} %copy-done.46, ...), custom_call_target="tpu_custom_call" | custom-call | flops 1000000000 | bytes 4325376 | tf_op jit(solution)/shard_map/pallas_call | solution.py:343
  226.2 7.3 %collective-permute-done.45.far_ref = bf16[272,384]{1,0:T(8,128)(2,1)S(1)} collective-permute-done((bf16[272,384]{1,0:T(8,128)(2,1)S(1)}, bf16[272,384]{1,0:T(8,128)(2,1)S(1)}, u32[]{:S(2)}, u32[]{:S(2)}) %collective-permute-start.45) | collective-permute-done | bytes 208928 | tf_op jit(solution)/shard_map/ppermute | solution.py:1081
  234.8 3.4 %all-to-all-start.4 = ((bf16[8,48,384]{2,1,0:T(8,128)(2,1)}), bf16[8,48,384]{2,1,0:T(8,128)(2,1)S(1)}, u32[]{:S(2)}, u32[]{:S(2)}) async-start(bf16[8,48,384]{2,1,0:T(8,128)(2,1)} %shard_map.156), calls=%async_computation.4 | async-start | bytes 589824 | tf_op jit(solution)/shard_map/all_to_all | solution.py:1093
  243.6 3.0 %collective-permute-start.55 = (bf16[2,128,1024]{2,1,0:T(8,128)(2,1)}, bf16[2,128,1024]{2,1,0:T(8,128)(2,1)}, u32[]{:S(2)}, u32[]{:S(2)}) collective-permute-start(bf16[2,128,1024]{2,1,0:T(8,128)(2,1)} %fusion.8), channel_id=1, source_target_pairs={{1,4},{3,6},{4,16},{5,20},{6,18},{7,22},{9,12},{11,14},{12,24},{13... | collective-permute-start | bytes 1572872 | tf_op jit(solution)/shard_map/ppermute | solution.py:1108
  252.7 7.9 %collective-permute-done.53 = bf16[32,1024]{1,0:T(8,128)(2,1)S(1)} collective-permute-done((bf16[32,1024]{1,0:T(8,128)(2,1)S(1)}, bf16[32,1024]{1,0:T(8,128)(2,1)S(1)}, u32[]{:S(2)}, u32[]{:S(2)}) %collective-permute-start.53) | collective-permute-done | bytes 65568 | tf_op jit(solution)/shard_map/ppermute | solution.py:1079
  268.3 3.1 %collective-permute-done.55 = bf16[2,128,1024]{2,1,0:T(8,128)(2,1)} collective-permute-done((bf16[2,128,1024]{2,1,0:T(8,128)(2,1)}, bf16[2,128,1024]{2,1,0:T(8,128)(2,1)}, u32[]{:S(2)}, u32[]{:S(2)}) %collective-permute-start.55) | collective-permute-done | bytes 524320 | tf_op jit(solution)/shard_map/ppermute | solution.py:1108
  (276 shorter events, 121.3 us)
Async XLA Ops:
  13.3 15.1 %all-to-all-start = ((bf16[8,112,128]{2,1,0:T(8,128)(2,1)}), bf16[8,112,128]{2,1,0:T(8,128)(2,1)S(1)}, u32[]{:S(2)}, u32[]{:S(2)}) async-start(bf16[8,112,128]{2,1,0:T(8,128)(2,1)} %maximum_maximum_fusion), calls=%async_computation | async-start | bytes 458752 | tf_op jit(solution)/shard_map/all_to_all | solution.py:839
  16.8 11.7 %collective-permute-start.4 = (bf16[128,1024]{1,0:T(8,128)(2,1)}, bf16[128,1024]{1,0:T(8,128)(2,1)}, u32[]{:S(2)}, u32[]{:S(2)}) collective-permute-start(bf16[128,1024]{1,0:T(8,128)(2,1)} %collective-permute-done.1), channel_id=1, source_target_pairs={{1,0},{2,3},{5,4},{6,7},{9,8},{10,11},{13,12},{14,15},{17,16},{18,... | collective-permute-start | bytes 786440 | tf_op jit(solution)/shard_map/ppermute | solution.py:837
  18.2 10.2 %collective-permute-start.5 = (bf16[128,1024]{1,0:T(8,128)(2,1)S(1)}, bf16[128,1024]{1,0:T(8,128)(2,1)S(1)}, u32[]{:S(2)}, u32[]{:S(2)}) collective-permute-start(bf16[128,1024]{1,0:T(8,128)(2,1)S(1)} %collective-permute-done.refs_6_), channel_id=1, source_target_pairs={{0,4},{4,0},{1,5},{5,1},{2,6},{6,2},{3,7},{7,3},{8,12},{12,8},{9,1... | collective-permute-start | bytes 786440 | tf_op jit(solution)/shard_map/ppermute | solution.py:315
  29.4 29.2 %all-to-all-start.1 = ((bf16[8,256,128]{2,1,0:T(8,128)(2,1)}), bf16[8,256,128]{2,1,0:T(8,128)(2,1)}, u32[]{:S(2)}, u32[]{:S(2)}) async-start(bf16[8,256,128]{2,1,0:T(8,128)(2,1)} %broadcast_in_dim.19), calls=%async_computation.1 | async-start | bytes 1048576 | tf_op jit(solution)/shard_map/all_to_all | solution.py:843
  38.9 12.6 %collective-permute-start.6 = (bf16[128,1024]{1,0:T(8,128)(2,1)}, bf16[128,1024]{1,0:T(8,128)(2,1)S(1)}, u32[]{:S(2)}, u32[]{:S(2)}) collective-permute-start(bf16[128,1024]{1,0:T(8,128)(2,1)} %collective-permute-done.3), channel_id=1, source_target_pairs={{1,0},{2,3},{5,4},{6,7},{9,8},{10,11},{13,12},{14,15},{17,16},{18,... | collective-permute-start | bytes 786440 | tf_op jit(solution)/shard_map/ppermute | solution.py:844
  58.6 24.1 %collective-permute-start.16 = (bf16[2,128,1024]{2,1,0:T(8,128)(2,1)}, bf16[2,128,1024]{2,1,0:T(8,128)(2,1)S(1)}, u32[]{:S(2)}, u32[]{:S(2)}) collective-permute-start(bf16[2,128,1024]{2,1,0:T(8,128)(2,1)} %pad_maximum_fusion.1), channel_id=1, source_target_pairs={{0,2},{2,0},{1,3},{3,1},{4,6},{6,4},{5,7},{7,5},{8,10},{10,8},{9,1... | collective-permute-start | bytes 1572872 | tf_op jit(solution)/shard_map/ppermute | solution.py:863
  60.2 13.6 %collective-permute-start.12 = (bf16[8,2,128,128]{3,2,1,0:T(8,128)(2,1)}, bf16[8,2,128,128]{3,2,1,0:T(8,128)(2,1)}, u32[]{:S(2)}, u32[]{:S(2)}) collective-permute-start(bf16[8,2,128,128]{3,2,1,0:T(8,128)(2,1)} %bitcast.18.refs_0_), channel_id=1, source_target_pairs={{0,16},{8,24},{16,0},{24,8},{1,17},{9,25},{17,1},{25,9},{2,18},{10... | collective-permute-start | bytes 1572872 | tf_op jit(solution)/shard_map/ppermute | solution.py:883
  73.8 14.2 %collective-permute-start.13 = (bf16[8,2,128,128]{3,2,1,0:T(8,128)(2,1)}, bf16[8,2,128,128]{3,2,1,0:T(8,128)(2,1)}, u32[]{:S(2)}, u32[]{:S(2)}) collective-permute-start(bf16[8,2,128,128]{3,2,1,0:T(8,128)(2,1)} %bitcast.18.refs_0_), channel_id=1, source_target_pairs={{0,8},{8,0},{16,24},{24,16},{1,9},{9,1},{17,25},{25,17},{2,10},{10... | collective-permute-start | bytes 1572872 | tf_op jit(solution)/shard_map/ppermute | solution.py:885
  73.9 14.2 %collective-permute-start.14 = (bf16[8,2,128,128]{3,2,1,0:T(8,128)(2,1)}, bf16[8,2,128,128]{3,2,1,0:T(8,128)(2,1)}, u32[]{:S(2)}, u32[]{:S(2)}) collective-permute-start(bf16[8,2,128,128]{3,2,1,0:T(8,128)(2,1)} %collective-permute-done.12.refs_2_), channel_id=1, source_target_pairs={{0,8},{8,0},{16,24},{24,16},{1,9},{9,1},{17,25},{25,17},{2,10},{10... | collective-permute-start | bytes 1572872 | tf_op jit(solution)/shard_map/ppermute | solution.py:886
  74.4 13.6 %all-to-all-start.2 = ((bf16[8,128,128]{2,1,0:T(8,128)(2,1)}), bf16[8,128,128]{2,1,0:T(8,128)(2,1)S(1)}, u32[]{:S(2)}, u32[]{:S(2)}) async-start(bf16[8,128,128]{2,1,0:T(8,128)(2,1)} %get-tuple-element.120), calls=%async_computation.2 | async-start | bytes 524288 | tf_op jit(solution)/shard_map/all_to_all | solution.py:887
  82.7 13.7 %collective-permute-start.18 = (bf16[2,128,1024]{2,1,0:T(8,128)(2,1)S(1)}, bf16[2,128,1024]{2,1,0:T(8,128)(2,1)S(1)}, u32[]{:S(2)}, u32[]{:S(2)}) collective-permute-start(bf16[2,128,1024]{2,1,0:T(8,128)(2,1)S(1)} %collective-permute-done.16.refs_3_.refs_2_), channel_id=1, source_target_pairs={{0,16},{8,24},{16,0},{24,8},{1,17},{9,25},{17,1},{25,9},{2,18},{10... | collective-permute-start | bytes 1572872 | tf_op jit(solution)/shard_map/ppermute | solution.py:319
  83.9 20.6 %collective-permute-start.17 = (bf16[2,128,1024]{2,1,0:T(8,128)(2,1)S(1)}, bf16[2,128,1024]{2,1,0:T(8,128)(2,1)}, u32[]{:S(2)}, u32[]{:S(2)}) collective-permute-start(bf16[2,128,1024]{2,1,0:T(8,128)(2,1)S(1)} %collective-permute-done.16.refs_3_.refs_2_), channel_id=1, source_target_pairs={{0,8},{8,0},{16,24},{24,16},{1,9},{9,1},{17,25},{25,17},{2,10},{10... | collective-permute-start | bytes 1572872 | tf_op jit(solution)/shard_map/ppermute | solution.py:320
  96.3 12.8 %collective-permute-start.19 = (bf16[2,128,1024]{2,1,0:T(8,128)(2,1)S(1)}, bf16[2,128,1024]{2,1,0:T(8,128)(2,1)S(1)}, u32[]{:S(2)}, u32[]{:S(2)}) collective-permute-start(bf16[2,128,1024]{2,1,0:T(8,128)(2,1)S(1)} %collective-permute-done.18.refs_5_.refs_4_), channel_id=1, source_target_pairs={{0,8},{8,0},{16,24},{24,16},{1,9},{9,1},{17,25},{25,17},{2,10},{10... | collective-permute-start | bytes 1572872 | tf_op jit(solution)/shard_map/ppermute | solution.py:320
  100.7 12.0 %collective-permute-start.25 = (bf16[8,3,32,128]{3,2,1,0:T(8,128)(2,1)S(1)}, bf16[8,3,32,128]{3,2,1,0:T(8,128)(2,1)S(1)}, u32[]{:S(2)}, u32[]{:S(2)}) collective-permute-start(bf16[8,3,32,128]{3,2,1,0:T(8,128)(2,1)S(1)} %bitcast.107), channel_id=1, source_target_pairs={{0,4},{4,0},{1,5},{5,1},{2,6},{6,2},{3,7},{7,3},{8,12},{12,8},{9,1... | collective-permute-start | bytes 589832 | tf_op jit(solution)/shard_map/ppermute | solution.py:315
  102.5 11.7 %collective-permute-start.15 = (bf16[128,1024]{1,0:T(8,128)(2,1)S(1)}, bf16[128,1024]{1,0:T(8,128)(2,1)S(1)}, u32[]{:S(2)}, u32[]{:S(2)}) collective-permute-start(bf16[128,1024]{1,0:T(8,128)(2,1)S(1)} %get-tuple-element.123.first_ref.refs_0_), channel_id=1, source_target_pairs={{0,1},{1,0},{2,3},{3,2},{4,5},{5,4},{6,7},{7,6},{8,9},{9,8},{10,11... | collective-permute-start | bytes 786440 | tf_op jit(solution)/shard_map/ppermute | solution.py:325
  130.9 15.2 %collective-permute-start.29 = (bf16[128,1024]{1,0:T(8,128)(2,1)S(1)}, bf16[128,1024]{1,0:T(8,128)(2,1)S(1)}, u32[]{:S(2)}, u32[]{:S(2)}) collective-permute-start(bf16[128,1024]{1,0:T(8,128)(2,1)S(1)} %get-tuple-element.135.first_ref.refs_0_), channel_id=1, source_target_pairs={{0,1},{1,0},{2,3},{3,2},{4,5},{5,4},{6,7},{7,6},{8,9},{9,8},{10,11... | collective-permute-start | bytes 786440 | tf_op jit(solution)/shard_map/ppermute | solution.py:325
  148.2 18.6 %collective-permute-start.35 = (bf16[4,128,1024]{2,1,0:T(8,128)(2,1)S(1)}, bf16[4,128,1024]{2,1,0:T(8,128)(2,1)S(1)}, u32[]{:S(2)}, u32[]{:S(2)}) collective-permute-start(bf16[4,128,1024]{2,1,0:T(8,128)(2,1)S(1)} %get-tuple-element.147), channel_id=1, source_target_pairs={{0,8},{8,0},{16,24},{24,16},{1,9},{9,1},{17,25},{25,17},{2,10},{10... | collective-permute-start | bytes 3145736 | tf_op jit(solution)/shard_map/ppermute | solution.py:994
  155.5 29.4 %collective-permute-start.36 = (bf16[4,128,1024]{2,1,0:T(8,128)(2,1)}, bf16[4,128,1024]{2,1,0:T(8,128)(2,1)}, u32[]{:S(2)}, u32[]{:S(2)}) collective-permute-start(bf16[4,128,1024]{2,1,0:T(8,128)(2,1)} %get-tuple-element.158), channel_id=1, source_target_pairs={{0,8},{8,0},{16,24},{24,16},{1,9},{9,1},{17,25},{25,17},{2,10},{10... | collective-permute-start | bytes 3145736 | tf_op jit(solution)/shard_map/ppermute | solution.py:1009
  156.2 13.9 %collective-permute-start.30 = (bf16[128,1024]{1,0:T(8,128)(2,1)}, bf16[128,1024]{1,0:T(8,128)(2,1)}, u32[]{:S(2)}, u32[]{:S(2)}) collective-permute-start(bf16[128,1024]{1,0:T(8,128)(2,1)} %get-tuple-element.138), channel_id=1, source_target_pairs={{0,1},{1,0},{2,3},{3,2},{4,5},{5,4},{6,7},{7,6},{8,9},{9,8},{10,11... | collective-permute-start | bytes 786440 | tf_op jit(solution)/shard_map/ppermute | solution.py:950
  168.0 18.9 %collective-permute-start.37 = (bf16[2,128,1024]{2,1,0:T(8,128)(2,1)}, bf16[2,128,1024]{2,1,0:T(8,128)(2,1)}, u32[]{:S(2)}, u32[]{:S(2)}) collective-permute-start(bf16[2,128,1024]{2,1,0:T(8,128)(2,1)} %add_convert_fusion), channel_id=1, source_target_pairs={{0,16},{8,24},{16,0},{24,8},{1,17},{9,25},{17,1},{25,9},{2,18},{10... | collective-permute-start | bytes 1572872 | tf_op jit(solution)/shard_map/ppermute | solution.py:1005
  179.6 12.0 %all-to-all-start.3 = ((bf16[8,128,128]{2,1,0:T(8,128)(2,1)}), bf16[8,128,128]{2,1,0:T(8,128)(2,1)S(1)}, u32[]{:S(2)}, u32[]{:S(2)}) async-start(bf16[8,128,128]{2,1,0:T(8,128)(2,1)} %copy-done.14), calls=%async_computation.3 | async-start | bytes 524288 | tf_op jit(solution)/shard_map/all_to_all | solution.py:1004
  191.6 17.5 %collective-permute-start.54 = (bf16[128,1024]{1,0:T(8,128)(2,1)}, bf16[128,1024]{1,0:T(8,128)(2,1)S(1)}, u32[]{:S(2)}, u32[]{:S(2)}) collective-permute-start(bf16[128,1024]{1,0:T(8,128)(2,1)} %fusion.12), channel_id=1, source_target_pairs={{0,2},{2,0},{1,3},{3,1},{4,6},{6,4},{5,7},{7,5},{8,10},{10,8},{9,1... | collective-permute-start | bytes 786440 | tf_op jit(solution)/shard_map/ppermute | solution.py:1021
  208.3 13.5 %collective-permute-start.44 = (bf16[2,272,384]{2,1,0:T(8,128)(2,1)S(1)}, bf16[2,272,384]{2,1,0:T(8,128)(2,1)S(1)}, u32[]{:S(2)}, u32[]{:S(2)}) collective-permute-start(bf16[2,272,384]{2,1,0:T(8,128)(2,1)S(1)} %get-tuple-element.178), channel_id=1, source_target_pairs={{0,8},{8,0},{16,24},{24,16},{1,9},{9,1},{17,25},{25,17},{2,10},{10... | collective-permute-start | bytes 1253384 | tf_op jit(solution)/shard_map/ppermute | solution.py:1051
  209.1 14.5 %collective-permute-start.41 = (bf16[2,128,1024]{2,1,0:T(8,128)(2,1)S(1)}, bf16[2,128,1024]{2,1,0:T(8,128)(2,1)S(1)}, u32[]{:S(2)}, u32[]{:S(2)}) collective-permute-start(bf16[2,128,1024]{2,1,0:T(8,128)(2,1)S(1)} %copy-done.54), channel_id=1, source_target_pairs={{0,16},{8,24},{16,0},{24,8},{1,17},{9,25},{17,1},{25,9},{2,18},{10... | collective-permute-start | bytes 1572872 | tf_op jit(solution)/shard_map/ppermute | solution.py:1020
  216.5 34.3 %collective-permute-start.40 = (bf16[2,128,1024]{2,1,0:T(8,128)(2,1)}, bf16[2,128,1024]{2,1,0:T(8,128)(2,1)}, u32[]{:S(2)}, u32[]{:S(2)}) collective-permute-start(bf16[2,128,1024]{2,1,0:T(8,128)(2,1)} %get-tuple-element.170), channel_id=1, source_target_pairs={{0,1},{1,0},{2,3},{3,2},{4,5},{5,4},{6,7},{7,6},{8,9},{9,8},{10,11... | collective-permute-start | bytes 1572872 | tf_op jit(solution)/shard_map/ppermute | solution.py:1064
  219.8 18.5 %collective-permute-start.51 = (bf16[4,32,1024]{2,1,0:T(8,128)(2,1)}, bf16[4,32,1024]{2,1,0:T(8,128)(2,1)}, u32[]{:S(2)}, u32[]{:S(2)}) collective-permute-start(bf16[4,32,1024]{2,1,0:T(8,128)(2,1)} %get-tuple-element.189), channel_id=1, source_target_pairs={{0,16},{8,24},{16,0},{24,8},{1,17},{9,25},{17,1},{25,9},{2,18},{10... | collective-permute-start | bytes 786440 | tf_op jit(solution)/shard_map/ppermute | solution.py:1073
  221.9 11.5 %collective-permute-start.45 = (bf16[272,384]{1,0:T(8,128)(2,1)S(1)}, bf16[272,384]{1,0:T(8,128)(2,1)S(1)}, u32[]{:S(2)}, u32[]{:S(2)}) collective-permute-start(bf16[272,384]{1,0:T(8,128)(2,1)S(1)} %get-tuple-element.194), channel_id=1, source_target_pairs={{0,16},{8,24},{16,0},{24,8},{1,17},{9,25},{17,1},{25,9},{2,18},{10... | collective-permute-start | bytes 626696 | tf_op jit(solution)/shard_map/ppermute | solution.py:1081
  225.5 15.9 %collective-permute-start.42 = (bf16[128,1024]{1,0:T(8,128)(2,1)}, bf16[128,1024]{1,0:T(8,128)(2,1)}, u32[]{:S(2)}, u32[]{:S(2)}) collective-permute-start(bf16[128,1024]{1,0:T(8,128)(2,1)} %fusion.14), channel_id=1, source_target_pairs={{0,2},{2,0},{1,3},{3,1},{4,6},{6,4},{5,7},{7,5},{8,10},{10,8},{9,1... | collective-permute-start | bytes 786440 | tf_op jit(solution)/shard_map/ppermute | solution.py:1040
  234.8 26.5 %all-to-all-start.4 = ((bf16[8,48,384]{2,1,0:T(8,128)(2,1)}), bf16[8,48,384]{2,1,0:T(8,128)(2,1)S(1)}, u32[]{:S(2)}, u32[]{:S(2)}) async-start(bf16[8,48,384]{2,1,0:T(8,128)(2,1)} %shard_map.156), calls=%async_computation.4 | async-start | bytes 589824 | tf_op jit(solution)/shard_map/all_to_all | solution.py:1093
  243.6 27.8 %collective-permute-start.55 = (bf16[2,128,1024]{2,1,0:T(8,128)(2,1)}, bf16[2,128,1024]{2,1,0:T(8,128)(2,1)}, u32[]{:S(2)}, u32[]{:S(2)}) collective-permute-start(bf16[2,128,1024]{2,1,0:T(8,128)(2,1)} %fusion.8), channel_id=1, source_target_pairs={{1,4},{3,6},{4,16},{5,20},{6,18},{7,22},{9,12},{11,14},{12,24},{13... | collective-permute-start | bytes 1572872 | tf_op jit(solution)/shard_map/ppermute | solution.py:1108
  248.7 11.9 %collective-permute-start.53 = (bf16[32,1024]{1,0:T(8,128)(2,1)S(1)}, bf16[32,1024]{1,0:T(8,128)(2,1)S(1)}, u32[]{:S(2)}, u32[]{:S(2)}) collective-permute-start(bf16[32,1024]{1,0:T(8,128)(2,1)S(1)} %fusion.19), channel_id=1, source_target_pairs={{0,2},{2,0},{1,3},{3,1},{4,6},{6,4},{5,7},{7,5},{8,10},{10,8},{9,1... | collective-permute-start | bytes 196616 | tf_op jit(solution)/shard_map/ppermute | solution.py:1079
  251.9 13.7 %collective-permute-start.43 = (bf16[128,1024]{1,0:T(8,128)(2,1)S(1)}, bf16[128,1024]{1,0:T(8,128)(2,1)S(1)}, u32[]{:S(2)}, u32[]{:S(2)}) collective-permute-start(bf16[128,1024]{1,0:T(8,128)(2,1)S(1)} %fusion.13), channel_id=1, source_target_pairs={{0,2},{2,0},{1,3},{3,1},{4,6},{6,4},{5,7},{7,5},{8,10},{10,8},{9,1... | collective-permute-start | bytes 786440 | tf_op jit(solution)/shard_map/ppermute | solution.py:1076
  (91 other events, 879.7 us)

commit v5 on v4

--- a/solution.py
+++ b/solution.py
@@ -989,10 +989,6 @@
             )
         )
     summed = scatter_parts(back_parts[0][1:3], back_parts[1][1:3])
-    acts = after((ffn_parts[0][1], ffn_parts[1][1]), back_parts[1][0])
-    out_near_grad, out_away_grad = weight_grads(acts, grad_ffn_slots)
-    out_sent = lax.ppermute(out_away_grad, "seq", CORE)
-    summed = after(summed, out_sent)
     grad_one, grad_attn, grad_context, mid_sums = call(
         mix_back_kernel,
         [per_row, per_row_low, shape_of((8, rows, own), LOW), three_sums],
@@ -1002,6 +998,9 @@
         far_in=4,
     )
     grad_context = lax.all_to_all(grad_context, GROUP, 0, 0, tiled=True)
+    acts = after((ffn_parts[0][1], ffn_parts[1][1]), grad_one)
+    out_near_grad, out_away_grad = weight_grads(acts, grad_ffn_slots)
+    out_sent = lax.ppermute(out_away_grad, "seq", CORE)
     out_across = lax.ppermute(
         add_low(out_near_grad[2:], out_sent[2:]).astype(LOW), "seq", ACROSS
     )

time: 275 us -> 273 us (level)
  local copies, waits for them, and re-layouts: 16.2 us -> 11.1 us
  waiting for transfers between devices: 101 us -> 105 us
    ppermute x2, waiting for transfers between devices: 10.3 us -> 2.9 us  [scatter_parts(): sent_far = lax.ppermute(far_part[1], 'blk', PAIRS).astype(FULL)]
    ppermute x1, waiting for transfers between devices: 0.01 us -> 5.27 us  [grouped_body(): lax.ppermute(add_low(out_near_grad[2:], out_sent[2:]).astype(LOW), 'seq',...]
    ppermute x12, starting transfers between devices: 17 us -> 12 us  [flip_head(): return lax.ppermute(value, 'head', FLIP)]
    ppermute x12, waiting for transfers between devices: 21.6 us -> 26.4 us  [flip_head(): return lax.ppermute(value, 'head', FLIP)]
    unnamed x127 -> x105, local copies, waits for them, and re-layouts: 8.49 us -> 5.12 us
    ppermute x2, waiting for transfers between devices: 2.16 us -> 5.1 us  [scatter_parts(): return (near_part[0], lax.ppermute(near_part[1], 'blk', PAIRS), far)]
    all_to_all x1, starting transfers between devices: 3.4 us -> 6.34 us  [grouped_body(): swapped = lax.all_to_all(to_swap, GROUP, 0, 0, tiled=True)]
  transfers between devices with their start and end apart: 61 -> 61, of which waited for: 31 -> 35; matrix products, arithmetic and copies ran while one was open for 11% -> 10% of each run, Pallas kernels for 19% -> 18%
where the time goes in v5:
time: 273 us; the launch traced here: 272 us
  waiting for transfers between devices  105 us (38%)
  starting transfers between devices  73.8 us (27%)
  Pallas kernels  56.8 us (21%)
  other arithmetic  23.6 us (9%)
  local copies, waits for them, and re-layouts  11.1 us (4%)
    pallas_call x16, Pallas kernels, call(): pl.pallas_call(kernel, out_shape=outs, in_specs=[pl.BlockSpec(memory_spac...  56.8 us
    ppermute x12, waiting for transfers between devices, flip_head(): return lax.ppermute(value, 'head', FLIP)  26.4 us
    ppermute x12, starting transfers between devices, flip_head(): return lax.ppermute(value, 'head', FLIP)  12 us
    ppermute x2, waiting for transfers between devices, gather_four(): return [own, beside, across, lax.ppermute(across, 'blk', PAIRS)]  11 us
    ppermute x1, waiting for transfers between devices, grouped_body(): lax.ppermute(add_low(out_rows[2], sent_rows[1]).astype(LOW), 'blk', TWO_ON)  7.9 us
    ppermute x1, waiting for transfers between devices, grouped_body(): far = lax.ppermute(add_low(near[1], sent[1]).astype(LOW), 'seq', ACROSS)  6.63 us
    all_to_all x1, starting transfers between devices, grouped_body(): swapped = lax.all_to_all(to_swap, GROUP, 0, 0, tiled=True)  6.34 us
  transfers between devices with their start and end apart: 61, of which 35 were waited for; matrix products, arithmetic and copies ran while one was open for 10% of the time, Pallas kernels for 18%

profile of v5, /device:TPU:2, one launch (start us, length us, event | category | flops | bytes accessed | tf_op | source)
XLA Modules:
  0.0 271.5 jit_solution(1365263659287209881)
XLA Ops:
  11.7 6.3 %all-to-all-start = ((bf16[8,112,128]{2,1,0:T(8,128)(2,1)}), bf16[8,112,128]{2,1,0:T(8,128)(2,1)S(1)}, u32[]{:S(2)}, u32[]{:S(2)}) async-start(bf16[8,112,128]{2,1,0:T(8,128)(2,1)} %maximum_maximum_fusion), calls=%async_computation | async-start | bytes 458752 | tf_op jit(solution)/shard_map/all_to_all | solution.py:839
  24.0 4.0 %collective-permute-done.5.refs_10_ = bf16[128,1024]{1,0:T(8,128)(2,1)S(1)} collective-permute-done((bf16[128,1024]{1,0:T(8,128)(2,1)S(1)}, bf16[128,1024]{1,0:T(8,128)(2,1)S(1)}, u32[]{:S(2)}, u32[]{:S(2)}) %collective-permute-start.5) | collective-permute-done | bytes 262176 | tf_op jit(solution)/shard_map/ppermute | solution.py:315
  28.0 3.3 %collective-permute-done.4 = bf16[128,1024]{1,0:T(8,128)(2,1)} collective-permute-done((bf16[128,1024]{1,0:T(8,128)(2,1)S(1)}, bf16[128,1024]{1,0:T(8,128)(2,1)}, u32[]{:S(2)}, u32[]{:S(2)}) %collective-permute-start.4) | collective-permute-done | bytes 262176 | tf_op jit(solution)/shard_map/ppermute | solution.py:837
  32.2 4.1 %all-to-all-start.1 = ((bf16[8,256,128]{2,1,0:T(8,128)(2,1)}), bf16[8,256,128]{2,1,0:T(8,128)(2,1)}, u32[]{:S(2)}, u32[]{:S(2)}) async-start(bf16[8,256,128]{2,1,0:T(8,128)(2,1)} %broadcast_in_dim.19), calls=%async_computation.1 | async-start | bytes 1048576 | tf_op jit(solution)/shard_map/all_to_all | solution.py:843
  41.2 5.1 %collective-permute-done.8.refs_3_ = bf16[8,3,32,128]{3,2,1,0:T(8,128)(2,1)S(1)} collective-permute-done((bf16[8,3,32,128]{3,2,1,0:T(8,128)(2,1)S(1)}, bf16[8,3,32,128]{3,2,1,0:T(8,128)(2,1)S(1)}, u32[]{:S(2)}, u32[]{:S(2)}) %collective-permute-start.8) | collective-permute-done | bytes 196640 | tf_op jit(solution)/shard_map/ppermute | solution.py:848
  47.0 4.6 %collective-permute-done.6 = bf16[128,1024]{1,0:T(8,128)(2,1)S(1)} collective-permute-done((bf16[128,1024]{1,0:T(8,128)(2,1)}, bf16[128,1024]{1,0:T(8,128)(2,1)S(1)}, u32[]{:S(2)}, u32[]{:S(2)}) %collective-permute-start.6) | collective-permute-done | bytes 262176 | tf_op jit(solution)/shard_map/ppermute | solution.py:844
  55.3 3.2 %collective-permute-done.9.refs_12_ = bf16[128,1024]{1,0:T(8,128)(2,1)} collective-permute-done((bf16[128,1024]{1,0:T(8,128)(2,1)S(1)}, bf16[128,1024]{1,0:T(8,128)(2,1)}, u32[]{:S(2)}, u32[]{:S(2)}) %collective-permute-start.9) | collective-permute-done | bytes 262176 | tf_op jit(solution)/shard_map/ppermute | solution.py:315
  61.8 11.1 %shard_map.143 = (bf16[8,128,128]{2,1,0:T(8,128)(2,1)}, bf16[1024,128]{1,0:T(8,128)(2,1)}, bf16[1024,128]{1,0:T(8,128)(2,1)}, bf16[1024,128]{1,0:T(8,128)(2,1)},...) custom-call(s32[9]{0:T(128)} %stack.57.place, ...), custom_call_target="tpu_custom_call" | custom-call | flops 4000000000 | bytes 9962496 | tf_op jit(solution)/shard_map/pallas_call | solution.py:343
  73.4 4.7 %all-to-all-start.2 = ((bf16[8,128,128]{2,1,0:T(8,128)(2,1)}), bf16[8,128,128]{2,1,0:T(8,128)(2,1)S(1)}, u32[]{:S(2)}, u32[]{:S(2)}) async-start(bf16[8,128,128]{2,1,0:T(8,128)(2,1)} %get-tuple-element.117), calls=%async_computation.2 | async-start | bytes 524288 | tf_op jit(solution)/shard_map/all_to_all | solution.py:887
  78.1 4.6 %collective-permute-done.16.refs_3_.refs_2_ = bf16[2,128,1024]{2,1,0:T(8,128)(2,1)S(1)} collective-permute-done((bf16[2,128,1024]{2,1,0:T(8,128)(2,1)}, bf16[2,128,1024]{2,1,0:T(8,128)(2,1)S(1)}, u32[]{:S(2)}, u32[]{:S(2)}) %collective-permute-start.16) | collective-permute-done | bytes 524320 | tf_op jit(solution)/shard_map/ppermute | solution.py:863
  85.1 4.6 %all-to-all-done.2.context_ref = bf16[8,128,128]{2,1,0:T(8,128)(2,1)S(1)} async-done(((bf16[8,128,128]{2,1,0:T(8,128)(2,1)}), bf16[8,128,128]{2,1,0:T(8,128)(2,1)S(1)}, u32[]{:S(2)}, u32[]{:S(2)}) %all-to-all-start.2) | async-done | bytes 262176 | tf_op jit(solution)/shard_map/all_to_all | solution.py:887
  90.6 2.8 %shard_map.144 = (f32[128,1024]{1,0:T(8,128)S(1)}, bf16[128,1024]{1,0:T(8,128)(2,1)S(1)}, f32[128,1024]{1,0:T(8,128)S(1)}, f32[128,1]{1,0:T(8,128)S(1)}) custom-call(s32[9]{0:T(128)S(1)} %copy-done.15, bf16[8,128,128]{2,1,0:T(8,128)(2,1)S(1)} %all-to-all-done.2.context_ref, bf16[128,1024]{1,0:T(8,128)(2,1)S(1)} %copy-done.17, ...), custom_call_target="tpu_custom_call" | custom-call | flops 1000000000 | bytes 3965440 | tf_op jit(solution)/shard_map/pallas_call | solution.py:343
  93.5 2.9 %collective-permute-done.18.refs_5_.refs_4_ = bf16[2,128,1024]{2,1,0:T(8,128)(2,1)S(1)} collective-permute-done((bf16[2,128,1024]{2,1,0:T(8,128)(2,1)S(1)}, bf16[2,128,1024]{2,1,0:T(8,128)(2,1)S(1)}, u32[]{:S(2)}, u32[]{:S(2)}) %collective-permute-start.18) | collective-permute-done | bytes 524320 | tf_op jit(solution)/shard_map/ppermute | solution.py:319
  96.4 5.3 %collective-permute-done.21.first_ref.refs_2_ = bf16[128,1024]{1,0:T(8,128)(2,1)S(1)} collective-permute-done((bf16[128,1024]{1,0:T(8,128)(2,1)S(1)}, bf16[128,1024]{1,0:T(8,128)(2,1)S(1)}, u32[]{:S(2)}, u32[]{:S(2)}) %collective-permute-start.21) | collective-permute-done | bytes 262176 | tf_op jit(solution)/shard_map/ppermute | solution.py:315
  104.0 6.9 %collective-permute-done.22.second_ref.refs_3_ = bf16[128,1024]{1,0:T(8,128)(2,1)S(1)} collective-permute-done((bf16[128,1024]{1,0:T(8,128)(2,1)S(1)}, bf16[128,1024]{1,0:T(8,128)(2,1)S(1)}, u32[]{:S(2)}, u32[]{:S(2)}) %collective-permute-start.22) | collective-permute-done | bytes 262176 | tf_op jit(solution)/shard_map/ppermute | solution.py:326
  111.0 3.4 %shard_map.146 = (f32[256,1024]{1,0:T(8,128)S(1)}, bf16[256,1024]{1,0:T(8,128)(2,1)S(1)}, f32[128,1024]{1,0:T(8,128)S(1)}, bf16[128,1024]{1,0:T(8,128)(2,1)S(1)}) custom-call(s32[9]{0:T(128)S(1)} %copy-done.15, bf16[128,1024]{1,0:T(8,128)(2,1)S(1)} %collective-permute-done.21.first_ref.refs_2_, ...), custom_call_target="tpu_custom_call" | custom-call | flops 1500000000 | bytes 7094272 | tf_op jit(solution)/shard_map/pallas_call | solution.py:343
  116.0 3.4 %shard_map.145 = (f32[256,1024]{1,0:T(8,128)S(1)}, bf16[256,1024]{1,0:T(8,128)(2,1)S(1)}, f32[128,1024]{1,0:T(8,128)S(1)}, bf16[128,1024]{1,0:T(8,128)(2,1)S(1)}) custom-call(s32[9]{0:T(128)S(1)} %copy-done.15, bf16[128,1024]{1,0:T(8,128)(2,1)S(1)} %get-tuple-element.120.first_ref.refs_0_, bf16[128,1024]{1,0:T(8,128)(2,1)S(1)} %collective-permute-done.15.second_ref.refs_1_, ...), custom_call_target="tpu_custom_call" | custom-call | flops 1500000000 | bytes 7094272 | tf_op jit(solution)/shard_map/pallas_call | solution.py:343
  130.9 6.4 %collective-permute-done.31.first_ref.refs_2_ = bf16[128,1024]{1,0:T(8,128)(2,1)S(1)} collective-permute-done((bf16[128,1024]{1,0:T(8,128)(2,1)S(1)}, bf16[128,1024]{1,0:T(8,128)(2,1)S(1)}, u32[]{:S(2)}, u32[]{:S(2)}) %collective-permute-start.31) | collective-permute-done | bytes 262176 | tf_op jit(solution)/shard_map/ppermute | solution.py:315
  139.7 4.1 %collective-permute-done.32.second_ref.refs_3_ = bf16[128,1024]{1,0:T(8,128)(2,1)S(1)} collective-permute-done((bf16[128,1024]{1,0:T(8,128)(2,1)S(1)}, bf16[128,1024]{1,0:T(8,128)(2,1)S(1)}, u32[]{:S(2)}, u32[]{:S(2)}) %collective-permute-start.32) | collective-permute-done | bytes 262176 | tf_op jit(solution)/shard_map/ppermute | solution.py:326
  143.8 3.3 %shard_map.149 = (bf16[256,1024]{1,0:T(8,128)(2,1)S(1)}, f32[128,1024]{1,0:T(8,128)S(1)}, bf16[128,1024]{1,0:T(8,128)(2,1)S(1)}, f32[8,1,128]{2,1,0:T(1,128)S(1)}) custom-call(s32[9]{0:T(128)S(1)} %copy-done.15, bf16[128,1024]{1,0:T(8,128)(2,1)S(1)} %collective-permute-done.31.first_ref.refs_2_, ...), custom_call_target="tpu_custom_call" | custom-call | flops 1500000000 | bytes 7081984 | tf_op jit(solution)/shard_map/pallas_call | solution.py:343
  149.4 3.5 %shard_map.148 = (bf16[256,1024]{1,0:T(8,128)(2,1)S(1)}, f32[128,1024]{1,0:T(8,128)S(1)}, bf16[128,1024]{1,0:T(8,128)(2,1)S(1)}, f32[8,1,128]{2,1,0:T(1,128)S(1)}) custom-call(s32[9]{0:T(128)S(1)} %copy-done.15, bf16[128,1024]{1,0:T(8,128)(2,1)S(1)} %get-tuple-element.132.first_ref.refs_0_, bf16[128,1024]{1,0:T(8,128)(2,1)S(1)} %collective-permute-done.29.second_ref.refs_1_, ...), custom_call_target="tpu_custom_call" | custom-call | flops 1500000000 | bytes 7081984 | tf_op jit(solution)/shard_map/pallas_call | solution.py:343
  156.1 3.3 %collective-permute-done.30.sent_ref = bf16[128,1024]{1,0:T(8,128)(2,1)S(1)} collective-permute-done((bf16[128,1024]{1,0:T(8,128)(2,1)S(1)}, bf16[128,1024]{1,0:T(8,128)(2,1)S(1)}, u32[]{:S(2)}, u32[]{:S(2)}) %collective-permute-start.30) | collective-permute-done | bytes 262176 | tf_op jit(solution)/shard_map/ppermute | solution.py:950
  161.4 3.6 %shard_map.150 = (f32[128,1024]{1,0:T(8,128)S(1)}, bf16[128,1024]{1,0:T(8,128)(2,1)S(1)}, bf16[8,128,128]{2,1,0:T(8,128)(2,1)}, f32[3,1024]{1,0:T(4,128)S(1)}) custom-call(s32[9]{0:T(128)S(1)} %copy-done.15, f32[128,1024]{1,0:T(8,128)S(1)} %get-tuple-element.134.near_ref, bf16[128,1024]{1,0:T(8,128)(2,1)S(1)} %collective-permute-done.30.sent_ref, ...), custom_call_target="tpu_custom_call" | custom-call | flops 1000000000 | bytes 5288448 | tf_op jit(solution)/shard_map/pallas_call | solution.py:343
  175.2 4.3 %all-to-all-start.3 = ((bf16[8,128,128]{2,1,0:T(8,128)(2,1)}), bf16[8,128,128]{2,1,0:T(8,128)(2,1)}, u32[]{:S(2)}, u32[]{:S(2)}) async-start(bf16[8,128,128]{2,1,0:T(8,128)(2,1)} %get-tuple-element.143), calls=%async_computation.3 | async-start | bytes 524288 | tf_op jit(solution)/shard_map/all_to_all | solution.py:1000
  181.6 5.3 %collective-permute-done.37 = bf16[2,128,1024]{2,1,0:T(8,128)(2,1)} collective-permute-done((bf16[2,128,1024]{2,1,0:T(8,128)(2,1)}, bf16[2,128,1024]{2,1,0:T(8,128)(2,1)}, u32[]{:S(2)}, u32[]{:S(2)}) %collective-permute-start.37) | collective-permute-done | bytes 524320 | tf_op jit(solution)/shard_map/ppermute | solution.py:1004
  189.1 8.3 %shard_map.153.own_ref.refs_0_ = bf16[8,128,384]{2,1,0:T(8,128)(2,1)} custom-call(s32[9]{0:T(128)} %stack.57.place, bf16[8,128,128]{2,1,0:T(8,128)(2,1)} %all-to-all-done.3.grad_ref, bf16[1024,128]{1,0:T(8,128)(2,1)} %get-tuple-element.156.refs_0_, bf16[1024,128]{1,0:T(8,128)(2,1)} %get-tuple-element.157.refs_1_, ...), custom_call_target="tpu_custom_call" | custom-call | flops 4000000000 | bytes 7077888 | tf_op jit(solution)/shard_map/pallas_call | solution.py:343
  209.5 3.3 %shard_map.154 = (f32[2,128,1024]{2,1,0:T(8,128)S(1)}, bf16[2,128,1024]{2,1,0:T(8,128)(2,1)}) custom-call(s32[9]{0:T(128)S(1)} %copy-done.16, bf16[4,128,384]{2,1,0:T(8,128)(2,1)S(1)} %collective-permute-done.39.across_ref, bf16[8,128,384]{2,1,0:T(8,128)(2,1)S(1)} %copy-done.14, bf16[1024,384]{1,0:T(8,128)(2,1)S(1)} %copy-done.37, ...), custom_call_target="tpu_custom_call" | custom-call | flops 1000000000 | bytes 4325376 | tf_op jit(solution)/shard_map/pallas_call | solution.py:343
  213.5 3.0 %shard_map.158 = (f32[4,32,1024]{2,1,0:T(8,128)S(1)}, bf16[4,32,1024]{2,1,0:T(8,128)(2,1)}) custom-call(s32[9]{0:T(128)S(1)} %copy-done.16, bf16[2,128,128]{2,1,0:T(8,128)(2,1)S(1)} %get-tuple-element.195.refs_0_, bf16[2,128,128]{2,1,0:T(8,128)(2,1)S(1)} %collective-permute-done.46.refs_1_, bf16[2,128,128]{2,1,0:T(8,128)(2,1)S(1)} %collective-permute-done.47.refs_2_, ...), custom_call_target="tpu_custom_call" | custom-call | flops 500000000 | bytes 2097152 | tf_op jit(solution)/shard_map/pallas_call | solution.py:343
  223.4 6.6 %collective-permute-done.45.far_ref = bf16[272,384]{1,0:T(8,128)(2,1)S(1)} collective-permute-done((bf16[272,384]{1,0:T(8,128)(2,1)S(1)}, bf16[272,384]{1,0:T(8,128)(2,1)S(1)}, u32[]{:S(2)}, u32[]{:S(2)}) %collective-permute-start.45) | collective-permute-done | bytes 208928 | tf_op jit(solution)/shard_map/ppermute | solution.py:1080
  231.3 5.3 %all-to-all-start.4 = ((bf16[8,48,384]{2,1,0:T(8,128)(2,1)}), bf16[8,48,384]{2,1,0:T(8,128)(2,1)S(1)}, u32[]{:S(2)}, u32[]{:S(2)}) async-start(bf16[8,48,384]{2,1,0:T(8,128)(2,1)} %shard_map.156), calls=%async_computation.4 | async-start | bytes 589824 | tf_op jit(solution)/shard_map/all_to_all | solution.py:1092
  250.6 7.9 %collective-permute-done.53 = bf16[32,1024]{1,0:T(8,128)(2,1)S(1)} collective-permute-done((bf16[32,1024]{1,0:T(8,128)(2,1)S(1)}, bf16[32,1024]{1,0:T(8,128)(2,1)S(1)}, u32[]{:S(2)}, u32[]{:S(2)}) %collective-permute-start.53) | collective-permute-done | bytes 65568 | tf_op jit(solution)/shard_map/ppermute | solution.py:1078
  265.5 3.8 %collective-permute-done.55 = bf16[2,128,1024]{2,1,0:T(8,128)(2,1)} collective-permute-done((bf16[2,128,1024]{2,1,0:T(8,128)(2,1)}, bf16[2,128,1024]{2,1,0:T(8,128)(2,1)}, u32[]{:S(2)}, u32[]{:S(2)}) %collective-permute-start.55) | collective-permute-done | bytes 524320 | tf_op jit(solution)/shard_map/ppermute | solution.py:1107
  (254 shorter events, 117.6 us)
Async XLA Ops:
  11.7 19.6 %all-to-all-start = ((bf16[8,112,128]{2,1,0:T(8,128)(2,1)}), bf16[8,112,128]{2,1,0:T(8,128)(2,1)S(1)}, u32[]{:S(2)}, u32[]{:S(2)}) async-start(bf16[8,112,128]{2,1,0:T(8,128)(2,1)} %maximum_maximum_fusion), calls=%async_computation | async-start | bytes 458752 | tf_op jit(solution)/shard_map/all_to_all | solution.py:839
  21.6 9.7 %collective-permute-start.4 = (bf16[128,1024]{1,0:T(8,128)(2,1)S(1)}, bf16[128,1024]{1,0:T(8,128)(2,1)}, u32[]{:S(2)}, u32[]{:S(2)}) collective-permute-start(bf16[128,1024]{1,0:T(8,128)(2,1)S(1)} %collective-permute-done.1), channel_id=1, source_target_pairs={{1,0},{2,3},{5,4},{6,7},{9,8},{10,11},{13,12},{14,15},{17,16},{18,... | collective-permute-start | bytes 786440 | tf_op jit(solution)/shard_map/ppermute | solution.py:837
  32.2 26.4 %all-to-all-start.1 = ((bf16[8,256,128]{2,1,0:T(8,128)(2,1)}), bf16[8,256,128]{2,1,0:T(8,128)(2,1)}, u32[]{:S(2)}, u32[]{:S(2)}) async-start(bf16[8,256,128]{2,1,0:T(8,128)(2,1)} %broadcast_in_dim.19), calls=%async_computation.1 | async-start | bytes 1048576 | tf_op jit(solution)/shard_map/all_to_all | solution.py:843
  37.3 9.5 %collective-permute-start.7 = (bf16[128,1024]{1,0:T(8,128)(2,1)S(1)}, bf16[128,1024]{1,0:T(8,128)(2,1)S(1)}, u32[]{:S(2)}, u32[]{:S(2)}) collective-permute-start(bf16[128,1024]{1,0:T(8,128)(2,1)S(1)} %broadcast_select_fusion.1.refs_7_), channel_id=1, source_target_pairs={{0,4},{4,0},{1,5},{5,1},{2,6},{6,2},{3,7},{7,3},{8,12},{12,8},{9,1... | collective-permute-start | bytes 786440 | tf_op jit(solution)/shard_map/ppermute | solution.py:315
  39.3 12.4 %collective-permute-start.6 = (bf16[128,1024]{1,0:T(8,128)(2,1)}, bf16[128,1024]{1,0:T(8,128)(2,1)S(1)}, u32[]{:S(2)}, u32[]{:S(2)}) collective-permute-start(bf16[128,1024]{1,0:T(8,128)(2,1)} %collective-permute-done.3), channel_id=1, source_target_pairs={{1,0},{2,3},{5,4},{6,7},{9,8},{10,11},{13,12},{14,15},{17,16},{18,... | collective-permute-start | bytes 786440 | tf_op jit(solution)/shard_map/ppermute | solution.py:844
  58.6 14.3 %collective-permute-start.12 = (bf16[8,2,128,128]{3,2,1,0:T(8,128)(2,1)}, bf16[8,2,128,128]{3,2,1,0:T(8,128)(2,1)}, u32[]{:S(2)}, u32[]{:S(2)}) collective-permute-start(bf16[8,2,128,128]{3,2,1,0:T(8,128)(2,1)} %bitcast.18.refs_0_), channel_id=1, source_target_pairs={{0,16},{8,24},{16,0},{24,8},{1,17},{9,25},{17,1},{25,9},{2,18},{10... | collective-permute-start | bytes 1572872 | tf_op jit(solution)/shard_map/ppermute | solution.py:883
  59.1 23.6 %collective-permute-start.16 = (bf16[2,128,1024]{2,1,0:T(8,128)(2,1)}, bf16[2,128,1024]{2,1,0:T(8,128)(2,1)S(1)}, u32[]{:S(2)}, u32[]{:S(2)}) collective-permute-start(bf16[2,128,1024]{2,1,0:T(8,128)(2,1)} %pad_maximum_fusion.1), channel_id=1, source_target_pairs={{0,2},{2,0},{1,3},{3,1},{4,6},{6,4},{5,7},{7,5},{8,10},{10,8},{9,1... | collective-permute-start | bytes 1572872 | tf_op jit(solution)/shard_map/ppermute | solution.py:863
  72.9 16.8 %collective-permute-start.13 = (bf16[8,2,128,128]{3,2,1,0:T(8,128)(2,1)}, bf16[8,2,128,128]{3,2,1,0:T(8,128)(2,1)}, u32[]{:S(2)}, u32[]{:S(2)}) collective-permute-start(bf16[8,2,128,128]{3,2,1,0:T(8,128)(2,1)} %bitcast.18.refs_0_), channel_id=1, source_target_pairs={{0,8},{8,0},{16,24},{24,16},{1,9},{9,1},{17,25},{25,17},{2,10},{10... | collective-permute-start | bytes 1572872 | tf_op jit(solution)/shard_map/ppermute | solution.py:885
  72.9 16.7 %collective-permute-start.14 = (bf16[8,2,128,128]{3,2,1,0:T(8,128)(2,1)}, bf16[8,2,128,128]{3,2,1,0:T(8,128)(2,1)}, u32[]{:S(2)}, u32[]{:S(2)}) collective-permute-start(bf16[8,2,128,128]{3,2,1,0:T(8,128)(2,1)} %collective-permute-done.12.refs_2_), channel_id=1, source_target_pairs={{0,8},{8,0},{16,24},{24,16},{1,9},{9,1},{17,25},{25,17},{2,10},{10... | collective-permute-start | bytes 1572872 | tf_op jit(solution)/shard_map/ppermute | solution.py:886
  73.4 16.2 %all-to-all-start.2 = ((bf16[8,128,128]{2,1,0:T(8,128)(2,1)}), bf16[8,128,128]{2,1,0:T(8,128)(2,1)S(1)}, u32[]{:S(2)}, u32[]{:S(2)}) async-start(bf16[8,128,128]{2,1,0:T(8,128)(2,1)} %get-tuple-element.117), calls=%async_computation.2 | async-start | bytes 524288 | tf_op jit(solution)/shard_map/all_to_all | solution.py:887
  82.7 13.7 %collective-permute-start.18 = (bf16[2,128,1024]{2,1,0:T(8,128)(2,1)S(1)}, bf16[2,128,1024]{2,1,0:T(8,128)(2,1)S(1)}, u32[]{:S(2)}, u32[]{:S(2)}) collective-permute-start(bf16[2,128,1024]{2,1,0:T(8,128)(2,1)S(1)} %collective-permute-done.16.refs_3_.refs_2_), channel_id=1, source_target_pairs={{0,16},{8,24},{16,0},{24,8},{1,17},{9,25},{17,1},{25,9},{2,18},{10... | collective-permute-start | bytes 1572872 | tf_op jit(solution)/shard_map/ppermute | solution.py:319
  85.0 19.0 %collective-permute-start.17 = (bf16[2,128,1024]{2,1,0:T(8,128)(2,1)S(1)}, bf16[2,128,1024]{2,1,0:T(8,128)(2,1)}, u32[]{:S(2)}, u32[]{:S(2)}) collective-permute-start(bf16[2,128,1024]{2,1,0:T(8,128)(2,1)S(1)} %collective-permute-done.16.refs_3_.refs_2_), channel_id=1, source_target_pairs={{0,8},{8,0},{16,24},{24,16},{1,9},{9,1},{17,25},{25,17},{2,10},{10... | collective-permute-start | bytes 1572872 | tf_op jit(solution)/shard_map/ppermute | solution.py:320
  96.4 14.6 %collective-permute-start.19 = (bf16[2,128,1024]{2,1,0:T(8,128)(2,1)S(1)}, bf16[2,128,1024]{2,1,0:T(8,128)(2,1)S(1)}, u32[]{:S(2)}, u32[]{:S(2)}) collective-permute-start(bf16[2,128,1024]{2,1,0:T(8,128)(2,1)S(1)} %collective-permute-done.18.refs_5_.refs_4_), channel_id=1, source_target_pairs={{0,8},{8,0},{16,24},{24,16},{1,9},{9,1},{17,25},{25,17},{2,10},{10... | collective-permute-start | bytes 1572872 | tf_op jit(solution)/shard_map/ppermute | solution.py:320
  101.7 12.7 %collective-permute-start.25 = (bf16[8,3,32,128]{3,2,1,0:T(8,128)(2,1)S(1)}, bf16[8,3,32,128]{3,2,1,0:T(8,128)(2,1)S(1)}, u32[]{:S(2)}, u32[]{:S(2)}) collective-permute-start(bf16[8,3,32,128]{3,2,1,0:T(8,128)(2,1)S(1)} %bitcast.107), channel_id=1, source_target_pairs={{0,4},{4,0},{1,5},{5,1},{2,6},{6,2},{3,7},{7,3},{8,12},{12,8},{9,1... | collective-permute-start | bytes 589832 | tf_op jit(solution)/shard_map/ppermute | solution.py:315
  102.1 13.9 %collective-permute-start.15 = (bf16[128,1024]{1,0:T(8,128)(2,1)S(1)}, bf16[128,1024]{1,0:T(8,128)(2,1)S(1)}, u32[]{:S(2)}, u32[]{:S(2)}) collective-permute-start(bf16[128,1024]{1,0:T(8,128)(2,1)S(1)} %get-tuple-element.120.first_ref.refs_0_), channel_id=1, source_target_pairs={{0,1},{1,0},{2,3},{3,2},{4,5},{5,4},{6,7},{7,6},{8,9},{9,8},{10,11... | collective-permute-start | bytes 786440 | tf_op jit(solution)/shard_map/ppermute | solution.py:325
  137.6 11.8 %collective-permute-start.29 = (bf16[128,1024]{1,0:T(8,128)(2,1)S(1)}, bf16[128,1024]{1,0:T(8,128)(2,1)S(1)}, u32[]{:S(2)}, u32[]{:S(2)}) collective-permute-start(bf16[128,1024]{1,0:T(8,128)(2,1)S(1)} %get-tuple-element.132.first_ref.refs_0_), channel_id=1, source_target_pairs={{0,1},{1,0},{2,3},{3,2},{4,5},{5,4},{6,7},{7,6},{8,9},{9,8},{10,11... | collective-permute-start | bytes 786440 | tf_op jit(solution)/shard_map/ppermute | solution.py:325
  170.1 9.4 %collective-permute-start.35 = (bf16[4,128,1024]{2,1,0:T(8,128)(2,1)S(1)}, bf16[4,128,1024]{2,1,0:T(8,128)(2,1)}, u32[]{:S(2)}, u32[]{:S(2)}) collective-permute-start(bf16[4,128,1024]{2,1,0:T(8,128)(2,1)S(1)} %get-tuple-element.147), channel_id=1, source_target_pairs={{0,8},{8,0},{16,24},{24,16},{1,9},{9,1},{17,25},{25,17},{2,10},{10... | collective-permute-start | bytes 3145736 | tf_op jit(solution)/shard_map/ppermute | solution.py:1008
  172.6 14.3 %collective-permute-start.37 = (bf16[2,128,1024]{2,1,0:T(8,128)(2,1)}, bf16[2,128,1024]{2,1,0:T(8,128)(2,1)}, u32[]{:S(2)}, u32[]{:S(2)}) collective-permute-start(bf16[2,128,1024]{2,1,0:T(8,128)(2,1)} %add_convert_fusion), channel_id=1, source_target_pairs={{0,16},{8,24},{16,0},{24,8},{1,17},{9,25},{17,1},{25,9},{2,18},{10... | collective-permute-start | bytes 1572872 | tf_op jit(solution)/shard_map/ppermute | solution.py:1004
  174.1 14.7 %collective-permute-start.38 = (bf16[128,1024]{1,0:T(8,128)(2,1)}, bf16[128,1024]{1,0:T(8,128)(2,1)}, u32[]{:S(2)}, u32[]{:S(2)}) collective-permute-start(bf16[128,1024]{1,0:T(8,128)(2,1)} %copy-done.27), channel_id=1, source_target_pairs={{0,4},{4,0},{1,5},{5,1},{2,6},{6,2},{3,7},{7,3},{8,12},{12,8},{9,1... | collective-permute-start | bytes 786440 | tf_op jit(solution)/shard_map/ppermute | solution.py:315
  175.2 13.8 %all-to-all-start.3 = ((bf16[8,128,128]{2,1,0:T(8,128)(2,1)}), bf16[8,128,128]{2,1,0:T(8,128)(2,1)}, u32[]{:S(2)}, u32[]{:S(2)}) async-start(bf16[8,128,128]{2,1,0:T(8,128)(2,1)} %get-tuple-element.143), calls=%async_computation.3 | async-start | bytes 524288 | tf_op jit(solution)/shard_map/all_to_all | solution.py:1000
  189.1 16.3 %collective-permute-start.54 = (bf16[128,1024]{1,0:T(8,128)(2,1)}, bf16[128,1024]{1,0:T(8,128)(2,1)S(1)}, u32[]{:S(2)}, u32[]{:S(2)}) collective-permute-start(bf16[128,1024]{1,0:T(8,128)(2,1)} %fusion.12), channel_id=1, source_target_pairs={{0,2},{2,0},{1,3},{3,1},{4,6},{6,4},{5,7},{7,5},{8,10},{10,8},{9,1... | collective-permute-start | bytes 786440 | tf_op jit(solution)/shard_map/ppermute | solution.py:1020
  198.5 10.7 %collective-permute-start.39 = (bf16[4,128,384]{2,1,0:T(8,128)(2,1)S(1)}, bf16[4,128,384]{2,1,0:T(8,128)(2,1)S(1)}, u32[]{:S(2)}, u32[]{:S(2)}) collective-permute-start(bf16[4,128,384]{2,1,0:T(8,128)(2,1)S(1)} %constant_dynamic-slice_fusion), channel_id=1, source_target_pairs={{0,4},{4,0},{1,5},{5,1},{2,6},{6,2},{3,7},{7,3},{8,12},{12,8},{9,1... | collective-permute-start | bytes 1179656 | tf_op jit(solution)/shard_map/ppermute | solution.py:315
  203.4 14.1 %collective-permute-start.44 = (bf16[2,272,384]{2,1,0:T(8,128)(2,1)S(1)}, bf16[2,272,384]{2,1,0:T(8,128)(2,1)S(1)}, u32[]{:S(2)}, u32[]{:S(2)}) collective-permute-start(bf16[2,272,384]{2,1,0:T(8,128)(2,1)S(1)} %get-tuple-element.172), channel_id=1, source_target_pairs={{0,8},{8,0},{16,24},{24,16},{1,9},{9,1},{17,25},{25,17},{2,10},{10... | collective-permute-start | bytes 1253384 | tf_op jit(solution)/shard_map/ppermute | solution.py:1050
  204.1 14.7 %collective-permute-start.41 = (bf16[2,128,1024]{2,1,0:T(8,128)(2,1)S(1)}, bf16[2,128,1024]{2,1,0:T(8,128)(2,1)S(1)}, u32[]{:S(2)}, u32[]{:S(2)}) collective-permute-start(bf16[2,128,1024]{2,1,0:T(8,128)(2,1)S(1)} %copy-done.45), channel_id=1, source_target_pairs={{0,16},{8,24},{16,0},{24,8},{1,17},{9,25},{17,1},{25,9},{2,18},{10... | collective-permute-start | bytes 1572872 | tf_op jit(solution)/shard_map/ppermute | solution.py:1019
  212.9 36.0 %collective-permute-start.40 = (bf16[2,128,1024]{2,1,0:T(8,128)(2,1)}, bf16[2,128,1024]{2,1,0:T(8,128)(2,1)}, u32[]{:S(2)}, u32[]{:S(2)}) collective-permute-start(bf16[2,128,1024]{2,1,0:T(8,128)(2,1)} %get-tuple-element.164), channel_id=1, source_target_pairs={{0,1},{1,0},{2,3},{3,2},{4,5},{5,4},{6,7},{7,6},{8,9},{9,8},{10,11... | collective-permute-start | bytes 1572872 | tf_op jit(solution)/shard_map/ppermute | solution.py:1063
  216.5 20.1 %collective-permute-start.51 = (bf16[4,32,1024]{2,1,0:T(8,128)(2,1)}, bf16[4,32,1024]{2,1,0:T(8,128)(2,1)}, u32[]{:S(2)}, u32[]{:S(2)}) collective-permute-start(bf16[4,32,1024]{2,1,0:T(8,128)(2,1)} %get-tuple-element.183), channel_id=1, source_target_pairs={{0,16},{8,24},{16,0},{24,8},{1,17},{9,25},{17,1},{25,9},{2,18},{10... | collective-permute-start | bytes 786440 | tf_op jit(solution)/shard_map/ppermute | solution.py:1072
  217.6 12.4 %collective-permute-start.45 = (bf16[272,384]{1,0:T(8,128)(2,1)S(1)}, bf16[272,384]{1,0:T(8,128)(2,1)S(1)}, u32[]{:S(2)}, u32[]{:S(2)}) collective-permute-start(bf16[272,384]{1,0:T(8,128)(2,1)S(1)} %get-tuple-element.188), channel_id=1, source_target_pairs={{0,16},{8,24},{16,0},{24,8},{1,17},{9,25},{17,1},{25,9},{2,18},{10... | collective-permute-start | bytes 626696 | tf_op jit(solution)/shard_map/ppermute | solution.py:1080
  220.7 19.2 %collective-permute-start.42 = (bf16[128,1024]{1,0:T(8,128)(2,1)}, bf16[128,1024]{1,0:T(8,128)(2,1)}, u32[]{:S(2)}, u32[]{:S(2)}) collective-permute-start(bf16[128,1024]{1,0:T(8,128)(2,1)} %fusion.14), channel_id=1, source_target_pairs={{0,2},{2,0},{1,3},{3,1},{4,6},{6,4},{5,7},{7,5},{8,10},{10,8},{9,1... | collective-permute-start | bytes 786440 | tf_op jit(solution)/shard_map/ppermute | solution.py:1039
  231.3 27.9 %all-to-all-start.4 = ((bf16[8,48,384]{2,1,0:T(8,128)(2,1)}), bf16[8,48,384]{2,1,0:T(8,128)(2,1)S(1)}, u32[]{:S(2)}, u32[]{:S(2)}) async-start(bf16[8,48,384]{2,1,0:T(8,128)(2,1)} %shard_map.156), calls=%async_computation.4 | async-start | bytes 589824 | tf_op jit(solution)/shard_map/all_to_all | solution.py:1092
  242.1 27.2 %collective-permute-start.55 = (bf16[2,128,1024]{2,1,0:T(8,128)(2,1)}, bf16[2,128,1024]{2,1,0:T(8,128)(2,1)}, u32[]{:S(2)}, u32[]{:S(2)}) collective-permute-start(bf16[2,128,1024]{2,1,0:T(8,128)(2,1)} %fusion.8), channel_id=1, source_target_pairs={{1,4},{3,6},{4,16},{5,20},{6,18},{7,22},{9,12},{11,14},{12,24},{13... | collective-permute-start | bytes 1572872 | tf_op jit(solution)/shard_map/ppermute | solution.py:1107
  246.6 12.0 %collective-permute-start.53 = (bf16[32,1024]{1,0:T(8,128)(2,1)S(1)}, bf16[32,1024]{1,0:T(8,128)(2,1)S(1)}, u32[]{:S(2)}, u32[]{:S(2)}) collective-permute-start(bf16[32,1024]{1,0:T(8,128)(2,1)S(1)} %fusion.19), channel_id=1, source_target_pairs={{0,2},{2,0},{1,3},{3,1},{4,6},{6,4},{5,7},{7,5},{8,10},{10,8},{9,1... | collective-permute-start | bytes 196616 | tf_op jit(solution)/shard_map/ppermute | solution.py:1078
  249.9 13.6 %collective-permute-start.43 = (bf16[128,1024]{1,0:T(8,128)(2,1)S(1)}, bf16[128,1024]{1,0:T(8,128)(2,1)}, u32[]{:S(2)}, u32[]{:S(2)}) collective-permute-start(bf16[128,1024]{1,0:T(8,128)(2,1)S(1)} %fusion.13), channel_id=1, source_target_pairs={{0,2},{2,0},{1,3},{3,1},{4,6},{6,4},{5,7},{7,5},{8,10},{10,8},{9,1... | collective-permute-start | bytes 786440 | tf_op jit(solution)/shard_map/ppermute | solution.py:1075
  (80 other events, 766.3 us)

commit v6 on v5

--- a/solution.py
+++ b/solution.py
@@ -1044,7 +1044,7 @@
         place, grad_cols, top_sums, mid_sums, back_parts[0][3], back_parts[1][3], *slots,
         scratch=[pltpu.VMEM((width, 3 * own), FULL), pltpu.VMEM((8, width), FULL)]
         + [pltpu.VMEM((seq_rows, width), LOW), pltpu.SemaphoreType.DMA((8,))],
-        flops=2 * 10**9,
+        vmem=56, flops=2 * 10**9,
         far_in=8,
     )
     sent = lax.ppermute(away, "seq", CORE)
@@ -1074,7 +1074,8 @@
     last_terms = after(add_low(near_terms[1], sent_terms[1]).astype(LOW), in_last)
     last_terms = lax.ppermute(last_terms, "blk", TWO_ON)
     out_rows = add_low(near_rows, sent_rows)
-    sent_rows = lax.ppermute(out_rows.reshape(2, 2, -1, width)[:, 1].astype(LOW), "blk", PAIRS)
+    odd_rows = after(out_rows.reshape(2, 2, -1, width)[:, 1].astype(LOW), sent_terms)
+    sent_rows = lax.ppermute(odd_rows, "blk", PAIRS)
     last_rows = lax.ppermute(add_low(out_rows[2], sent_rows[1]).astype(LOW), "blk", TWO_ON)
     grad_w_out = add_low(add_low(out_rows[0], sent_rows[0]), last_rows)
     far = lax.ppermute(add_low(near[1], sent[1]).astype(LOW), "seq", ACROSS)

time: 273 us -> 271 us (level)
  waiting for transfers between devices: 105 us -> 101 us
  transfers between devices with their start and end apart: 61 -> 61, of which waited for: 35 -> 33; matrix products, arithmetic and copies ran while one was open for 10% -> 9% of each run, Pallas kernels for 18% -> 19%
where the time goes in v6:
time: 271 us; the launch traced here: 269 us
  waiting for transfers between devices  101 us (37%)
  starting transfers between devices  75 us (28%)
  Pallas kernels  59.2 us (22%)
  other arithmetic  22 us (8%)
  local copies, waits for them, and re-layouts  10.8 us (4%)
    pallas_call x16, Pallas kernels, call(): pl.pallas_call(kernel, out_shape=outs, in_specs=[pl.BlockSpec(memory_spac...  59.2 us
    ppermute x12, waiting for transfers between devices, flip_head(): return lax.ppermute(value, 'head', FLIP)  23.8 us
    ppermute x12, starting transfers between devices, flip_head(): return lax.ppermute(value, 'head', FLIP)  14.4 us
    ppermute x2, waiting for transfers between devices, gather_four(): return [own, beside, across, lax.ppermute(across, 'blk', PAIRS)]  10.3 us
    ppermute x1, waiting for transfers between devices, grouped_body(): far = lax.ppermute(add_low(near[1], sent[1]).astype(LOW), 'seq', ACROSS)  8.32 us
    ppermute x1, waiting for transfers between devices, grouped_body(): lax.ppermute(add_low(out_rows[2], sent_rows[1]).astype(LOW), 'blk', TWO_ON)  7.49 us
    all_to_all x1, starting transfers between devices, grouped_body(): swapped = lax.all_to_all(to_swap, GROUP, 0, 0, tiled=True)  6.34 us
    ppermute x1, waiting for transfers between devices, grouped_body(): lax.ppermute(add_low(out_near_grad[2:], out_sent[2:]).astype(LOW), 'seq',...  5.46 us
  transfers between devices with their start and end apart: 61, of which 33 were waited for; matrix products, arithmetic and copies ran while one was open for 9% of the time, Pallas kernels for 19%

profile of v6, /device:TPU:2, one launch (start us, length us, event | category | flops | bytes accessed | tf_op | source)
XLA Modules:
  0.0 269.4 jit_solution(11626465941265693797)
XLA Ops:
  11.7 6.3 %all-to-all-start = ((bf16[8,112,128]{2,1,0:T(8,128)(2,1)}), bf16[8,112,128]{2,1,0:T(8,128)(2,1)S(1)}, u32[]{:S(2)}, u32[]{:S(2)}) async-start(bf16[8,112,128]{2,1,0:T(8,128)(2,1)} %maximum_maximum_fusion), calls=%async_computation | async-start | bytes 458752 | tf_op jit(solution)/shard_map/all_to_all | solution.py:839
  23.4 4.4 %collective-permute-done.5.refs_10_ = bf16[128,1024]{1,0:T(8,128)(2,1)} collective-permute-done((bf16[128,1024]{1,0:T(8,128)(2,1)}, bf16[128,1024]{1,0:T(8,128)(2,1)}, u32[]{:S(2)}, u32[]{:S(2)}) %collective-permute-start.5) | collective-permute-done | bytes 262176 | tf_op jit(solution)/shard_map/ppermute | solution.py:315
  27.7 3.4 %collective-permute-done.4 = bf16[128,1024]{1,0:T(8,128)(2,1)S(1)} collective-permute-done((bf16[128,1024]{1,0:T(8,128)(2,1)S(1)}, bf16[128,1024]{1,0:T(8,128)(2,1)S(1)}, u32[]{:S(2)}, u32[]{:S(2)}) %collective-permute-start.4) | collective-permute-done | bytes 262176 | tf_op jit(solution)/shard_map/ppermute | solution.py:837
  32.2 4.1 %all-to-all-start.1 = ((bf16[8,256,128]{2,1,0:T(8,128)(2,1)}), bf16[8,256,128]{2,1,0:T(8,128)(2,1)}, u32[]{:S(2)}, u32[]{:S(2)}) async-start(bf16[8,256,128]{2,1,0:T(8,128)(2,1)} %broadcast_in_dim.19), calls=%async_computation.1 | async-start | bytes 1048576 | tf_op jit(solution)/shard_map/all_to_all | solution.py:843
  41.2 5.1 %collective-permute-done.8.refs_3_ = bf16[8,3,32,128]{3,2,1,0:T(8,128)(2,1)S(1)} collective-permute-done((bf16[8,3,32,128]{3,2,1,0:T(8,128)(2,1)S(1)}, bf16[8,3,32,128]{3,2,1,0:T(8,128)(2,1)S(1)}, u32[]{:S(2)}, u32[]{:S(2)}) %collective-permute-start.8) | collective-permute-done | bytes 196640 | tf_op jit(solution)/shard_map/ppermute | solution.py:848
  47.7 3.9 %collective-permute-done.6 = bf16[128,1024]{1,0:T(8,128)(2,1)S(1)} collective-permute-done((bf16[128,1024]{1,0:T(8,128)(2,1)S(1)}, bf16[128,1024]{1,0:T(8,128)(2,1)S(1)}, u32[]{:S(2)}, u32[]{:S(2)}) %collective-permute-start.6) | collective-permute-done | bytes 262176 | tf_op jit(solution)/shard_map/ppermute | solution.py:844
  55.2 3.2 %collective-permute-done.9.refs_12_ = bf16[128,1024]{1,0:T(8,128)(2,1)} collective-permute-done((bf16[128,1024]{1,0:T(8,128)(2,1)S(1)}, bf16[128,1024]{1,0:T(8,128)(2,1)}, u32[]{:S(2)}, u32[]{:S(2)}) %collective-permute-start.9) | collective-permute-done | bytes 262176 | tf_op jit(solution)/shard_map/ppermute | solution.py:315
  61.2 11.2 %shard_map.143 = (bf16[8,128,128]{2,1,0:T(8,128)(2,1)}, bf16[1024,128]{1,0:T(8,128)(2,1)}, bf16[1024,128]{1,0:T(8,128)(2,1)}, bf16[1024,128]{1,0:T(8,128)(2,1)},...) custom-call(s32[9]{0:T(128)} %stack.57.place, ...), custom_call_target="tpu_custom_call" | custom-call | flops 4000000000 | bytes 9962496 | tf_op jit(solution)/shard_map/pallas_call | solution.py:343
  73.0 5.0 %all-to-all-start.2 = ((bf16[8,128,128]{2,1,0:T(8,128)(2,1)}), bf16[8,128,128]{2,1,0:T(8,128)(2,1)S(1)}, u32[]{:S(2)}, u32[]{:S(2)}) async-start(bf16[8,128,128]{2,1,0:T(8,128)(2,1)} %get-tuple-element.118), calls=%async_computation.2 | async-start | bytes 524288 | tf_op jit(solution)/shard_map/all_to_all | solution.py:887
  78.0 3.7 %collective-permute-done.16.refs_3_.refs_2_ = bf16[2,128,1024]{2,1,0:T(8,128)(2,1)S(1)} collective-permute-done((bf16[2,128,1024]{2,1,0:T(8,128)(2,1)S(1)}, bf16[2,128,1024]{2,1,0:T(8,128)(2,1)S(1)}, u32[]{:S(2)}, u32[]{:S(2)}) %collective-permute-start.16) | collective-permute-done | bytes 524320 | tf_op jit(solution)/shard_map/ppermute | solution.py:863
  84.1 4.3 %all-to-all-done.2.context_ref = bf16[8,128,128]{2,1,0:T(8,128)(2,1)S(1)} async-done(((bf16[8,128,128]{2,1,0:T(8,128)(2,1)}), bf16[8,128,128]{2,1,0:T(8,128)(2,1)S(1)}, u32[]{:S(2)}, u32[]{:S(2)}) %all-to-all-start.2) | async-done | bytes 262176 | tf_op jit(solution)/shard_map/all_to_all | solution.py:887
  92.6 2.9 %collective-permute-done.18.refs_5_.refs_4_ = bf16[2,128,1024]{2,1,0:T(8,128)(2,1)S(1)} collective-permute-done((bf16[2,128,1024]{2,1,0:T(8,128)(2,1)S(1)}, bf16[2,128,1024]{2,1,0:T(8,128)(2,1)S(1)}, u32[]{:S(2)}, u32[]{:S(2)}) %collective-permute-start.18) | collective-permute-done | bytes 524320 | tf_op jit(solution)/shard_map/ppermute | solution.py:319
  95.5 3.1 %collective-permute-done.21.first_ref.refs_2_ = bf16[128,1024]{1,0:T(8,128)(2,1)S(1)} collective-permute-done((bf16[128,1024]{1,0:T(8,128)(2,1)S(1)}, bf16[128,1024]{1,0:T(8,128)(2,1)S(1)}, u32[]{:S(2)}, u32[]{:S(2)}) %collective-permute-start.21) | collective-permute-done | bytes 262176 | tf_op jit(solution)/shard_map/ppermute | solution.py:315
  101.0 6.3 %collective-permute-done.22.second_ref.refs_3_ = bf16[128,1024]{1,0:T(8,128)(2,1)S(1)} collective-permute-done((bf16[128,1024]{1,0:T(8,128)(2,1)S(1)}, bf16[128,1024]{1,0:T(8,128)(2,1)S(1)}, u32[]{:S(2)}, u32[]{:S(2)}) %collective-permute-start.22) | collective-permute-done | bytes 262176 | tf_op jit(solution)/shard_map/ppermute | solution.py:326
  107.3 3.4 %shard_map.146 = (f32[256,1024]{1,0:T(8,128)S(1)}, bf16[256,1024]{1,0:T(8,128)(2,1)S(1)}, f32[128,1024]{1,0:T(8,128)S(1)}, bf16[128,1024]{1,0:T(8,128)(2,1)S(1)}) custom-call(s32[9]{0:T(128)S(1)} %copy-done.10, bf16[128,1024]{1,0:T(8,128)(2,1)S(1)} %collective-permute-done.21.first_ref.refs_2_, ...), custom_call_target="tpu_custom_call" | custom-call | flops 1500000000 | bytes 7094272 | tf_op jit(solution)/shard_map/pallas_call | solution.py:343
  112.9 3.4 %shard_map.145 = (f32[256,1024]{1,0:T(8,128)S(1)}, bf16[256,1024]{1,0:T(8,128)(2,1)S(1)}, f32[128,1024]{1,0:T(8,128)S(1)}, bf16[128,1024]{1,0:T(8,128)(2,1)S(1)}) custom-call(s32[9]{0:T(128)S(1)} %copy-done.10, bf16[128,1024]{1,0:T(8,128)(2,1)S(1)} %get-tuple-element.121.first_ref.refs_0_, bf16[128,1024]{1,0:T(8,128)(2,1)S(1)} %collective-permute-done.15.second_ref.refs_1_, ...), custom_call_target="tpu_custom_call" | custom-call | flops 1500000000 | bytes 7094272 | tf_op jit(solution)/shard_map/pallas_call | solution.py:343
  127.7 5.9 %collective-permute-done.31.first_ref.refs_2_ = bf16[128,1024]{1,0:T(8,128)(2,1)S(1)} collective-permute-done((bf16[128,1024]{1,0:T(8,128)(2,1)S(1)}, bf16[128,1024]{1,0:T(8,128)(2,1)S(1)}, u32[]{:S(2)}, u32[]{:S(2)}) %collective-permute-start.31) | collective-permute-done | bytes 262176 | tf_op jit(solution)/shard_map/ppermute | solution.py:315
  136.1 4.0 %collective-permute-done.32.second_ref.refs_3_ = bf16[128,1024]{1,0:T(8,128)(2,1)S(1)} collective-permute-done((bf16[128,1024]{1,0:T(8,128)(2,1)S(1)}, bf16[128,1024]{1,0:T(8,128)(2,1)S(1)}, u32[]{:S(2)}, u32[]{:S(2)}) %collective-permute-start.32) | collective-permute-done | bytes 262176 | tf_op jit(solution)/shard_map/ppermute | solution.py:326
  140.1 3.3 %shard_map.149 = (bf16[256,1024]{1,0:T(8,128)(2,1)S(1)}, f32[128,1024]{1,0:T(8,128)S(1)}, bf16[128,1024]{1,0:T(8,128)(2,1)S(1)}, f32[8,1,128]{2,1,0:T(1,128)S(1)}) custom-call(s32[9]{0:T(128)S(1)} %copy-done.10, bf16[128,1024]{1,0:T(8,128)(2,1)S(1)} %collective-permute-done.31.first_ref.refs_2_, ...), custom_call_target="tpu_custom_call" | custom-call | flops 1500000000 | bytes 7081984 | tf_op jit(solution)/shard_map/pallas_call | solution.py:343
  145.7 3.5 %shard_map.148 = (bf16[256,1024]{1,0:T(8,128)(2,1)S(1)}, f32[128,1024]{1,0:T(8,128)S(1)}, bf16[128,1024]{1,0:T(8,128)(2,1)S(1)}, f32[8,1,128]{2,1,0:T(1,128)S(1)}) custom-call(s32[9]{0:T(128)S(1)} %copy-done.10, bf16[128,1024]{1,0:T(8,128)(2,1)S(1)} %get-tuple-element.133.first_ref.refs_0_, bf16[128,1024]{1,0:T(8,128)(2,1)S(1)} %collective-permute-done.29.second_ref.refs_1_, ...), custom_call_target="tpu_custom_call" | custom-call | flops 1500000000 | bytes 7081984 | tf_op jit(solution)/shard_map/pallas_call | solution.py:343
  152.5 3.2 %collective-permute-done.30.sent_ref = bf16[128,1024]{1,0:T(8,128)(2,1)S(1)} collective-permute-done((bf16[128,1024]{1,0:T(8,128)(2,1)S(1)}, bf16[128,1024]{1,0:T(8,128)(2,1)S(1)}, u32[]{:S(2)}, u32[]{:S(2)}) %collective-permute-start.30) | collective-permute-done | bytes 262176 | tf_op jit(solution)/shard_map/ppermute | solution.py:950
  157.8 3.7 %shard_map.150 = (f32[128,1024]{1,0:T(8,128)S(1)}, bf16[128,1024]{1,0:T(8,128)(2,1)S(1)}, bf16[8,128,128]{2,1,0:T(8,128)(2,1)}, f32[3,1024]{1,0:T(4,128)S(1)}) custom-call(s32[9]{0:T(128)S(1)} %copy-done.10, f32[128,1024]{1,0:T(8,128)S(1)} %get-tuple-element.135.near_ref, bf16[128,1024]{1,0:T(8,128)(2,1)S(1)} %collective-permute-done.30.sent_ref, ...), custom_call_target="tpu_custom_call" | custom-call | flops 1000000000 | bytes 5288448 | tf_op jit(solution)/shard_map/pallas_call | solution.py:343
  171.5 4.3 %all-to-all-start.3 = ((bf16[8,128,128]{2,1,0:T(8,128)(2,1)}), bf16[8,128,128]{2,1,0:T(8,128)(2,1)}, u32[]{:S(2)}, u32[]{:S(2)}) async-start(bf16[8,128,128]{2,1,0:T(8,128)(2,1)} %get-tuple-element.144), calls=%async_computation.3 | async-start | bytes 524288 | tf_op jit(solution)/shard_map/all_to_all | solution.py:1000
  177.8 5.5 %collective-permute-done.37 = bf16[2,128,1024]{2,1,0:T(8,128)(2,1)} collective-permute-done((bf16[2,128,1024]{2,1,0:T(8,128)(2,1)}, bf16[2,128,1024]{2,1,0:T(8,128)(2,1)}, u32[]{:S(2)}, u32[]{:S(2)}) %collective-permute-start.37) | collective-permute-done | bytes 524320 | tf_op jit(solution)/shard_map/ppermute | solution.py:1004
  186.9 8.2 %shard_map.153.own_ref.refs_0_ = bf16[8,128,384]{2,1,0:T(8,128)(2,1)} custom-call(s32[9]{0:T(128)} %stack.57.place, bf16[8,128,128]{2,1,0:T(8,128)(2,1)} %all-to-all-done.3.grad_ref, bf16[1024,128]{1,0:T(8,128)(2,1)} %get-tuple-element.157.refs_0_, bf16[1024,128]{1,0:T(8,128)(2,1)} %get-tuple-element.158.refs_1_, ...), custom_call_target="tpu_custom_call" | custom-call | flops 4000000000 | bytes 7077888 | tf_op jit(solution)/shard_map/pallas_call | solution.py:343
  197.4 5.0 %shard_map.155 = (f32[2,272,384]{2,1,0:T(8,128)}, bf16[2,272,384]{2,1,0:T(8,128)(2,1)}) custom-call(s32[9]{0:T(128)} %stack.57.place, bf16[8,128,384]{2,1,0:T(8,128)(2,1)} %shard_map.153.own_ref.refs_0_, f32[3,1024]{1,0:T(4,128)} %copy-done.23, f32[3,1024]{1,0:T(4,128)} %copy-done.24, f32[8,1,128]{2,1,0:T(1,128)} %copy-done.26, f32[8,1,128]{2,1,0:T(1,128)} %copy-done.25, ...), custom_call_target="tpu_custom_call" | custom-call | flops 1000000000 | bytes 4169728 | tf_op jit(solution)/shard_map/pallas_call | solution.py:343
  209.0 3.3 %shard_map.154 = (f32[2,128,1024]{2,1,0:T(8,128)S(1)}, bf16[2,128,1024]{2,1,0:T(8,128)(2,1)}) custom-call(s32[9]{0:T(128)S(1)} %copy-done.11, bf16[4,128,384]{2,1,0:T(8,128)(2,1)S(1)} %collective-permute-done.39.across_ref, bf16[8,128,384]{2,1,0:T(8,128)(2,1)S(1)} %copy-done.9, bf16[1024,384]{1,0:T(8,128)(2,1)S(1)} %copy-done.27, ...), custom_call_target="tpu_custom_call" | custom-call | flops 1000000000 | bytes 4325376 | tf_op jit(solution)/shard_map/pallas_call | solution.py:343
  213.1 3.0 %shard_map.158 = (f32[4,32,1024]{2,1,0:T(8,128)S(1)}, bf16[4,32,1024]{2,1,0:T(8,128)(2,1)}) custom-call(s32[9]{0:T(128)S(1)} %copy-done.11, bf16[2,128,128]{2,1,0:T(8,128)(2,1)S(1)} %get-tuple-element.197.refs_0_, bf16[2,128,128]{2,1,0:T(8,128)(2,1)S(1)} %collective-permute-done.46.refs_1_, bf16[2,128,128]{2,1,0:T(8,128)(2,1)S(1)} %collective-permute-done.47.refs_2_, ...), custom_call_target="tpu_custom_call" | custom-call | flops 500000000 | bytes 2097152 | tf_op jit(solution)/shard_map/pallas_call | solution.py:343
  221.2 8.3 %collective-permute-done.45.far_ref = bf16[272,384]{1,0:T(8,128)(2,1)S(1)} collective-permute-done((bf16[272,384]{1,0:T(8,128)(2,1)S(1)}, bf16[272,384]{1,0:T(8,128)(2,1)S(1)}, u32[]{:S(2)}, u32[]{:S(2)}) %collective-permute-start.45) | collective-permute-done | bytes 208928 | tf_op jit(solution)/shard_map/ppermute | solution.py:1081
  230.8 3.4 %all-to-all-start.4 = ((bf16[8,48,384]{2,1,0:T(8,128)(2,1)}), bf16[8,48,384]{2,1,0:T(8,128)(2,1)S(1)}, u32[]{:S(2)}, u32[]{:S(2)}) async-start(bf16[8,48,384]{2,1,0:T(8,128)(2,1)} %shard_map.156), calls=%async_computation.4 | async-start | bytes 589824 | tf_op jit(solution)/shard_map/all_to_all | solution.py:1093
  248.8 7.5 %collective-permute-done.53 = bf16[32,1024]{1,0:T(8,128)(2,1)S(1)} collective-permute-done((bf16[32,1024]{1,0:T(8,128)(2,1)S(1)}, bf16[32,1024]{1,0:T(8,128)(2,1)S(1)}, u32[]{:S(2)}, u32[]{:S(2)}) %collective-permute-start.53) | collective-permute-done | bytes 65568 | tf_op jit(solution)/shard_map/ppermute | solution.py:1079
  263.6 3.5 %collective-permute-done.55 = bf16[2,128,1024]{2,1,0:T(8,128)(2,1)} collective-permute-done((bf16[2,128,1024]{2,1,0:T(8,128)(2,1)}, bf16[2,128,1024]{2,1,0:T(8,128)(2,1)}, u32[]{:S(2)}, u32[]{:S(2)}) %collective-permute-start.55) | collective-permute-done | bytes 524320 | tf_op jit(solution)/shard_map/ppermute | solution.py:1108
  (240 shorter events, 118.6 us)
Async XLA Ops:
  11.7 19.4 %all-to-all-start = ((bf16[8,112,128]{2,1,0:T(8,128)(2,1)}), bf16[8,112,128]{2,1,0:T(8,128)(2,1)S(1)}, u32[]{:S(2)}, u32[]{:S(2)}) async-start(bf16[8,112,128]{2,1,0:T(8,128)(2,1)} %maximum_maximum_fusion), calls=%async_computation | async-start | bytes 458752 | tf_op jit(solution)/shard_map/all_to_all | solution.py:839
  21.0 10.2 %collective-permute-start.4 = (bf16[128,1024]{1,0:T(8,128)(2,1)S(1)}, bf16[128,1024]{1,0:T(8,128)(2,1)S(1)}, u32[]{:S(2)}, u32[]{:S(2)}) collective-permute-start(bf16[128,1024]{1,0:T(8,128)(2,1)S(1)} %collective-permute-done.1), channel_id=1, source_target_pairs={{1,0},{2,3},{5,4},{6,7},{9,8},{10,11},{13,12},{14,15},{17,16},{18,... | collective-permute-start | bytes 786440 | tf_op jit(solution)/shard_map/ppermute | solution.py:837
  32.2 26.3 %all-to-all-start.1 = ((bf16[8,256,128]{2,1,0:T(8,128)(2,1)}), bf16[8,256,128]{2,1,0:T(8,128)(2,1)}, u32[]{:S(2)}, u32[]{:S(2)}) async-start(bf16[8,256,128]{2,1,0:T(8,128)(2,1)} %broadcast_in_dim.19), calls=%async_computation.1 | async-start | bytes 1048576 | tf_op jit(solution)/shard_map/all_to_all | solution.py:843
  37.3 9.4 %collective-permute-start.7 = (bf16[128,1024]{1,0:T(8,128)(2,1)S(1)}, bf16[128,1024]{1,0:T(8,128)(2,1)S(1)}, u32[]{:S(2)}, u32[]{:S(2)}) collective-permute-start(bf16[128,1024]{1,0:T(8,128)(2,1)S(1)} %broadcast_select_fusion.1.refs_7_), channel_id=1, source_target_pairs={{0,4},{4,0},{1,5},{5,1},{2,6},{6,2},{3,7},{7,3},{8,12},{12,8},{9,1... | collective-permute-start | bytes 786440 | tf_op jit(solution)/shard_map/ppermute | solution.py:315
  39.3 12.3 %collective-permute-start.6 = (bf16[128,1024]{1,0:T(8,128)(2,1)S(1)}, bf16[128,1024]{1,0:T(8,128)(2,1)S(1)}, u32[]{:S(2)}, u32[]{:S(2)}) collective-permute-start(bf16[128,1024]{1,0:T(8,128)(2,1)S(1)} %collective-permute-done.3), channel_id=1, source_target_pairs={{1,0},{2,3},{5,4},{6,7},{9,8},{10,11},{13,12},{14,15},{17,16},{18,... | collective-permute-start | bytes 786440 | tf_op jit(solution)/shard_map/ppermute | solution.py:844
  58.5 13.9 %collective-permute-start.12 = (bf16[8,2,128,128]{3,2,1,0:T(8,128)(2,1)}, bf16[8,2,128,128]{3,2,1,0:T(8,128)(2,1)}, u32[]{:S(2)}, u32[]{:S(2)}) collective-permute-start(bf16[8,2,128,128]{3,2,1,0:T(8,128)(2,1)} %bitcast.18.refs_0_), channel_id=1, source_target_pairs={{0,16},{8,24},{16,0},{24,8},{1,17},{9,25},{17,1},{25,9},{2,18},{10... | collective-permute-start | bytes 1572872 | tf_op jit(solution)/shard_map/ppermute | solution.py:883
  59.1 22.6 %collective-permute-start.16 = (bf16[2,128,1024]{2,1,0:T(8,128)(2,1)S(1)}, bf16[2,128,1024]{2,1,0:T(8,128)(2,1)S(1)}, u32[]{:S(2)}, u32[]{:S(2)}) collective-permute-start(bf16[2,128,1024]{2,1,0:T(8,128)(2,1)S(1)} %pad_maximum_fusion.1), channel_id=1, source_target_pairs={{0,2},{2,0},{1,3},{3,1},{4,6},{6,4},{5,7},{7,5},{8,10},{10,8},{9,1... | collective-permute-start | bytes 1572872 | tf_op jit(solution)/shard_map/ppermute | solution.py:863
  72.4 15.9 %collective-permute-start.13 = (bf16[8,2,128,128]{3,2,1,0:T(8,128)(2,1)}, bf16[8,2,128,128]{3,2,1,0:T(8,128)(2,1)}, u32[]{:S(2)}, u32[]{:S(2)}) collective-permute-start(bf16[8,2,128,128]{3,2,1,0:T(8,128)(2,1)} %bitcast.18.refs_0_), channel_id=1, source_target_pairs={{0,8},{8,0},{16,24},{24,16},{1,9},{9,1},{17,25},{25,17},{2,10},{10... | collective-permute-start | bytes 1572872 | tf_op jit(solution)/shard_map/ppermute | solution.py:885
  72.5 15.9 %collective-permute-start.14 = (bf16[8,2,128,128]{3,2,1,0:T(8,128)(2,1)}, bf16[8,2,128,128]{3,2,1,0:T(8,128)(2,1)}, u32[]{:S(2)}, u32[]{:S(2)}) collective-permute-start(bf16[8,2,128,128]{3,2,1,0:T(8,128)(2,1)} %collective-permute-done.12.refs_2_), channel_id=1, source_target_pairs={{0,8},{8,0},{16,24},{24,16},{1,9},{9,1},{17,25},{25,17},{2,10},{10... | collective-permute-start | bytes 1572872 | tf_op jit(solution)/shard_map/ppermute | solution.py:886
  73.0 15.4 %all-to-all-start.2 = ((bf16[8,128,128]{2,1,0:T(8,128)(2,1)}), bf16[8,128,128]{2,1,0:T(8,128)(2,1)S(1)}, u32[]{:S(2)}, u32[]{:S(2)}) async-start(bf16[8,128,128]{2,1,0:T(8,128)(2,1)} %get-tuple-element.118), calls=%async_computation.2 | async-start | bytes 524288 | tf_op jit(solution)/shard_map/all_to_all | solution.py:887
  81.7 13.7 %collective-permute-start.18 = (bf16[2,128,1024]{2,1,0:T(8,128)(2,1)S(1)}, bf16[2,128,1024]{2,1,0:T(8,128)(2,1)S(1)}, u32[]{:S(2)}, u32[]{:S(2)}) collective-permute-start(bf16[2,128,1024]{2,1,0:T(8,128)(2,1)S(1)} %collective-permute-done.16.refs_3_.refs_2_), channel_id=1, source_target_pairs={{0,16},{8,24},{16,0},{24,8},{1,17},{9,25},{17,1},{25,9},{2,18},{10... | collective-permute-start | bytes 1572872 | tf_op jit(solution)/shard_map/ppermute | solution.py:319
  84.0 17.0 %collective-permute-start.17 = (bf16[2,128,1024]{2,1,0:T(8,128)(2,1)S(1)}, bf16[2,128,1024]{2,1,0:T(8,128)(2,1)}, u32[]{:S(2)}, u32[]{:S(2)}) collective-permute-start(bf16[2,128,1024]{2,1,0:T(8,128)(2,1)S(1)} %collective-permute-done.16.refs_3_.refs_2_), channel_id=1, source_target_pairs={{0,8},{8,0},{16,24},{24,16},{1,9},{9,1},{17,25},{25,17},{2,10},{10... | collective-permute-start | bytes 1572872 | tf_op jit(solution)/shard_map/ppermute | solution.py:320
  95.5 11.8 %collective-permute-start.19 = (bf16[2,128,1024]{2,1,0:T(8,128)(2,1)S(1)}, bf16[2,128,1024]{2,1,0:T(8,128)(2,1)S(1)}, u32[]{:S(2)}, u32[]{:S(2)}) collective-permute-start(bf16[2,128,1024]{2,1,0:T(8,128)(2,1)S(1)} %collective-permute-done.18.refs_5_.refs_4_), channel_id=1, source_target_pairs={{0,8},{8,0},{16,24},{24,16},{1,9},{9,1},{17,25},{25,17},{2,10},{10... | collective-permute-start | bytes 1572872 | tf_op jit(solution)/shard_map/ppermute | solution.py:320
  98.7 12.7 %collective-permute-start.25 = (bf16[8,3,32,128]{3,2,1,0:T(8,128)(2,1)S(1)}, bf16[8,3,32,128]{3,2,1,0:T(8,128)(2,1)S(1)}, u32[]{:S(2)}, u32[]{:S(2)}) collective-permute-start(bf16[8,3,32,128]{3,2,1,0:T(8,128)(2,1)S(1)} %bitcast.107), channel_id=1, source_target_pairs={{0,4},{4,0},{1,5},{5,1},{2,6},{6,2},{3,7},{7,3},{8,12},{12,8},{9,1... | collective-permute-start | bytes 589832 | tf_op jit(solution)/shard_map/ppermute | solution.py:315
  100.4 12.5 %collective-permute-start.15 = (bf16[128,1024]{1,0:T(8,128)(2,1)S(1)}, bf16[128,1024]{1,0:T(8,128)(2,1)S(1)}, u32[]{:S(2)}, u32[]{:S(2)}) collective-permute-start(bf16[128,1024]{1,0:T(8,128)(2,1)S(1)} %get-tuple-element.121.first_ref.refs_0_), channel_id=1, source_target_pairs={{0,1},{1,0},{2,3},{3,2},{4,5},{5,4},{6,7},{7,6},{8,9},{9,8},{10,11... | collective-permute-start | bytes 786440 | tf_op jit(solution)/shard_map/ppermute | solution.py:325
  135.2 10.5 %collective-permute-start.29 = (bf16[128,1024]{1,0:T(8,128)(2,1)S(1)}, bf16[128,1024]{1,0:T(8,128)(2,1)S(1)}, u32[]{:S(2)}, u32[]{:S(2)}) collective-permute-start(bf16[128,1024]{1,0:T(8,128)(2,1)S(1)} %get-tuple-element.133.first_ref.refs_0_), channel_id=1, source_target_pairs={{0,1},{1,0},{2,3},{3,2},{4,5},{5,4},{6,7},{7,6},{8,9},{9,8},{10,11... | collective-permute-start | bytes 786440 | tf_op jit(solution)/shard_map/ppermute | solution.py:325
  166.5 9.3 %collective-permute-start.35 = (bf16[4,128,1024]{2,1,0:T(8,128)(2,1)S(1)}, bf16[4,128,1024]{2,1,0:T(8,128)(2,1)}, u32[]{:S(2)}, u32[]{:S(2)}) collective-permute-start(bf16[4,128,1024]{2,1,0:T(8,128)(2,1)S(1)} %get-tuple-element.148), channel_id=1, source_target_pairs={{0,8},{8,0},{16,24},{24,16},{1,9},{9,1},{17,25},{25,17},{2,10},{10... | collective-permute-start | bytes 3145736 | tf_op jit(solution)/shard_map/ppermute | solution.py:1008
  169.0 14.3 %collective-permute-start.37 = (bf16[2,128,1024]{2,1,0:T(8,128)(2,1)}, bf16[2,128,1024]{2,1,0:T(8,128)(2,1)}, u32[]{:S(2)}, u32[]{:S(2)}) collective-permute-start(bf16[2,128,1024]{2,1,0:T(8,128)(2,1)} %add_convert_fusion), channel_id=1, source_target_pairs={{0,16},{8,24},{16,0},{24,8},{1,17},{9,25},{17,1},{25,9},{2,18},{10... | collective-permute-start | bytes 1572872 | tf_op jit(solution)/shard_map/ppermute | solution.py:1004
  170.6 13.9 %collective-permute-start.38 = (bf16[128,1024]{1,0:T(8,128)(2,1)}, bf16[128,1024]{1,0:T(8,128)(2,1)}, u32[]{:S(2)}, u32[]{:S(2)}) collective-permute-start(bf16[128,1024]{1,0:T(8,128)(2,1)} %copy-done.13), channel_id=1, source_target_pairs={{0,4},{4,0},{1,5},{5,1},{2,6},{6,2},{3,7},{7,3},{8,12},{12,8},{9,1... | collective-permute-start | bytes 786440 | tf_op jit(solution)/shard_map/ppermute | solution.py:315
  171.5 14.1 %all-to-all-start.3 = ((bf16[8,128,128]{2,1,0:T(8,128)(2,1)}), bf16[8,128,128]{2,1,0:T(8,128)(2,1)}, u32[]{:S(2)}, u32[]{:S(2)}) async-start(bf16[8,128,128]{2,1,0:T(8,128)(2,1)} %get-tuple-element.144), calls=%async_computation.3 | async-start | bytes 524288 | tf_op jit(solution)/shard_map/all_to_all | solution.py:1000
  185.6 19.3 %collective-permute-start.54 = (bf16[128,1024]{1,0:T(8,128)(2,1)S(1)}, bf16[128,1024]{1,0:T(8,128)(2,1)S(1)}, u32[]{:S(2)}, u32[]{:S(2)}) collective-permute-start(bf16[128,1024]{1,0:T(8,128)(2,1)S(1)} %fusion.12), channel_id=1, source_target_pairs={{0,2},{2,0},{1,3},{3,1},{4,6},{6,4},{5,7},{7,5},{8,10},{10,8},{9,1... | collective-permute-start | bytes 786440 | tf_op jit(solution)/shard_map/ppermute | solution.py:1020
  196.2 12.2 %collective-permute-start.39 = (bf16[4,128,384]{2,1,0:T(8,128)(2,1)S(1)}, bf16[4,128,384]{2,1,0:T(8,128)(2,1)S(1)}, u32[]{:S(2)}, u32[]{:S(2)}) collective-permute-start(bf16[4,128,384]{2,1,0:T(8,128)(2,1)S(1)} %constant_dynamic-slice_fusion), channel_id=1, source_target_pairs={{0,4},{4,0},{1,5},{5,1},{2,6},{6,2},{3,7},{7,3},{8,12},{12,8},{9,1... | collective-permute-start | bytes 1179656 | tf_op jit(solution)/shard_map/ppermute | solution.py:315
  202.4 14.6 %collective-permute-start.44 = (bf16[2,272,384]{2,1,0:T(8,128)(2,1)}, bf16[2,272,384]{2,1,0:T(8,128)(2,1)S(1)}, u32[]{:S(2)}, u32[]{:S(2)}) collective-permute-start(bf16[2,272,384]{2,1,0:T(8,128)(2,1)} %get-tuple-element.173), channel_id=1, source_target_pairs={{0,8},{8,0},{16,24},{24,16},{1,9},{9,1},{17,25},{25,17},{2,10},{10... | collective-permute-start | bytes 1253384 | tf_op jit(solution)/shard_map/ppermute | solution.py:1050
  203.1 15.2 %collective-permute-start.41 = (bf16[2,128,1024]{2,1,0:T(8,128)(2,1)}, bf16[2,128,1024]{2,1,0:T(8,128)(2,1)S(1)}, u32[]{:S(2)}, u32[]{:S(2)}) collective-permute-start(bf16[2,128,1024]{2,1,0:T(8,128)(2,1)} %add_convert_fusion.1), channel_id=1, source_target_pairs={{0,16},{8,24},{16,0},{24,8},{1,17},{9,25},{17,1},{25,9},{2,18},{10... | collective-permute-start | bytes 1572872 | tf_op jit(solution)/shard_map/ppermute | solution.py:1019
  212.3 23.2 %collective-permute-start.40 = (bf16[2,128,1024]{2,1,0:T(8,128)(2,1)}, bf16[2,128,1024]{2,1,0:T(8,128)(2,1)}, u32[]{:S(2)}, u32[]{:S(2)}) collective-permute-start(bf16[2,128,1024]{2,1,0:T(8,128)(2,1)} %get-tuple-element.165), channel_id=1, source_target_pairs={{0,1},{1,0},{2,3},{3,2},{4,5},{5,4},{6,7},{7,6},{8,9},{9,8},{10,11... | collective-permute-start | bytes 1572872 | tf_op jit(solution)/shard_map/ppermute | solution.py:1063
  216.1 18.2 %collective-permute-start.51 = (bf16[4,32,1024]{2,1,0:T(8,128)(2,1)}, bf16[4,32,1024]{2,1,0:T(8,128)(2,1)}, u32[]{:S(2)}, u32[]{:S(2)}) collective-permute-start(bf16[4,32,1024]{2,1,0:T(8,128)(2,1)} %get-tuple-element.184), channel_id=1, source_target_pairs={{0,16},{8,24},{16,0},{24,8},{1,17},{9,25},{17,1},{25,9},{2,18},{10... | collective-permute-start | bytes 786440 | tf_op jit(solution)/shard_map/ppermute | solution.py:1072
  217.1 12.4 %collective-permute-start.45 = (bf16[272,384]{1,0:T(8,128)(2,1)S(1)}, bf16[272,384]{1,0:T(8,128)(2,1)S(1)}, u32[]{:S(2)}, u32[]{:S(2)}) collective-permute-start(bf16[272,384]{1,0:T(8,128)(2,1)S(1)} %get-tuple-element.190), channel_id=1, source_target_pairs={{0,16},{8,24},{16,0},{24,8},{1,17},{9,25},{17,1},{25,9},{2,18},{10... | collective-permute-start | bytes 626696 | tf_op jit(solution)/shard_map/ppermute | solution.py:1081
  220.3 17.3 %collective-permute-start.42 = (bf16[128,1024]{1,0:T(8,128)(2,1)}, bf16[128,1024]{1,0:T(8,128)(2,1)}, u32[]{:S(2)}, u32[]{:S(2)}) collective-permute-start(bf16[128,1024]{1,0:T(8,128)(2,1)} %fusion.14), channel_id=1, source_target_pairs={{0,2},{2,0},{1,3},{3,1},{4,6},{6,4},{5,7},{7,5},{8,10},{10,8},{9,1... | collective-permute-start | bytes 786440 | tf_op jit(solution)/shard_map/ppermute | solution.py:1039
  230.8 26.2 %all-to-all-start.4 = ((bf16[8,48,384]{2,1,0:T(8,128)(2,1)}), bf16[8,48,384]{2,1,0:T(8,128)(2,1)S(1)}, u32[]{:S(2)}, u32[]{:S(2)}) async-start(bf16[8,48,384]{2,1,0:T(8,128)(2,1)} %shard_map.156), calls=%async_computation.4 | async-start | bytes 589824 | tf_op jit(solution)/shard_map/all_to_all | solution.py:1093
  239.7 27.4 %collective-permute-start.55 = (bf16[2,128,1024]{2,1,0:T(8,128)(2,1)}, bf16[2,128,1024]{2,1,0:T(8,128)(2,1)}, u32[]{:S(2)}, u32[]{:S(2)}) collective-permute-start(bf16[2,128,1024]{2,1,0:T(8,128)(2,1)} %fusion.8), channel_id=1, source_target_pairs={{1,4},{3,6},{4,16},{5,20},{6,18},{7,22},{9,12},{11,14},{12,24},{13... | collective-permute-start | bytes 1572872 | tf_op jit(solution)/shard_map/ppermute | solution.py:1108
  244.7 11.6 %collective-permute-start.53 = (bf16[32,1024]{1,0:T(8,128)(2,1)S(1)}, bf16[32,1024]{1,0:T(8,128)(2,1)S(1)}, u32[]{:S(2)}, u32[]{:S(2)}) collective-permute-start(bf16[32,1024]{1,0:T(8,128)(2,1)S(1)} %fusion.19), channel_id=1, source_target_pairs={{0,2},{2,0},{1,3},{3,1},{4,6},{6,4},{5,7},{7,5},{8,10},{10,8},{9,1... | collective-permute-start | bytes 196616 | tf_op jit(solution)/shard_map/ppermute | solution.py:1079
  247.7 13.9 %collective-permute-start.43 = (bf16[128,1024]{1,0:T(8,128)(2,1)S(1)}, bf16[128,1024]{1,0:T(8,128)(2,1)}, u32[]{:S(2)}, u32[]{:S(2)}) collective-permute-start(bf16[128,1024]{1,0:T(8,128)(2,1)S(1)} %fusion.13), channel_id=1, source_target_pairs={{0,2},{2,0},{1,3},{3,1},{4,6},{6,4},{5,7},{7,5},{8,10},{10,8},{9,1... | collective-permute-start | bytes 786440 | tf_op jit(solution)/shard_map/ppermute | solution.py:1075
  (73 other events, 623.0 us)
